TPU v7x, 512 devices: a whole 4x4x16 slice. The times are simulated.
512 devices in a mesh: dp: 32 (over z, x_lo), mp: 16 (over x_hi, y, core).
Axes of the slice: x: 4 (x_hi: 2, x_lo: 2; x = x_hi * 2 + x_lo), y: 4, z: 16, core: 2. Of those that a mesh axis runs over, the one named last changes fastest.
Arguments:
- teacher_query: bfloat16 [2048, 8192], P('mp', 'dp'), may hold values from -120 to 120
- teacher_keys: bfloat16 [2048, 1024], P('mp'), may hold values from -6 to 6
- teacher_values: bfloat16 [2048, 1024], P('mp'), may hold values from -6 to 6
- teacher_out: bfloat16 [8192, 8192], P('dp', 'mp'), may hold values from -0.0625 to 0.0625
- teacher_resid: bfloat16 [2048, 8192], P('dp', 'mp'), may hold values from -1.5 to 1.5
- distill_proj: bfloat16 [8192, 4096], P('mp', 'dp'), may hold values from -1 to 2
- student_context: bfloat16 [2048, 4096], P('mp'), may hold values from -6 to 6
- student_resid: bfloat16 [2048, 4096], P('mp', 'dp'), may hold values from -3 to 3
- student_out: bfloat16 [4096, 4096], P(None, 'dp'), may hold values from -0.09375 to 0.09375
- student_gain: float32 [4096], replicated, may hold values from 0.5 to 1.5
Outputs:
- grad_wo: bfloat16 [4096, 4096], P(None, 'dp')
- grad_gain: float32 [4096], P('dp')
- grad_proj: float32 [8192, 4096], P('mp', 'dp')
All inputs are finite; a program needn't handle non-finite values.
Results may differ from a plain program's by a relative error of at most 0.03.
Values may be sent and summed in bfloat16 or wider, within the bound.
No kernel may reach another device: no remote copies, remote signals or barrier semaphores. Data moves between devices by JAX's collectives and lax.ppermute only.
A program may use at most 64 MiB of HBM per device.

v0:
```python
import jax
import jax.numpy as jnp
from jax import lax
from jax.sharding import PartitionSpec as P

HEADS = 64
KV_HEADS = 8
HEAD = 128


EPS = 1e-05


def on_device(
    teacher_query,
    teacher_keys,
    teacher_values,
    teacher_out,
    teacher_resid,
    distill_proj,
    student_context,
    student_resid,
    student_out,
    student_gain,
):
    groups = HEADS // KV_HEADS
    dp_index = lax.axis_index("dp")
    mp_index = lax.axis_index("mp")
    query_rows, query_width = teacher_query.shape
    local_heads = query_width // HEAD
    kv_local = max(local_heads // groups, 1)
    kv_start = dp_index * local_heads // groups
    key_mine = lax.dynamic_slice_in_dim(teacher_keys, kv_start * HEAD, kv_local * HEAD, 1)
    value_mine = lax.dynamic_slice_in_dim(teacher_values, kv_start * HEAD, kv_local * HEAD, 1)
    keys_all, values_all = (
        lax.all_gather(key_mine, "mp", axis=0, tiled=True),
        lax.all_gather(value_mine, "mp", axis=0, tiled=True),
    )
    total = keys_all.shape[0]
    repeat = local_heads // kv_local
    queries = teacher_query.reshape(query_rows, kv_local, repeat, HEAD)
    keyed = keys_all.reshape(total, kv_local, HEAD)
    valued = values_all.reshape(total, kv_local, HEAD)
    scores = jnp.einsum(
        "qgrd,kgd->grqk", queries, keyed, preferred_element_type=jnp.float32
    ) * HEAD ** (-0.5)
    query_pos = mp_index * query_rows + lax.iota(jnp.int32, query_rows)
    key_pos = lax.iota(jnp.int32, total)
    allowed = query_pos[:, None] >= key_pos[None, :]
    scores = jnp.where(allowed, scores, -jnp.inf)
    top = jnp.max(scores, axis=-1, keepdims=True)
    weights = jnp.exp(scores - top)
    probs = (weights / jnp.sum(weights, axis=-1, keepdims=True)).astype(jnp.bfloat16)
    context = jnp.einsum("grqk,kgd->qgrd", probs, valued, preferred_element_type=jnp.float32)
    context = context.astype(jnp.bfloat16).reshape(query_rows, query_width)
    head_terms = jnp.dot(
        lax.all_gather(context, "mp", axis=0, tiled=True),
        teacher_out,
        preferred_element_type=jnp.float32,
    )
    summed = lax.psum_scatter(
        head_terms.astype(jnp.bfloat16), "dp", scatter_dimension=0, tiled=True
    ).astype(jnp.float32)
    hidden = (teacher_resid.astype(jnp.float32) + summed).astype(jnp.bfloat16)
    hidden_all = lax.all_gather(hidden, "dp", axis=0, tiled=True)
    rows = hidden_all
    target = lax.psum_scatter(
        jnp.dot(rows, distill_proj, preferred_element_type=jnp.float32),
        "mp",
        scatter_dimension=0,
        tiled=True,
    )
    width = student_context.shape[1]
    columns = student_out.shape[1]
    state = student_resid.astype(jnp.float32) + jnp.dot(
        student_context, student_out, preferred_element_type=jnp.float32
    )
    grad_scale = total ** (-0.5)
    gain_mine = lax.dynamic_slice_in_dim(student_gain, dp_index * columns, columns, 0)
    squares = lax.psum(jnp.sum(state * state, axis=1), "dp")
    inverse = lax.rsqrt(squares / width + EPS)[:, None]
    pred = state * inverse * gain_mine
    error = (pred - target) * grad_scale
    upstream = error * gain_mine
    inner = lax.psum(jnp.sum(upstream * state, axis=1), "dp")
    grad_state = inverse * upstream - state * inverse**3 * (inner / width)[:, None]
    gain_term = error * state * inverse
    grad_bf = grad_state.astype(jnp.bfloat16)
    error_bf = error.astype(jnp.bfloat16)
    gain_part = jnp.sum(gain_term, axis=0)
    contract_rows = (((0,), (0,)), ((), ()))
    weight_part = lax.dot_general(
        student_context, grad_bf, contract_rows, preferred_element_type=jnp.float32
    )
    weight_sum, gain_sum = lax.psum((weight_part, gain_part), "mp")
    grad_wo = weight_sum.astype(jnp.bfloat16)
    empty = jnp.zeros((hidden_all.shape[1], columns), jnp.float32)
    rows = hidden_all
    grad_proj = empty - lax.dot_general(
        rows,
        lax.all_gather(error_bf, "mp", axis=0, tiled=True),
        contract_rows,
        preferred_element_type=jnp.float32,
    )
    return (grad_wo, gain_sum, grad_proj)


def solution(mesh):
    in_specs = (
        P("mp", "dp"),
        P("mp", None),
        P("mp", None),
        P("dp", "mp"),
        P("dp", "mp"),
        P("mp", "dp"),
        P("mp", None),
        P("mp", "dp"),
        P(None, "dp"),
        P(),
    )
    out_specs = (P(None, "dp"), P("dp"), P("mp", "dp"))
    return jax.shard_map(
        on_device, mesh=mesh, in_specs=in_specs, out_specs=out_specs, check_vma=False
    )
```

profile of v0, /device:TPU:1, one launch (start us, length us, event | category | flops | bytes accessed | tf_op | source)
XLA Modules:
  0.0 668.1 jit_solution(13781305007240357976)
XLA Ops:
  7.3 0.8 constant_dynamic-slice_fusion
  8.1 0.8 constant_dynamic-slice_fusion.1
  9.2 27.3 %all_gather.15 = bf16[2048,128]{0,1:T(8,128)(2,1)S(1)} all-gather(bf16[128,128]{0,1:T(8,128)(2,1)S(1)} %copy.21), channel_id=1, replica_groups=mesh['dp'=32,'mp'=16] {'mp'}, dimensions={0}, use_global_device_ids=true | all-gather | bytes 557056 | tf_op jit(solution)/shard_map/all_gather | solution.py:37
  36.4 22.2 %all_gather.16 = bf16[2048,128]{1,0:T(8,128)(2,1)S(1)} all-gather(bf16[128,128]{1,0:T(8,128)(2,1)S(1)} %constant_dynamic-slice_fusion), channel_id=1, replica_groups=mesh['dp'=32,'mp'=16] {'mp'}, dimensions={0}, use_global_device_ids=true | all-gather | bytes 557056 | tf_op jit(solution)/shard_map/all_gather | solution.py:36
  58.6 1.3 fusion.12
  60.0 0.3 fusion.2
  60.3 1.1 convolution_convert_fusion.1
  61.5 57.6 %all-gather.3.cloned.1.call-done = bf16[2048,256]{0,1:T(8,128)(2,1)} async-done(((bf16[128,256]{0,1:T(8,128)(2,1)}), bf16[2048,256]{0,1:T(8,128)(2,1)}) %all-gather.3.cloned.1.call-update) | async-done | bytes 1048592 | tf_op jit(solution)/shard_map/all_gather | solution.py:57
  119.1 3.3 convolution_convert_fusion
  122.5 115.1 %reduce-scatter.3.cloned.1.call-done = bf16[64,512]{1,0:T(8,128)(2,1)} async-done(((bf16[2048,512]{1,0:T(8,128)(2,1)}), bf16[64,512]{1,0:T(8,128)(2,1)}) %reduce-scatter.3.cloned.1.call-update) | async-done | bytes 65552 | tf_op jit(solution)/shard_map/reduce_scatter | solution.py:61
  237.5 1.5 add_convert_fusion
  239.1 135.5 %all-gather.5.cloned.1.call-done = bf16[2048,512]{1,0:T(8,128)(2,1)} async-done(((bf16[64,512]{1,0:T(8,128)(2,1)}), bf16[2048,512]{1,0:T(8,128)(2,1)}) %all-gather.5.cloned.1.call-update) | async-done | bytes 2097168 | tf_op jit(solution)/shard_map/all_gather | solution.py:65
  374.6 3.4 fusion.13
  378.2 0.5 multiply_reduce_fusion.2
  378.7 47.8 %psum.28 = f32[128]{0:T(128)S(1)} all-reduce(f32[128]{0:T(128)S(1)} %get-tuple-element.15), channel_id=1, replica_groups=mesh['dp'=32,'mp'=16] {'dp'}, use_global_device_ids=true, to_apply=%region_1.2 | all-reduce | flops 128 | bytes 1024 | tf_op jit(solution)/shard_map/psum | solution.py:80
  426.5 0.8 broadcast_multiply_fusion
  427.3 60.6 %reduce-scatter.5.cloned.1.call-done = f32[128,128]{0,1:T(8,128)} async-done(((f32[2048,128]{0,1:T(8,128)}), f32[128,128]{0,1:T(8,128)}) %reduce-scatter.5.cloned.1.call-update) | async-done | bytes 65552 | tf_op jit(solution)/shard_map/reduce_scatter | solution.py:67
  487.9 1.0 multiply_reduce_fusion
  488.9 50.9 %psum.29 = f32[128]{0:T(128)S(1)} all-reduce(f32[128]{0:T(128)S(1)} %get-tuple-element.7), channel_id=1, replica_groups=mesh['dp'=32,'mp'=16] {'dp'}, use_global_device_ids=true, to_apply=%region_7.8 | all-reduce | flops 128 | bytes 1024 | tf_op jit(solution)/shard_map/psum | solution.py:85
  539.8 41.1 %all_gather.19 = bf16[2048,128]{0,1:T(8,128)(2,1)} all-gather(bf16[128,128]{0,1:T(8,128)(2,1)S(1)} %get-tuple-element.12), channel_id=1, replica_groups=mesh['dp'=32,'mp'=16] {'mp'}, dimensions={0}, use_global_device_ids=true | all-gather | bytes 557056 | tf_op jit(solution)/shard_map/all_gather | solution.py:101
  580.9 2.6 convolution_bitcast_fusion
  583.5 73.3 %all-reduce.2 = (bf16[4096,128]{0,1:T(8,128)(2,1)}, f32[128]{0:T(128)}) all-reduce(f32[4096,128]{0,1:T(8,128)} %convolution_bitcast_fusion, f32[128]{0:T(128)S(1)} %get-tuple-element.6), channel_id=1, replica_groups=mesh['dp'=32,'mp'=16] {'mp'}, use_global_device_ids=true, to_apply=%region_8.9 | all-reduce | flops 524416 | bytes 3146752 | tf_op jit(solution)/shard_map/psum | solution.py:95
  656.8 2.3 copy.18
  659.1 2.5 convolution_subtract_fusion
  (28 shorter events, 0.7 us)
Async XLA Ops:
  7.2 371.0 %copy-start = (bf16[128,4096]{1,0:T(8,128)(2,1)S(1)}, bf16[128,4096]{1,0:T(8,128)(2,1)}, u32[]{:S(2)}) copy-start(bf16[128,4096]{1,0:T(8,128)(2,1)} %param.16) | copy-start | bytes 3145732
  7.2 111.9 %all-gather.3.cloned.1.call-start = ((), (), s32[]{:S(2)}) async-start(), calls=%async_computation.2 | async-start | bytes 1114112 | tf_op jit(solution)/shard_map/all_gather | solution.py:57
  60.3 58.8 %copy-start.3 = (bf16[256,512]{1,0:T(8,128)(2,1)S(1)}, bf16[256,512]{1,0:T(8,128)(2,1)}, u32[]{:S(2)}) copy-start(bf16[256,512]{1,0:T(8,128)(2,1)} %param.13) | copy-start | bytes 786436
  61.4 176.1 %reduce-scatter.3.cloned.1.call-start = ((), (), s32[]{:S(2)}) async-start(), calls=%async_computation.3 | async-start | bytes 2162688 | tf_op jit(solution)/shard_map/reduce_scatter | solution.py:61
  122.4 115.1 %copy-start.5 = (bf16[64,512]{1,0:T(8,128)(2,1)S(1)}, bf16[64,512]{1,0:T(8,128)(2,1)}, u32[]{:S(2)}) copy-start(bf16[64,512]{1,0:T(8,128)(2,1)} %param.14) | copy-start | bytes 196612
  122.4 252.2 %copy-start.4 = (bf16[512,128]{1,0:T(8,128)(2,1)S(1)}, bf16[512,128]{1,0:T(8,128)(2,1)}, u32[]{:S(2)}) copy-start(bf16[512,128]{1,0:T(8,128)(2,1)} %param.15) | copy-start | bytes 393220
  122.4 252.2 %all-gather.5.cloned.1.call-start = ((), (), s32[]{:S(2)}) async-start(), calls=%async_computation.4 | async-start | bytes 2162688 | tf_op jit(solution)/shard_map/all_gather | solution.py:65
  239.0 139.0 %copy-start.6 = (bf16[128,128]{1,0:T(8,128)(2,1)S(1)}, bf16[128,128]{1,0:T(8,128)(2,1)}, u32[]{:S(2)}) copy-start(bf16[128,128]{1,0:T(8,128)(2,1)} %param.17) | copy-start | bytes 98308
  239.1 139.1 %copy-start.2 = (bf16[4096,128]{1,0:T(8,128)(2,1)S(1)}, bf16[4096,128]{1,0:T(8,128)(2,1)}, u32[]{:S(2)}) copy-start(bf16[4096,128]{1,0:T(8,128)(2,1)} %param.18) | copy-start | bytes 3145732
  239.1 248.8 %reduce-scatter.5.cloned.1.call-start = ((), (), s32[]{:S(2)}) async-start(), calls=%async_computation.5 | async-start | bytes 1114112 | tf_op jit(solution)/shard_map/reduce_scatter | solution.py:67
  583.5 75.5 %copy-start.1 = (bf16[2048,512]{1,0:T(8,128)(2,1)S(1)}, bf16[2048,512]{1,0:T(8,128)(2,1)}, u32[]{:S(2)}) copy-start(bf16[2048,512]{1,0:T(8,128)(2,1)} %all-gather.5.cloned.1.call-done) | copy-start | bytes 6291460
Sparse Core Ops, SparseCore 0:
  61.6 57.4 all-gather.2
  122.5 114.9 reduce-scatter.2
  240.4 134.1 all-gather.4
  380.4 107.4 reduce-scatter.4
where the time goes:
time: 672 us; the launch traced here: 668 us
  waiting for transfers between devices  369 us (55%)
  blocking collectives  263 us (39%)
  matrix products  14.8 us (2%)
  between operations  13.9 us (2%)
    all_gather x1, waiting for transfers between devices, on_device(): hidden_all = lax.all_gather(hidden, 'dp', axis=0, tiled=True)  135 us
    reduce_scatter x1, waiting for transfers between devices, on_device(): lax.psum_scatter(head_terms.astype(jnp.bfloat16), 'dp', scatter_dimension...  115 us
    psum x1, blocking collectives, on_device(): weight_sum, gain_sum = lax.psum((weight_part, gain_part), 'mp')  73.3 us
    reduce_scatter x1, waiting for transfers between devices, on_device(): lax.psum_scatter(jnp.dot(rows, distill_proj, preferred_element_type=jnp.f...  60.6 us
    all_gather x1, waiting for transfers between devices, on_device(): lax.all_gather(context, 'mp', axis=0, tiled=True)  57.6 us
    psum x1, blocking collectives, on_device(): inner = lax.psum(jnp.sum(upstream * state, axis=1), 'dp')  50.9 us
    psum x1, blocking collectives, on_device(): squares = lax.psum(jnp.sum(state * state, axis=1), 'dp')  47.8 us
    all_gather x1, blocking collectives, on_device(): lax.all_gather(error_bf, 'mp', axis=0, tiled=True)  41.1 us
  transfers between devices with their start and end apart: 4, of which 4 were waited for; matrix products, arithmetic and copies ran while one was open for 0% of the time, Pallas kernels for 0%

commit v1 on v0

v1 whole, which is shorter than its diff:
```python
import jax
import jax.numpy as jnp
from jax import lax
from jax.sharding import Mesh
from jax.sharding import PartitionSpec as P

HEADS = 64
KV_HEADS = 8
HEAD = 128
EPS = 1e-05

DP = ("zh", "zl", "xl")
MP = ("xh", "y", "core")
NEAR = ("zl", "xl")
FAR = ("zh",)
AXES = DP + MP
SIZES = (4, 4, 2, 2, 4, 2)
N_FAR, N_NEAR, N_MP = 4, 8, 16

BF = jnp.bfloat16
F32 = jnp.float32


def exchange(pieces, axes):
    return lax.all_to_all(pieces, axes, 0, 0, tiled=True)


def to_all(block, axes, count):
    return exchange(jnp.broadcast_to(block[None], (count,) + block.shape), axes)


def on_device(
    teacher_query,
    teacher_keys,
    teacher_values,
    teacher_out,
    teacher_resid,
    distill_proj,
    student_context,
    student_resid,
    student_out,
    student_gain,
):
    far = lax.axis_index("zh")
    near = lax.axis_index(NEAR)
    dp_index = lax.axis_index(DP)
    mp_index = lax.axis_index(MP)
    rows, query_width = teacher_query.shape
    local_heads = query_width // HEAD
    total = rows * N_MP
    sub = rows // N_NEAR
    columns = student_out.shape[1]
    width = student_context.shape[1]
    d_cols = teacher_out.shape[1]
    head_rows = teacher_out.shape[0]

    packed = jnp.concatenate([teacher_out, teacher_resid], axis=0)
    packed_all = lax.all_gather(packed, NEAR, axis=0, tiled=False)
    out_near = packed_all[:, :head_rows].reshape(N_NEAR * head_rows, d_cols)
    resid_near = packed_all[:, head_rows:].reshape(N_FAR, N_NEAR, sub, d_cols)
    resid_mine = lax.dynamic_index_in_dim(resid_near, near, 1, keepdims=False)

    kv_start = dp_index * local_heads // (HEADS // KV_HEADS)
    key_mine = lax.dynamic_slice_in_dim(teacher_keys, kv_start * HEAD, HEAD, 1)
    value_mine = lax.dynamic_slice_in_dim(teacher_values, kv_start * HEAD, HEAD, 1)
    kv_all = to_all(jnp.concatenate([key_mine, value_mine], axis=1), MP, N_MP)
    kv_all = kv_all.reshape(total, 2 * HEAD)
    keyed = kv_all[:, :HEAD]
    valued = kv_all[:, HEAD:]
    queries = teacher_query.reshape(rows, local_heads, HEAD)
    scores = jnp.einsum(
        "qrd,kd->rqk", queries, keyed, preferred_element_type=F32
    ) * HEAD ** (-0.5)
    query_pos = mp_index * rows + lax.iota(jnp.int32, rows)
    key_pos = lax.iota(jnp.int32, total)
    allowed = query_pos[:, None] >= key_pos[None, :]
    scores = jnp.where(allowed, scores, -jnp.inf)
    top = jnp.max(scores, axis=-1, keepdims=True)
    weights = jnp.exp(scores - top)
    probs = (weights / jnp.sum(weights, axis=-1, keepdims=True)).astype(BF)
    context = jnp.einsum("rqk,kd->qrd", probs, valued, preferred_element_type=F32)
    context = context.astype(BF).reshape(N_NEAR, 1, sub, query_width)

    context = jnp.broadcast_to(context, (N_NEAR, N_MP, sub, query_width))
    context = exchange(
        context.reshape(N_NEAR * N_MP, sub, query_width), NEAR + MP
    ).reshape(N_NEAR, N_MP * sub, query_width)
    context = context.transpose(1, 0, 2).reshape(N_MP * sub, N_NEAR * query_width)
    head_terms = jnp.dot(context, out_near, preferred_element_type=F32).astype(BF)
    head_terms = exchange(
        head_terms.reshape(N_FAR, N_MP * sub // N_FAR, d_cols), FAR
    )
    summed = jnp.sum(head_terms.astype(F32), axis=0)
    resid_mine = resid_mine.reshape(N_MP * sub // N_FAR, d_cols).astype(F32)
    hidden = (resid_mine + summed).astype(BF)
    hidden_near = to_all(hidden, FAR, N_FAR).reshape(N_MP * sub, d_cols)

    proj_near = lax.all_gather(distill_proj, NEAR, axis=0, tiled=False)
    partial = jnp.einsum(
        "tk,gkc->tgc", hidden_near, proj_near, preferred_element_type=F32
    ).astype(BF)
    partial = exchange(partial.reshape(N_MP, sub, N_NEAR * columns), MP)
    target = jnp.sum(partial.astype(F32), axis=0)

    state = student_resid.astype(F32) + jnp.dot(
        student_context, student_out, preferred_element_type=F32
    )
    state = exchange(state.reshape(N_NEAR, sub, columns), NEAR)
    state = state.transpose(1, 0, 2).reshape(sub, N_NEAR * columns)
    gain = lax.dynamic_slice_in_dim(
        student_gain, far * N_NEAR * columns, N_NEAR * columns, 0
    )
    grad_scale = total ** (-0.5)
    gained = state * gain
    sums = jnp.stack(
        [
            jnp.sum(state * state, axis=1),
            jnp.sum(gained * gained, axis=1),
            jnp.sum(target * gained, axis=1),
        ]
    )
    sums = jnp.pad(sums, ((0, 5), (0, 128 - sub)))
    sums = jnp.sum(to_all(sums, FAR, N_FAR), axis=0)[:3, :sub]
    inverse = lax.rsqrt(sums[0] / width + EPS)
    inner = (inverse * sums[1] - sums[2]) * (grad_scale / width)
    inverse = inverse[:, None]
    error = (gained * inverse - target) * grad_scale
    grad_state = inverse * error * gain - state * (inverse**3 * inner[:, None])
    gain_part = jnp.sum(error * state * inverse, axis=0).reshape(N_NEAR, 1, columns)
    gain_high = gain_part.astype(BF)
    gain_low = (gain_part - gain_high.astype(F32)).astype(BF)

    def by_near(values):
        return values.reshape(sub, N_NEAR, columns).transpose(1, 0, 2)

    sent = jnp.concatenate(
        [
            by_near(error.astype(BF)),
            by_near(grad_state.astype(BF)),
            gain_high,
            gain_low,
            jnp.zeros((N_NEAR, 6, columns), BF),
        ],
        axis=1,
    )
    slab = sent.shape[1]
    sent = jnp.broadcast_to(sent[:, None], (N_NEAR, N_MP, slab, columns))
    got = exchange(sent.reshape(N_NEAR * N_MP, slab, columns), NEAR + MP)
    error_all = got[:, :sub].reshape(total, columns)
    grad_all = got[:, sub : 2 * sub].reshape(total, columns)
    grad_gain = jnp.sum(got[:, 2 * sub : 2 * sub + 2].astype(F32), axis=(0, 1))

    contract_rows = (((0,), (0,)), ((), ()))
    part = width // N_MP
    context_cols = exchange(
        student_context.reshape(rows, N_MP, part).transpose(1, 0, 2), MP
    )
    context_cols = context_cols.reshape(N_MP, N_NEAR, sub, part)
    context_cols = context_cols.transpose(1, 0, 2, 3).reshape(total, part)
    grad_wo = lax.dot_general(
        context_cols, grad_all, contract_rows, preferred_element_type=F32
    ).astype(BF)
    grad_wo = to_all(grad_wo, MP, N_MP).reshape(width, columns)

    hidden_all = lax.all_gather(hidden_near, NEAR, axis=0, tiled=True)
    grad_proj = -lax.dot_general(
        hidden_all, error_all, contract_rows, preferred_element_type=F32
    )
    return (grad_wo, grad_gain, grad_proj)


def solution(mesh):
    fine = Mesh(mesh.devices.reshape(SIZES), AXES)
    in_specs = (
        P(MP, DP),
        P(MP, None),
        P(MP, None),
        P(DP, MP),
        P(DP, MP),
        P(MP, DP),
        P(MP, None),
        P(MP, DP),
        P(None, DP),
        P(),
    )
    out_specs = (P(None, DP), P(DP), P(MP, DP))
    return jax.shard_map(
        on_device, mesh=fine, in_specs=in_specs, out_specs=out_specs, check_vma=False
    )
```

time: 672 us -> 345 us (0.51)
  blocking collectives: 263 us -> 0 us
  waiting for transfers between devices: 369 us -> 218 us
  starting transfers between devices: 0.16 us -> 82.1 us
  local copies, waits for them, and re-layouts: 4.12 us -> 16.2 us
    reduce_scatter x2 -> x0, waiting for transfers between devices: 176 us -> none  [the longest x1 115 us: on_device(): lax.psum_scatter(head_terms.astype(jnp.bfloat16), 'dp', scatter_dimension...]
    psum x3 -> x0, blocking collectives: 172 us -> none  [the longest x1 73.3 us: on_device(): weight_sum, gain_sum = lax.psum((weight_part, gain_part), 'mp')]
    all_to_all x0 -> x10, waiting for transfers between devices: none -> 122 us  [exchange(): return lax.all_to_all(pieces, axes, 0, 0, tiled=True)]
    all_gather x2 -> x3, waiting for transfers between devices: 193 us -> 94.3 us  [the longest x1 56.3 us: on_device(): packed_all = lax.all_gather(packed, NEAR, axis=0, tiled=False)]
    all_gather x3 -> x0, blocking collectives: 90.5 us -> none  [the longest x1 41.1 us: on_device(): lax.all_gather(error_bf, 'mp', axis=0, tiled=True)]
    all_to_all x0 -> x10, starting transfers between devices: none -> 82.1 us  [exchange(): return lax.all_to_all(pieces, axes, 0, 0, tiled=True)]
    dot_general x7 -> x6, matrix products: 14.8 us -> 10.6 us  [the longest x1 3.12 us: on_device(): lax.dot_general(hidden_all, error_all, contract_rows, preferred_element_t...]
  transfers between devices with their start and end apart: 4 -> 13, of which waited for: 4 -> 11; matrix products, arithmetic and copies ran while one was open for 0% -> 5% of each run, Pallas kernels for 0% -> 0%
where the time goes in v1:
time: 345 us; the launch traced here: 344 us
  waiting for transfers between devices  218 us (63%)
  starting transfers between devices  82.1 us (24%)
  local copies, waits for them, and re-layouts  16.2 us (5%)
  between operations  14 us (4%)
  matrix products  11.6 us (3%)
    all_to_all x10, waiting for transfers between devices, exchange(): return lax.all_to_all(pieces, axes, 0, 0, tiled=True)  122 us
    all_to_all x10, starting transfers between devices, exchange(): return lax.all_to_all(pieces, axes, 0, 0, tiled=True)  82.1 us
    all_gather x1, waiting for transfers between devices, on_device(): packed_all = lax.all_gather(packed, NEAR, axis=0, tiled=False)  56.3 us
    all_gather x1, waiting for transfers between devices, on_device(): proj_near = lax.all_gather(distill_proj, NEAR, axis=0, tiled=False)  27.3 us
    all_gather x1, waiting for transfers between devices, on_device(): hidden_all = lax.all_gather(hidden_near, NEAR, axis=0, tiled=True)  10.7 us
  transfers between devices with their start and end apart: 13, of which 11 were waited for; matrix products, arithmetic and copies ran while one was open for 5% of the time, Pallas kernels for 0%

profile of v1, /device:TPU:1, one launch (start us, length us, event | category | flops | bytes accessed | tf_op | source)
XLA Modules:
  0.0 344.0 jit_solution(1444549970995108693)
XLA Ops:
  9.2 10.3 %all-to-all-start.1 = ((bf16[16,128,256]{2,1,0:T(8,128)(2,1)}), bf16[16,128,256]{2,1,0:T(8,128)(2,1)S(1)}, u32[]{:S(2)}, u32[]{:S(2)}) async-start(bf16[16,128,256]{2,1,0:T(8,128)(2,1)} %broadcast_in_dim.24), calls=%async_computation.1 | async-start | bytes 2097152 | tf_op jit(solution)/shard_map/all_to_all | solution.py:25
  20.6 16.2 %all-to-all-done.1 = bf16[16,128,256]{2,1,0:T(8,128)(2,1)S(1)} async-done(((bf16[16,128,256]{2,1,0:T(8,128)(2,1)}), bf16[16,128,256]{2,1,0:T(8,128)(2,1)S(1)}, u32[]{:S(2)}, u32[]{:S(2)}) %all-to-all-start.1) | async-done | bytes 1048608 | tf_op jit(solution)/shard_map/all_to_all | solution.py:25
  40.3 7.1 %all-to-all-start.2 = ((bf16[128,16,256]{2,1,0:T(8,128)(2,1)}), bf16[128,16,256]{2,1,0:T(8,128)(2,1)S(1)}, u32[]{:S(2)}, u32[]{:S(2)}) async-start(bf16[128,16,256]{2,1,0:T(8,128)(2,1)} %bitcast.13), calls=%async_computation.2 | async-start | bytes 2097152 | tf_op jit(solution)/shard_map/all_to_all | solution.py:25
  47.5 56.3 %all-gather.8.cloned.1.call-done = bf16[2560,512]{1,0:T(8,128)(2,1)} async-done(((bf16[320,512]{1,0:T(8,128)(2,1)}), bf16[2560,512]{1,0:T(8,128)(2,1)}) %all-gather.8.cloned.1.call-update) | async-done | bytes 2621456 | tf_op jit(solution)/shard_map/all_gather | solution.py:58
  103.8 3.0 fusion.10
  106.8 12.0 %all-to-all-start.3 = ((bf16[4,64,512]{2,1,0:T(8,128)(2,1)}), bf16[4,64,512]{2,1,0:T(8,128)(2,1)S(1)}, u32[]{:S(2)}, u32[]{:S(2)}) async-start(bf16[4,64,512]{2,1,0:T(8,128)(2,1)} %bitcast.17), calls=%async_computation.3 | async-start | bytes 524288 | tf_op jit(solution)/shard_map/all_to_all | solution.py:25
  120.6 14.3 %all-to-all-done.3 = bf16[4,64,512]{2,1,0:T(8,128)(2,1)S(1)} async-done(((bf16[4,64,512]{2,1,0:T(8,128)(2,1)}), bf16[4,64,512]{2,1,0:T(8,128)(2,1)S(1)}, u32[]{:S(2)}, u32[]{:S(2)}) %all-to-all-start.3) | async-done | bytes 262176 | tf_op jit(solution)/shard_map/all_to_all | solution.py:25
  135.7 6.7 %all-to-all-start.4 = ((bf16[4,64,512]{2,1,0:T(8,128)(2,1)}), bf16[4,64,512]{2,1,0:T(8,128)(2,1)S(1)}, u32[]{:S(2)}, u32[]{:S(2)}) async-start(bf16[4,64,512]{2,1,0:T(8,128)(2,1)} %broadcast_in_dim.29), calls=%async_computation.4 | async-start | bytes 524288 | tf_op jit(solution)/shard_map/all_to_all | solution.py:25
  142.3 27.3 %all-gather.10.cloned.1.call-done = bf16[4096,128]{1,0:T(8,128)(2,1)} async-done(((bf16[512,128]{1,0:T(8,128)(2,1)}), bf16[4096,128]{1,0:T(8,128)(2,1)}) %all-gather.10.cloned.1.call-update) | async-done | bytes 1048592 | tf_op jit(solution)/shard_map/all_gather | solution.py:98
  169.6 1.8 convolution_convert_fusion
  172.8 11.1 %all-to-all-start.5 = ((bf16[16,16,1024]{2,1,0:T(8,128)(2,1)}), bf16[16,16,1024]{2,1,0:T(8,128)(2,1)S(1)}, u32[]{:S(2)}, u32[]{:S(2)}) async-start(bf16[16,16,1024]{2,1,0:T(8,128)(2,1)} %reshape.215), calls=%async_computation.5 | async-start | bytes 1048576 | tf_op jit(solution)/shard_map/all_to_all | solution.py:25
  185.0 10.2 %all-to-all-done.5 = bf16[16,16,1024]{2,1,0:T(8,128)(2,1)S(1)} async-done(((bf16[16,16,1024]{2,1,0:T(8,128)(2,1)}), bf16[16,16,1024]{2,1,0:T(8,128)(2,1)S(1)}, u32[]{:S(2)}, u32[]{:S(2)}) %all-to-all-start.5) | async-done | bytes 524320 | tf_op jit(solution)/shard_map/all_to_all | solution.py:25
  195.2 4.8 %all-to-all-start = ((f32[8,16,128]{2,1,0:T(8,128)}), f32[8,16,128]{2,1,0:T(8,128)S(1)}, u32[]{:S(2)}, u32[]{:S(2)}) async-start(f32[8,16,128]{2,1,0:T(8,128)} %bitcast), calls=%async_computation | async-start | bytes 131072 | tf_op jit(solution)/shard_map/all_to_all | solution.py:25
  200.8 5.0 %all-to-all-done = f32[8,16,128]{2,1,0:T(8,128)S(1)} async-done(((f32[8,16,128]{2,1,0:T(8,128)}), f32[8,16,128]{2,1,0:T(8,128)S(1)}, u32[]{:S(2)}, u32[]{:S(2)}) %all-to-all-start) | async-done | bytes 65568 | tf_op jit(solution)/shard_map/all_to_all | solution.py:25
  206.6 10.1 %all-to-all-start.6 = ((f32[4,8,128]{2,1,0:T(8,128)}), f32[4,8,128]{2,1,0:T(8,128)S(1)}, u32[]{:S(2)}, u32[]{:S(2)}) async-start(f32[4,8,128]{2,1,0:T(8,128)} %broadcast_in_dim.30), calls=%async_computation.6 | async-start | bytes 32768 | tf_op jit(solution)/shard_map/all_to_all | solution.py:25
  218.0 10.1 %all-to-all-done.6 = f32[4,8,128]{2,1,0:T(8,128)S(1)} async-done(((f32[4,8,128]{2,1,0:T(8,128)}), f32[4,8,128]{2,1,0:T(8,128)S(1)}, u32[]{:S(2)}, u32[]{:S(2)}) %all-to-all-start.6) | async-done | bytes 16416 | tf_op jit(solution)/shard_map/all_to_all | solution.py:25
  228.2 7.5 %all-to-all-start.8 = ((bf16[16,128,256]{1,2,0:T(8,128)(2,1)}), bf16[16,128,256]{1,2,0:T(8,128)(2,1)S(1)}, u32[]{:S(2)}, u32[]{:S(2)}) async-start(bf16[16,128,256]{1,2,0:T(8,128)(2,1)} %bitcast.31), calls=%async_computation.8 | async-start | bytes 2097152 | tf_op jit(solution)/shard_map/all_to_all | solution.py:25
  235.9 17.0 %all-to-all-done.8 = bf16[16,128,256]{1,2,0:T(8,128)(2,1)S(1)} async-done(((bf16[16,128,256]{1,2,0:T(8,128)(2,1)}), bf16[16,128,256]{1,2,0:T(8,128)(2,1)S(1)}, u32[]{:S(2)}, u32[]{:S(2)}) %all-to-all-start.8) | async-done | bytes 1048608 | tf_op jit(solution)/shard_map/all_to_all | solution.py:25
  254.2 6.1 %all-to-all-start.7 = ((bf16[128,40,128]{2,1,0:T(8,128)(2,1)}), bf16[128,40,128]{2,1,0:T(8,128)(2,1)S(1)}, u32[]{:S(2)}, u32[]{:S(2)}) async-start(bf16[128,40,128]{2,1,0:T(8,128)(2,1)} %bitcast.28), calls=%async_computation.7 | async-start | bytes 2621440 | tf_op jit(solution)/shard_map/all_to_all | solution.py:25
  263.6 40.9 %all-to-all-done.7 = bf16[128,40,128]{2,1,0:T(8,128)(2,1)S(1)} async-done(((bf16[128,40,128]{2,1,0:T(8,128)(2,1)}), bf16[128,40,128]{2,1,0:T(8,128)(2,1)S(1)}, u32[]{:S(2)}, u32[]{:S(2)}) %all-to-all-start.7) | async-done | bytes 1310752 | tf_op jit(solution)/shard_map/all_to_all | solution.py:25
  307.3 6.3 %all-to-all-start.9 = ((bf16[16,256,128]{2,1,0:T(8,128)(2,1)}), bf16[16,256,128]{2,1,0:T(8,128)(2,1)S(1)}, u32[]{:S(2)}, u32[]{:S(2)}) async-start(bf16[16,256,128]{2,1,0:T(8,128)(2,1)} %broadcast_in_dim.33), calls=%async_computation.9 | async-start | bytes 2097152 | tf_op jit(solution)/shard_map/all_to_all | solution.py:25
  314.2 10.7 %all-gather.6.cloned.1.call-done = bf16[2048,512]{1,0:T(8,128)(2,1)} async-done(((bf16[256,512]{1,0:T(8,128)(2,1)}), bf16[2048,512]{1,0:T(8,128)(2,1)}) %all-gather.6.cloned.1.call-update) | async-done | bytes 2097168 | tf_op jit(solution)/shard_map/all_gather | solution.py:165
  324.9 3.1 convolution_negate_fusion
  328.0 8.5 %all-to-all-done.9 = bf16[16,256,128]{2,1,0:T(8,128)(2,1)S(1)} async-done(((bf16[16,256,128]{2,1,0:T(8,128)(2,1)}), bf16[16,256,128]{2,1,0:T(8,128)(2,1)S(1)}, u32[]{:S(2)}, u32[]{:S(2)}) %all-to-all-start.9) | async-done | bytes 1048608 | tf_op jit(solution)/shard_map/all_to_all | solution.py:25
  (68 shorter events, 23.4 us)
Async XLA Ops:
  7.2 176.8 %copy-start = (bf16[4096,128]{1,0:T(8,128)(2,1)S(1)}, bf16[4096,128]{1,0:T(8,128)(2,1)}, u32[]{:S(2)}) copy-start(bf16[4096,128]{1,0:T(8,128)(2,1)} %param.18) | copy-start | bytes 3145732
  7.2 12.4 %copy-start.4 = (bf16[64,512]{1,0:T(8,128)(2,1)S(1)}, bf16[64,512]{1,0:T(8,128)(2,1)}, u32[]{:S(2)}) copy-start(bf16[64,512]{1,0:T(8,128)(2,1)} %param.14) | copy-start | bytes 196612
  7.2 12.4 %copy-start.3 = (bf16[256,512]{1,0:T(8,128)(2,1)S(1)}, bf16[256,512]{1,0:T(8,128)(2,1)}, u32[]{:S(2)}) copy-start(bf16[256,512]{1,0:T(8,128)(2,1)} %param.13) | copy-start | bytes 786436
  8.1 28.7 %copy-start.6 = (bf16[128,256]{1,0:T(8,128)(2,1)S(1)}, bf16[128,256]{1,0:T(8,128)(2,1)}, u32[]{:S(2)}) copy-start(bf16[128,256]{1,0:T(8,128)(2,1)} %param.10) | copy-start | bytes 196612
  9.2 27.6 %all-to-all-start.1 = ((bf16[16,128,256]{2,1,0:T(8,128)(2,1)}), bf16[16,128,256]{2,1,0:T(8,128)(2,1)S(1)}, u32[]{:S(2)}, u32[]{:S(2)}) async-start(bf16[16,128,256]{2,1,0:T(8,128)(2,1)} %broadcast_in_dim.24), calls=%async_computation.1 | async-start | bytes 2097152 | tf_op jit(solution)/shard_map/all_to_all | solution.py:25
  19.5 84.2 %all-gather.8.cloned.1.call-start = ((), (), s32[]{:S(2)}) async-start(), calls=%async_computation.11 | async-start | bytes 2949120 | tf_op jit(solution)/shard_map/all_gather | solution.py:58
  40.3 63.4 %all-to-all-start.2 = ((bf16[128,16,256]{2,1,0:T(8,128)(2,1)}), bf16[128,16,256]{2,1,0:T(8,128)(2,1)S(1)}, u32[]{:S(2)}, u32[]{:S(2)}) async-start(bf16[128,16,256]{2,1,0:T(8,128)(2,1)} %bitcast.13), calls=%async_computation.2 | async-start | bytes 2097152 | tf_op jit(solution)/shard_map/all_to_all | solution.py:25
  106.8 28.1 %all-to-all-start.3 = ((bf16[4,64,512]{2,1,0:T(8,128)(2,1)}), bf16[4,64,512]{2,1,0:T(8,128)(2,1)S(1)}, u32[]{:S(2)}, u32[]{:S(2)}) async-start(bf16[4,64,512]{2,1,0:T(8,128)(2,1)} %bitcast.17), calls=%async_computation.3 | async-start | bytes 524288 | tf_op jit(solution)/shard_map/all_to_all | solution.py:25
  118.8 50.9 %all-gather.10.cloned.1.call-start = ((), (), s32[]{:S(2)}) async-start(), calls=%async_computation.12 | async-start | bytes 1179648 | tf_op jit(solution)/shard_map/all_gather | solution.py:98
  135.7 34.0 %all-to-all-start.4 = ((bf16[4,64,512]{2,1,0:T(8,128)(2,1)}), bf16[4,64,512]{2,1,0:T(8,128)(2,1)S(1)}, u32[]{:S(2)}, u32[]{:S(2)}) async-start(bf16[4,64,512]{2,1,0:T(8,128)(2,1)} %broadcast_in_dim.29), calls=%async_computation.4 | async-start | bytes 524288 | tf_op jit(solution)/shard_map/all_to_all | solution.py:25
  169.6 3.2 copy-start.2
  169.6 14.3 %copy-start.1 = (bf16[128,4096]{1,0:T(8,128)(2,1)S(1)}, bf16[128,4096]{1,0:T(8,128)(2,1)}, u32[]{:S(2)}) copy-start(bf16[128,4096]{1,0:T(8,128)(2,1)} %param.16) | copy-start | bytes 3145732
  169.6 14.3 %copy-start.5 = (bf16[128,128]{1,0:T(8,128)(2,1)S(1)}, bf16[128,128]{1,0:T(8,128)(2,1)}, u32[]{:S(2)}) copy-start(bf16[128,128]{1,0:T(8,128)(2,1)} %param.17) | copy-start | bytes 98308
  172.8 22.4 %all-to-all-start.5 = ((bf16[16,16,1024]{2,1,0:T(8,128)(2,1)}), bf16[16,16,1024]{2,1,0:T(8,128)(2,1)S(1)}, u32[]{:S(2)}, u32[]{:S(2)}) async-start(bf16[16,16,1024]{2,1,0:T(8,128)(2,1)} %reshape.215), calls=%async_computation.5 | async-start | bytes 1048576 | tf_op jit(solution)/shard_map/all_to_all | solution.py:25
  195.2 10.6 %all-to-all-start = ((f32[8,16,128]{2,1,0:T(8,128)}), f32[8,16,128]{2,1,0:T(8,128)S(1)}, u32[]{:S(2)}, u32[]{:S(2)}) async-start(f32[8,16,128]{2,1,0:T(8,128)} %bitcast), calls=%async_computation | async-start | bytes 131072 | tf_op jit(solution)/shard_map/all_to_all | solution.py:25
  206.6 21.5 %all-to-all-start.6 = ((f32[4,8,128]{2,1,0:T(8,128)}), f32[4,8,128]{2,1,0:T(8,128)S(1)}, u32[]{:S(2)}, u32[]{:S(2)}) async-start(f32[4,8,128]{2,1,0:T(8,128)} %broadcast_in_dim.30), calls=%async_computation.6 | async-start | bytes 32768 | tf_op jit(solution)/shard_map/all_to_all | solution.py:25
  228.2 24.7 %all-to-all-start.8 = ((bf16[16,128,256]{1,2,0:T(8,128)(2,1)}), bf16[16,128,256]{1,2,0:T(8,128)(2,1)S(1)}, u32[]{:S(2)}, u32[]{:S(2)}) async-start(bf16[16,128,256]{1,2,0:T(8,128)(2,1)} %bitcast.31), calls=%async_computation.8 | async-start | bytes 2097152 | tf_op jit(solution)/shard_map/all_to_all | solution.py:25
  254.2 50.4 %all-to-all-start.7 = ((bf16[128,40,128]{2,1,0:T(8,128)(2,1)}), bf16[128,40,128]{2,1,0:T(8,128)(2,1)S(1)}, u32[]{:S(2)}, u32[]{:S(2)}) async-start(bf16[128,40,128]{2,1,0:T(8,128)(2,1)} %bitcast.28), calls=%async_computation.7 | async-start | bytes 2621440 | tf_op jit(solution)/shard_map/all_to_all | solution.py:25
  260.3 64.6 %all-gather.6.cloned.1.call-start = ((), (), s32[]{:S(2)}) async-start(), calls=%async_computation.10 | async-start | bytes 2359296 | tf_op jit(solution)/shard_map/all_gather | solution.py:165
  307.3 29.2 %all-to-all-start.9 = ((bf16[16,256,128]{2,1,0:T(8,128)(2,1)}), bf16[16,256,128]{2,1,0:T(8,128)(2,1)S(1)}, u32[]{:S(2)}, u32[]{:S(2)}) async-start(bf16[16,256,128]{2,1,0:T(8,128)(2,1)} %broadcast_in_dim.33), calls=%async_computation.9 | async-start | bytes 2097152 | tf_op jit(solution)/shard_map/all_to_all | solution.py:25
Sparse Core Ops, SparseCore 0:
  22.4 81.2 all-gather.7
  121.7 47.9 all-gather.9
  263.8 61.0 all-gather.5

commit v2 on v1

v2 whole, which is shorter than its diff:
```python
import jax
import jax.numpy as jnp
from jax import lax
from jax.sharding import Mesh
from jax.sharding import PartitionSpec as P

HEADS = 64
KV_HEADS = 8
HEAD = 128
EPS = 1e-05

DP = ("zh", "zn", "xl")
MP = ("xh", "y", "core")
NEAR = ("zn",)
FAR = ("zh", "xl")
AXES = DP + MP
SIZES = (2, 8, 2, 2, 4, 2)
N_ZH, N_XL, N_FAR, N_NEAR, N_MP = 2, 2, 4, 8, 16

BF = jnp.bfloat16
F32 = jnp.float32


def exchange(pieces, axes):
    return lax.all_to_all(pieces, axes, 0, 0, tiled=True)


def to_all(block, axes, count):
    return exchange(jnp.broadcast_to(block[None], (count,) + block.shape), axes)


def split(values):
    high = values.astype(BF)
    return high, (values - high.astype(F32)).astype(BF)


def on_device(
    teacher_query,
    teacher_keys,
    teacher_values,
    teacher_out,
    teacher_resid,
    distill_proj,
    student_context,
    student_resid,
    student_out,
    student_gain,
):
    far = lax.axis_index(FAR)
    near = lax.axis_index(NEAR)
    dp_index = lax.axis_index(DP)
    mp_index = lax.axis_index(MP)
    rows, query_width = teacher_query.shape
    local_heads = query_width // HEAD
    total = rows * N_MP
    sub = rows // N_NEAR
    columns = student_out.shape[1]
    width = student_context.shape[1]
    head_rows, d_cols = teacher_out.shape
    resid_rows = teacher_resid.shape[0]
    few = sub // N_XL

    packed = jnp.concatenate(
        [teacher_out, teacher_resid, distill_proj.reshape(-1, d_cols)], axis=0
    )
    packed_all = lax.all_gather(packed, NEAR, axis=0, tiled=False)
    out_near = packed_all[:, :head_rows].reshape(N_NEAR * head_rows, d_cols)
    resid_near = packed_all[:, head_rows : head_rows + resid_rows]
    resid_near = resid_near.reshape(N_NEAR, N_NEAR, few, d_cols)
    resid_mine = lax.dynamic_index_in_dim(resid_near, near, 1, keepdims=False)
    proj_near = packed_all[:, head_rows + resid_rows :]
    proj_near = proj_near.reshape(N_NEAR, d_cols, columns)

    def by_near(values):
        values = values.reshape(N_XL, N_NEAR, few, values.shape[-1])
        return values.transpose(1, 0, 2, 3).reshape(N_NEAR, sub, values.shape[-1])

    kv_start = dp_index * local_heads // (HEADS // KV_HEADS)
    key_mine = lax.dynamic_slice_in_dim(teacher_keys, kv_start * HEAD, HEAD, 1)
    value_mine = lax.dynamic_slice_in_dim(teacher_values, kv_start * HEAD, HEAD, 1)
    kv_all = to_all(jnp.concatenate([key_mine, value_mine], axis=1), MP, N_MP)
    kv_all = kv_all.reshape(total, 2 * HEAD)
    keyed = kv_all[:, :HEAD]
    valued = kv_all[:, HEAD:]
    queries = teacher_query.reshape(rows, local_heads, HEAD)
    scores = jnp.einsum(
        "qrd,kd->rqk", queries, keyed, preferred_element_type=F32
    ) * HEAD ** (-0.5)
    query_pos = mp_index * rows + lax.iota(jnp.int32, rows)
    key_pos = lax.iota(jnp.int32, total)
    allowed = query_pos[:, None] >= key_pos[None, :]
    scores = jnp.where(allowed, scores, -jnp.inf)
    top = jnp.max(scores, axis=-1, keepdims=True)
    weights = jnp.exp(scores - top)
    probs = (weights / jnp.sum(weights, axis=-1, keepdims=True)).astype(BF)
    context = jnp.einsum("rqk,kd->qrd", probs, valued, preferred_element_type=F32)
    context = by_near(context.astype(BF).reshape(rows, query_width))

    state = student_resid.astype(F32) + jnp.dot(
        student_context, student_out, preferred_element_type=F32
    )
    gain = lax.dynamic_slice_in_dim(student_gain, dp_index * columns, columns, 0)

    state_high, state_low = split(state)
    state_parts = jnp.concatenate([state_high, state_low], axis=1)
    state_parts = by_near(state_parts)
    got = exchange(jnp.concatenate([context, state_parts], axis=1), NEAR)
    state_parts = got[:, sub:].astype(F32)
    state_wide = state_parts[:, :, :columns] + state_parts[:, :, columns:]
    context = got[:, :sub].transpose(1, 0, 2).reshape(sub, N_NEAR * query_width)
    context = to_all(context, MP, N_MP).reshape(N_MP * sub, N_NEAR * query_width)

    part = width // N_MP
    context_cols = exchange(
        student_context.reshape(rows, N_MP, part).transpose(1, 0, 2), MP
    ).reshape(total, part)
    context, context_cols = lax.optimization_barrier((context, context_cols))

    head_terms = jnp.dot(context, out_near, preferred_element_type=F32).astype(BF)
    head_terms = head_terms.reshape(N_ZH, N_NEAR, N_XL, few, d_cols)
    head_terms = head_terms.transpose(0, 2, 1, 3, 4)
    head_terms = exchange(
        head_terms.reshape(N_FAR, N_NEAR * few, d_cols), FAR
    )
    summed = jnp.sum(head_terms.astype(F32), axis=0)
    resid_mine = resid_mine.reshape(N_NEAR * few, d_cols).astype(F32)
    hidden = (resid_mine + summed).astype(BF)
    hidden_near = to_all(hidden, FAR, N_FAR)
    hidden_near = hidden_near.reshape(N_ZH, N_XL, N_NEAR, few, d_cols)
    hidden_near = hidden_near.transpose(0, 2, 1, 3, 4).reshape(N_MP * sub, d_cols)

    partial = jnp.einsum(
        "tk,gkc->tgc", hidden_near, proj_near, preferred_element_type=F32
    ).astype(BF)
    partial = exchange(partial.reshape(N_MP, sub, N_NEAR * columns), MP)
    target_wide = jnp.sum(partial.astype(F32), axis=0)
    target_wide = target_wide.reshape(sub, N_NEAR, columns).transpose(1, 0, 2)

    gain_wide = student_gain.reshape(N_ZH, N_NEAR, N_XL, columns)
    gain_wide = gain_wide.transpose(0, 2, 1, 3).reshape(N_FAR, N_NEAR, columns)
    gain_wide = lax.dynamic_index_in_dim(gain_wide, far, 0, keepdims=False)[:, None]
    gained = state_wide * gain_wide
    sums = jnp.stack(
        [
            jnp.sum(state_wide * state_wide, axis=(0, 2)),
            jnp.sum(gained * gained, axis=(0, 2)),
            jnp.sum(target_wide * gained, axis=(0, 2)),
        ]
    )
    sums = jnp.stack(split(sums)).reshape(1, 6 * sub)
    sums = jnp.pad(sums, ((0, 7), (0, columns - 6 * sub)))
    here = (lax.iota(jnp.int32, N_FAR) == far)[:, None, None, None]
    sent = jnp.where(here, target_wide.astype(BF)[None], jnp.zeros((), BF))
    sums = jnp.broadcast_to(sums, (N_FAR, N_NEAR, 8, columns))
    sent = jnp.concatenate([sent, sums], axis=2)
    sent = sent.reshape(N_ZH, N_XL, N_NEAR, sub + 8, columns)
    sent = sent.transpose(0, 2, 1, 3, 4)
    got = exchange(sent.reshape(N_FAR * N_NEAR, sub + 8, columns), DP)
    got = got.reshape(N_ZH, N_NEAR, N_XL, sub + 8, columns)
    got = jnp.sum(got.astype(F32), axis=(0, 2))
    target = got[:, :sub].reshape(N_NEAR, N_XL, few, columns)
    target = target.transpose(1, 0, 2, 3).reshape(rows, columns)
    sums = got[:, sub, : 6 * sub].reshape(N_NEAR, 2, 3, N_XL, few).sum(axis=1)
    sums = sums.transpose(1, 2, 0, 3).reshape(3, rows)

    grad_scale = total ** (-0.5)
    inverse = lax.rsqrt(sums[0] / width + EPS)
    inner = (inverse * sums[1] - sums[2]) * (grad_scale / width)
    inverse = inverse[:, None]
    error = (state * inverse * gain - target) * grad_scale
    grad_state = inverse * error * gain - state * (inverse**3 * inner[:, None])
    gain_part = jnp.sum(error * state * inverse, axis=0)[None]
    gain_part = jnp.pad(jnp.concatenate(split(gain_part), axis=1), ((0, 7), (0, 0)))
    sent = jnp.concatenate([error.astype(BF), grad_state.astype(BF)], axis=1)
    got = to_all(jnp.concatenate([sent, gain_part], axis=0), MP, N_MP)
    error_all = got[:, :rows, :columns]
    grad_all = got[:, :rows, columns:].reshape(total, columns)
    grad_gain = jnp.sum(got[:, rows].astype(F32), axis=0)
    grad_gain = grad_gain[:columns] + grad_gain[columns:]

    contract_rows = (((0,), (0,)), ((), ()))
    grad_wo = lax.dot_general(
        context_cols, grad_all, contract_rows, preferred_element_type=F32
    ).astype(BF)
    grad_wo = to_all(grad_wo, MP, N_MP).reshape(width, columns)

    hidden_all = lax.all_gather(hidden_near, NEAR, axis=0, tiled=True)
    error_all = error_all.reshape(N_MP, N_XL, N_NEAR, few, columns)
    error_all = error_all.transpose(2, 0, 1, 3, 4).reshape(total, columns)
    grad_proj = -lax.dot_general(
        hidden_all, error_all, contract_rows, preferred_element_type=F32
    )
    return (grad_wo, grad_gain, grad_proj)


def solution(mesh):
    fine = Mesh(mesh.devices.reshape(SIZES), AXES)
    in_specs = (
        P(MP, DP),
        P(MP, None),
        P(MP, None),
        P(DP, MP),
        P(DP, MP),
        P(MP, DP),
        P(MP, None),
        P(MP, DP),
        P(None, DP),
        P(),
    )
    out_specs = (P(None, DP), P(DP), P(MP, DP))
    return jax.shard_map(
        on_device, mesh=fine, in_specs=in_specs, out_specs=out_specs, check_vma=False
    )
```

time: 345 us -> 283 us (0.82)
  the two profiles are of different devices: /device:TPU:1 before, /device:TPU:2 now
where the time goes in v2:
time: 283 us; the launch traced here: 281 us
  waiting for transfers between devices  141 us (50%)
  starting transfers between devices  64.7 us (23%)
  local copies, waits for them, and re-layouts  23.9 us (8%)
  blocking collectives  22.1 us (8%)
  between operations  14.6 us (5%)
  matrix products  10.1 us (4%)
  other arithmetic  4.65 us (2%)
    all_to_all x9, waiting for transfers between devices, exchange(): return lax.all_to_all(pieces, axes, 0, 0, tiled=True)  135 us
    all_to_all x9, starting transfers between devices, exchange(): return lax.all_to_all(pieces, axes, 0, 0, tiled=True)  64.6 us
    all_to_all x1, blocking collectives, exchange(): return lax.all_to_all(pieces, axes, 0, 0, tiled=True)  22.1 us
    all_gather x1, waiting for transfers between devices, on_device(): hidden_all = lax.all_gather(hidden_near, NEAR, axis=0, tiled=True)  5.76 us
  transfers between devices with their start and end apart: 11, of which 10 were waited for; matrix products, arithmetic and copies ran while one was open for 8% of the time, Pallas kernels for 0%

profile of v2, /device:TPU:2, one launch (start us, length us, event | category | flops | bytes accessed | tf_op | source)
XLA Modules:
  0.0 281.1 jit_solution(3142230047027352695)
XLA Ops:
  12.1 6.3 %all-to-all-start = ((bf16[16,128,256]{2,1,0:T(8,128)(2,1)}), bf16[16,128,256]{2,1,0:T(8,128)(2,1)S(1)}, u32[]{:S(2)}, u32[]{:S(2)}) async-start(bf16[16,128,256]{2,1,0:T(8,128)(2,1)} %broadcast_in_dim.42), calls=%async_computation | async-start | bytes 2097152 | tf_op jit(solution)/shard_map/all_to_all | solution.py:25
  20.0 16.5 %all-to-all-done = bf16[16,128,256]{2,1,0:T(8,128)(2,1)S(1)} async-done(((bf16[16,128,256]{2,1,0:T(8,128)(2,1)}), bf16[16,128,256]{2,1,0:T(8,128)(2,1)S(1)}, u32[]{:S(2)}, u32[]{:S(2)}) %all-to-all-start) | async-done | bytes 1048608 | tf_op jit(solution)/shard_map/all_to_all | solution.py:25
  37.4 2.1 fusion.5
  40.4 12.5 %all-to-all-start.1 = ((bf16[8,32,256]{2,1,0:T(8,128)(2,1)}), bf16[8,32,256]{2,1,0:T(8,128)(2,1)S(1)}, u32[]{:S(2)}, u32[]{:S(2)}) async-start(bf16[8,32,256]{2,1,0:T(8,128)(2,1)} %pad_maximum_fusion.2), calls=%async_computation.1 | async-start | bytes 262144 | tf_op jit(solution)/shard_map/all_to_all | solution.py:25
  54.3 15.7 %all-to-all-done.1 = bf16[8,32,256]{2,1,0:T(8,128)(2,1)S(1)} async-done(((bf16[8,32,256]{2,1,0:T(8,128)(2,1)}), bf16[8,32,256]{2,1,0:T(8,128)(2,1)S(1)}, u32[]{:S(2)}, u32[]{:S(2)}) %all-to-all-start.1) | async-done | bytes 131104 | tf_op jit(solution)/shard_map/all_to_all | solution.py:25
  70.0 4.4 %all-to-all-start.3 = ((bf16[16,128,256]{1,2,0:T(8,128)(2,1)}), bf16[16,128,256]{1,2,0:T(8,128)(2,1)S(1)}, u32[]{:S(2)}, u32[]{:S(2)}) async-start(bf16[16,128,256]{1,2,0:T(8,128)(2,1)} %bitcast.13), calls=%async_computation.3 | async-start | bytes 2097152 | tf_op jit(solution)/shard_map/all_to_all | solution.py:25
  74.4 18.0 %all-to-all-done.3 = bf16[16,128,256]{1,2,0:T(8,128)(2,1)S(1)} async-done(((bf16[16,128,256]{1,2,0:T(8,128)(2,1)}), bf16[16,128,256]{1,2,0:T(8,128)(2,1)S(1)}, u32[]{:S(2)}, u32[]{:S(2)}) %all-to-all-start.3) | async-done | bytes 1048608 | tf_op jit(solution)/shard_map/all_to_all | solution.py:25
  93.5 4.3 %all-to-all-start.2 = ((bf16[16,16,2048]{2,1,0:T(8,128)(2,1)}), bf16[16,16,2048]{2,1,0:T(8,128)(2,1)}, u32[]{:S(2)}, u32[]{:S(2)}) async-start(bf16[16,16,2048]{2,1,0:T(8,128)(2,1)} %broadcast_in_dim.46), calls=%async_computation.2 | async-start | bytes 2097152 | tf_op jit(solution)/shard_map/all_to_all | solution.py:25
  98.4 17.5 %all-to-all-done.2 = bf16[16,16,2048]{2,1,0:T(8,128)(2,1)} async-done(((bf16[16,16,2048]{2,1,0:T(8,128)(2,1)}), bf16[16,16,2048]{2,1,0:T(8,128)(2,1)}, u32[]{:S(2)}, u32[]{:S(2)}) %all-to-all-start.2) | async-done | bytes 1048608 | tf_op jit(solution)/shard_map/all_to_all | solution.py:25
  120.4 9.0 %all-to-all-start.4 = ((bf16[4,64,512]{2,1,0:T(8,128)(2,1)}), bf16[4,64,512]{2,1,0:T(8,128)(2,1)S(1)}, u32[]{:S(2)}, u32[]{:S(2)}) async-start(bf16[4,64,512]{2,1,0:T(8,128)(2,1)} %bitcast.21), calls=%async_computation.4 | async-start | bytes 524288 | tf_op jit(solution)/shard_map/all_to_all | solution.py:25
  130.5 12.2 %all-to-all-done.4 = bf16[4,64,512]{2,1,0:T(8,128)(2,1)S(1)} async-done(((bf16[4,64,512]{2,1,0:T(8,128)(2,1)}), bf16[4,64,512]{2,1,0:T(8,128)(2,1)S(1)}, u32[]{:S(2)}, u32[]{:S(2)}) %all-to-all-start.4) | async-done | bytes 262176 | tf_op jit(solution)/shard_map/all_to_all | solution.py:25
  143.6 4.7 %all-to-all-start.5 = ((bf16[4,64,512]{2,1,0:T(8,128)(2,1)}), bf16[4,64,512]{2,1,0:T(8,128)(2,1)S(1)}, u32[]{:S(2)}, u32[]{:S(2)}) async-start(bf16[4,64,512]{2,1,0:T(8,128)(2,1)} %broadcast_in_dim.48), calls=%async_computation.5 | async-start | bytes 524288 | tf_op jit(solution)/shard_map/all_to_all | solution.py:25
  148.3 2.3 slice.84
  152.3 9.4 %all-to-all-done.5 = bf16[4,64,512]{2,1,0:T(8,128)(2,1)S(1)} async-done(((bf16[4,64,512]{2,1,0:T(8,128)(2,1)}), bf16[4,64,512]{2,1,0:T(8,128)(2,1)S(1)}, u32[]{:S(2)}, u32[]{:S(2)}) %all-to-all-start.5) | async-done | bytes 262176 | tf_op jit(solution)/shard_map/all_to_all | solution.py:25
  165.1 7.6 %all-to-all-start.6 = ((bf16[16,16,1024]{2,1,0:T(8,128)(2,1)}), bf16[16,16,1024]{2,1,0:T(8,128)(2,1)S(1)}, u32[]{:S(2)}, u32[]{:S(2)}) async-start(bf16[16,16,1024]{2,1,0:T(8,128)(2,1)} %reshape.323), calls=%async_computation.6 | async-start | bytes 1048576 | tf_op jit(solution)/shard_map/all_to_all | solution.py:25
  172.8 12.3 %all-to-all-done.6 = bf16[16,16,1024]{2,1,0:T(8,128)(2,1)S(1)} async-done(((bf16[16,16,1024]{2,1,0:T(8,128)(2,1)}), bf16[16,16,1024]{2,1,0:T(8,128)(2,1)S(1)}, u32[]{:S(2)}, u32[]{:S(2)}) %all-to-all-start.6) | async-done | bytes 524320 | tf_op jit(solution)/shard_map/all_to_all | solution.py:25
  186.3 12.1 %all-to-all-start.7 = ((bf16[32,24,128]{2,1,0:T(8,128)(2,1)}), bf16[32,24,128]{2,1,0:T(8,128)(2,1)S(1)}, u32[]{:S(2)}, u32[]{:S(2)}) async-start(bf16[32,24,128]{2,1,0:T(8,128)(2,1)} %bitcast.35), calls=%async_computation.7 | async-start | bytes 393216 | tf_op jit(solution)/shard_map/all_to_all | solution.py:25
  199.2 17.5 %all-to-all-done.7 = bf16[32,24,128]{2,1,0:T(8,128)(2,1)S(1)} async-done(((bf16[32,24,128]{2,1,0:T(8,128)(2,1)}), bf16[32,24,128]{2,1,0:T(8,128)(2,1)S(1)}, u32[]{:S(2)}, u32[]{:S(2)}) %all-to-all-start.7) | async-done | bytes 196640 | tf_op jit(solution)/shard_map/all_to_all | solution.py:25
  217.9 22.1 %all_to_all.50 = bf16[16,136,256]{2,1,0:T(8,128)(2,1)S(1)} all-to-all(bf16[16,136,256]{2,1,0:T(8,128)(2,1)S(1)} %broadcast_in_dim.84), channel_id=1, replica_groups=mesh['zh'=2,'zn'=8,'xl'=2,'xh'=2,'y'=4,'core'=2] {'xh','y','core'}, dimensions={0} | all-to-all | bytes 2228224 | tf_op jit(solution)/shard_map/all_to_all | solution.py:25
  242.8 3.7 %all-to-all-start.9 = ((bf16[16,256,128]{2,1,0:T(8,128)(2,1)}), bf16[16,256,128]{2,1,0:T(8,128)(2,1)S(1)}, u32[]{:S(2)}, u32[]{:S(2)}) async-start(bf16[16,256,128]{2,1,0:T(8,128)(2,1)} %broadcast_in_dim.85), calls=%async_computation.9 | async-start | bytes 2097152 | tf_op jit(solution)/shard_map/all_to_all | solution.py:25
  246.4 1.9 copy.105
  248.9 15.5 %all-to-all-done.9 = bf16[16,256,128]{2,1,0:T(8,128)(2,1)S(1)} async-done(((bf16[16,256,128]{2,1,0:T(8,128)(2,1)}), bf16[16,256,128]{2,1,0:T(8,128)(2,1)S(1)}, u32[]{:S(2)}, u32[]{:S(2)}) %all-to-all-start.9) | async-done | bytes 1048608 | tf_op jit(solution)/shard_map/all_to_all | solution.py:25
  264.5 5.8 %all-gather.4.cloned.1.call-done = bf16[2048,512]{1,0:T(8,128)(2,1)} async-done(((bf16[256,512]{1,0:T(8,128)(2,1)}), bf16[2048,512]{1,0:T(8,128)(2,1)}) %all-gather.4.cloned.1.call-update) | async-done | bytes 2097168 | tf_op jit(solution)/shard_map/all_gather | solution.py:187
  270.2 3.1 %convolution_negate_fusion = f32[512,128]{1,0:T(8,128)} fusion(bf16[2048,512]{1,0:T(8,128)(2,1)} %all-gather.4.cloned.1.call-done, bf16[2048,128]{1,0:T(8,128)(2,1)} %bitcast.175), kind=kOutput, calls=%fused_computation.9 | convolution fusion | flops 268500992 | bytes 2883584 | tf_op jit(solution)/shard_map/dot_general | solution.py:190
  (97 shorter events, 30.0 us)
Async XLA Ops:
  7.2 11.4 %copy-start = (bf16[4096,128]{1,0:T(8,128)(2,1)S(1)}, bf16[4096,128]{1,0:T(8,128)(2,1)}, u32[]{:S(2)}) copy-start(bf16[4096,128]{1,0:T(8,128)(2,1)} %param.18) | copy-start | bytes 3145732
  7.2 108.8 %all-gather.6.cloned.1.call-start = ((), (), s32[]{:S(2)}) async-start(), calls=%async_computation.11 | async-start | bytes 4128768 | tf_op jit(solution)/shard_map/all_gather | solution.py:66
  10.1 8.3 %copy-start.5 = (bf16[128,128]{1,0:T(8,128)(2,1)S(1)}, bf16[128,128]{1,0:T(8,128)(2,1)}, u32[]{:S(2)}) copy-start(bf16[128,128]{1,0:T(8,128)(2,1)} %param.17) | copy-start | bytes 98308
  10.1 8.4 %copy-start.1 = (bf16[128,4096]{1,0:T(8,128)(2,1)S(1)}, bf16[128,4096]{1,0:T(8,128)(2,1)}, u32[]{:S(2)}) copy-start(bf16[128,4096]{1,0:T(8,128)(2,1)} %param.16) | copy-start | bytes 3145732
  12.1 24.3 %copy-start.7 = (bf16[128,256]{1,0:T(8,128)(2,1)S(1)}, bf16[128,256]{1,0:T(8,128)(2,1)}, u32[]{:S(2)}) copy-start(bf16[128,256]{1,0:T(8,128)(2,1)} %param.10) | copy-start | bytes 196612
  12.1 24.3 %all-to-all-start = ((bf16[16,128,256]{2,1,0:T(8,128)(2,1)}), bf16[16,128,256]{2,1,0:T(8,128)(2,1)S(1)}, u32[]{:S(2)}, u32[]{:S(2)}) async-start(bf16[16,128,256]{2,1,0:T(8,128)(2,1)} %broadcast_in_dim.42), calls=%async_computation | async-start | bytes 2097152 | tf_op jit(solution)/shard_map/all_to_all | solution.py:25
  40.4 29.5 %all-to-all-start.1 = ((bf16[8,32,256]{2,1,0:T(8,128)(2,1)}), bf16[8,32,256]{2,1,0:T(8,128)(2,1)S(1)}, u32[]{:S(2)}, u32[]{:S(2)}) async-start(bf16[8,32,256]{2,1,0:T(8,128)(2,1)} %pad_maximum_fusion.2), calls=%async_computation.1 | async-start | bytes 262144 | tf_op jit(solution)/shard_map/all_to_all | solution.py:25
  70.0 22.5 %all-to-all-start.3 = ((bf16[16,128,256]{1,2,0:T(8,128)(2,1)}), bf16[16,128,256]{1,2,0:T(8,128)(2,1)S(1)}, u32[]{:S(2)}, u32[]{:S(2)}) async-start(bf16[16,128,256]{1,2,0:T(8,128)(2,1)} %bitcast.13), calls=%async_computation.3 | async-start | bytes 2097152 | tf_op jit(solution)/shard_map/all_to_all | solution.py:25
  93.5 22.4 %all-to-all-start.2 = ((bf16[16,16,2048]{2,1,0:T(8,128)(2,1)}), bf16[16,16,2048]{2,1,0:T(8,128)(2,1)}, u32[]{:S(2)}, u32[]{:S(2)}) async-start(bf16[16,16,2048]{2,1,0:T(8,128)(2,1)} %broadcast_in_dim.46), calls=%async_computation.2 | async-start | bytes 2097152 | tf_op jit(solution)/shard_map/all_to_all | solution.py:25
  120.4 22.3 %all-to-all-start.4 = ((bf16[4,64,512]{2,1,0:T(8,128)(2,1)}), bf16[4,64,512]{2,1,0:T(8,128)(2,1)S(1)}, u32[]{:S(2)}, u32[]{:S(2)}) async-start(bf16[4,64,512]{2,1,0:T(8,128)(2,1)} %bitcast.21), calls=%async_computation.4 | async-start | bytes 524288 | tf_op jit(solution)/shard_map/all_to_all | solution.py:25
  143.6 18.1 %all-to-all-start.5 = ((bf16[4,64,512]{2,1,0:T(8,128)(2,1)}), bf16[4,64,512]{2,1,0:T(8,128)(2,1)S(1)}, u32[]{:S(2)}, u32[]{:S(2)}) async-start(bf16[4,64,512]{2,1,0:T(8,128)(2,1)} %broadcast_in_dim.48), calls=%async_computation.5 | async-start | bytes 524288 | tf_op jit(solution)/shard_map/all_to_all | solution.py:25
  161.6 0.7 copy-start.3
  163.3 1.8 copy-start.2
  163.3 9.4 %copy-start.6 = (f32[4096]{0:T(1024)S(1)}, f32[4096]{0:T(1024)}, u32[]{:S(2)}) copy-start(f32[4096]{0:T(1024)} %param.19) | copy-start | bytes 49156
  165.1 52.2 %copy-start.4 = (f32[128,128]{0,1:T(8,128)S(1)}, f32[128,128]{0,1:T(8,128)}, u32[]{:S(2)}) copy-start(f32[128,128]{0,1:T(8,128)} %get-tuple-element.24) | copy-start | bytes 196612
  165.1 20.0 %all-to-all-start.6 = ((bf16[16,16,1024]{2,1,0:T(8,128)(2,1)}), bf16[16,16,1024]{2,1,0:T(8,128)(2,1)S(1)}, u32[]{:S(2)}, u32[]{:S(2)}) async-start(bf16[16,16,1024]{2,1,0:T(8,128)(2,1)} %reshape.323), calls=%async_computation.6 | async-start | bytes 1048576 | tf_op jit(solution)/shard_map/all_to_all | solution.py:25
  186.3 30.4 %all-to-all-start.7 = ((bf16[32,24,128]{2,1,0:T(8,128)(2,1)}), bf16[32,24,128]{2,1,0:T(8,128)(2,1)S(1)}, u32[]{:S(2)}, u32[]{:S(2)}) async-start(bf16[32,24,128]{2,1,0:T(8,128)(2,1)} %bitcast.35), calls=%async_computation.7 | async-start | bytes 393216 | tf_op jit(solution)/shard_map/all_to_all | solution.py:25
  198.4 71.8 %all-gather.4.cloned.1.call-start = ((), (), s32[]{:S(2)}) async-start(), calls=%async_computation.10 | async-start | bytes 2359296 | tf_op jit(solution)/shard_map/all_gather | solution.py:187
  242.8 21.7 %all-to-all-start.9 = ((bf16[16,256,128]{2,1,0:T(8,128)(2,1)}), bf16[16,256,128]{2,1,0:T(8,128)(2,1)S(1)}, u32[]{:S(2)}, u32[]{:S(2)}) async-start(bf16[16,256,128]{2,1,0:T(8,128)(2,1)} %broadcast_in_dim.85), calls=%async_computation.9 | async-start | bytes 2097152 | tf_op jit(solution)/shard_map/all_to_all | solution.py:25
Sparse Core Ops, SparseCore 0:
  10.3 100.7 all-gather.5
  201.9 68.2 all-gather.3

commit v3 on v2

--- a/solution.py
+++ b/solution.py
@@ -1,6 +1,10 @@
+import functools
+
 import jax
 import jax.numpy as jnp
 from jax import lax
+from jax.experimental import pallas as pl
+from jax.experimental.pallas import tpu as pltpu
 from jax.sharding import Mesh
 from jax.sharding import PartitionSpec as P
 
@@ -9,13 +13,15 @@
 HEAD = 128
 EPS = 1e-05
 
-DP = ("zh", "zn", "xl")
+DP = ("zn", "zf", "xl")
 MP = ("xh", "y", "core")
 NEAR = ("zn",)
-FAR = ("zh", "xl")
+FAR = ("zf", "xl")
 AXES = DP + MP
-SIZES = (2, 8, 2, 2, 4, 2)
-N_ZH, N_XL, N_FAR, N_NEAR, N_MP = 2, 2, 4, 8, 16
+N_NEAR, N_XL, N_MP = 8, 2, 16
+N_ZF = 16 // N_NEAR
+N_FAR = N_ZF * N_XL
+SIZES = (N_NEAR, N_ZF, N_XL, 2, 4, 2)
 
 BF = jnp.bfloat16
 F32 = jnp.float32
@@ -32,6 +38,56 @@
 def split(values):
     high = values.astype(BF)
     return high, (values - high.astype(F32)).astype(BF)
+
+
+def head_sum_kernel(few, context_ref, out_ref, sum_ref, total):
+    step = pl.program_id(0)
+    context = context_ref[...]
+    rows = context.shape[0] * context.shape[2]
+    part = jnp.dot(
+        context.reshape(rows, context.shape[3]),
+        out_ref[0],
+        preferred_element_type=F32,
+    )
+
+    @pl.when(step == 0)
+    def _():
+        total[...] = part
+
+    @pl.when(step > 0)
+    def _():
+        total[...] += part
+
+    @pl.when(step == N_NEAR - 1)
+    def _():
+        for far in range(N_FAR):
+            pieces = []
+            for block in range(N_NEAR):
+                first = (block * N_FAR + far) * few
+                pieces.append(total[first : first + few])
+            sum_ref[far] = jnp.concatenate(pieces, axis=0).astype(BF)
+
+
+def head_sum(context, packed, few, head_rows):
+    n_mp, _, sub, features = context.shape
+    d_cols = packed.shape[2]
+    return pl.pallas_call(
+        functools.partial(head_sum_kernel, few),
+        grid=(N_NEAR,),
+        in_specs=[
+            pl.BlockSpec((n_mp, 1, sub, features), lambda g: (0, g, 0, 0)),
+            pl.BlockSpec((1, head_rows, d_cols), lambda g: (g, 0, 0)),
+        ],
+        out_specs=pl.BlockSpec((N_FAR, N_NEAR * few, d_cols), lambda g: (0, 0, 0)),
+        out_shape=jax.ShapeDtypeStruct((N_FAR, N_NEAR * few, d_cols), BF),
+        scratch_shapes=[pltpu.VMEM((n_mp * sub, d_cols), F32)],
+        compiler_params=pltpu.CompilerParams(vmem_limit_bytes=24 * 2**20),
+        cost_estimate=pl.CostEstimate(
+            flops=2 * n_mp * sub * features * N_NEAR * d_cols,
+            bytes_accessed=4 * 2**20,
+            transcendentals=0,
+        ),
+    )(context, packed)
 
 
 def on_device(
@@ -64,7 +120,6 @@
         [teacher_out, teacher_resid, distill_proj.reshape(-1, d_cols)], axis=0
     )
     packed_all = lax.all_gather(packed, NEAR, axis=0, tiled=False)
-    out_near = packed_all[:, :head_rows].reshape(N_NEAR * head_rows, d_cols)
     resid_near = packed_all[:, head_rows : head_rows + resid_rows]
     resid_near = resid_near.reshape(N_NEAR, N_NEAR, few, d_cols)
     resid_mine = lax.dynamic_index_in_dim(resid_near, near, 1, keepdims=False)
@@ -107,27 +162,23 @@
     got = exchange(jnp.concatenate([context, state_parts], axis=1), NEAR)
     state_parts = got[:, sub:].astype(F32)
     state_wide = state_parts[:, :, :columns] + state_parts[:, :, columns:]
-    context = got[:, :sub].transpose(1, 0, 2).reshape(sub, N_NEAR * query_width)
-    context = to_all(context, MP, N_MP).reshape(N_MP * sub, N_NEAR * query_width)
-
     part = width // N_MP
-    context_cols = exchange(
-        student_context.reshape(rows, N_MP, part).transpose(1, 0, 2), MP
-    ).reshape(total, part)
-    context, context_cols = lax.optimization_barrier((context, context_cols))
-
-    head_terms = jnp.dot(context, out_near, preferred_element_type=F32).astype(BF)
-    head_terms = head_terms.reshape(N_ZH, N_NEAR, N_XL, few, d_cols)
-    head_terms = head_terms.transpose(0, 2, 1, 3, 4)
-    head_terms = exchange(
-        head_terms.reshape(N_FAR, N_NEAR * few, d_cols), FAR
-    )
+    context = got[:, :sub].reshape(rows, query_width)
+    context = jnp.broadcast_to(context[None], (N_MP, rows, query_width))
+    sent = student_context.reshape(rows, N_MP, part).transpose(1, 0, 2)
+    got = exchange(jnp.concatenate([context, sent], axis=1), MP)
+    context_cols = got[:, rows:].reshape(total, part)
+
+    head_terms = head_sum(
+        got.reshape(N_MP, 2 * N_NEAR, sub, query_width), packed_all, few, head_rows
+    )
+    head_terms = exchange(head_terms, FAR)
     summed = jnp.sum(head_terms.astype(F32), axis=0)
     resid_mine = resid_mine.reshape(N_NEAR * few, d_cols).astype(F32)
     hidden = (resid_mine + summed).astype(BF)
     hidden_near = to_all(hidden, FAR, N_FAR)
-    hidden_near = hidden_near.reshape(N_ZH, N_XL, N_NEAR, few, d_cols)
-    hidden_near = hidden_near.transpose(0, 2, 1, 3, 4).reshape(N_MP * sub, d_cols)
+    hidden_near = hidden_near.reshape(N_FAR, N_NEAR, few, d_cols)
+    hidden_near = hidden_near.transpose(1, 0, 2, 3).reshape(N_MP * sub, d_cols)
 
     partial = jnp.einsum(
         "tk,gkc->tgc", hidden_near, proj_near, preferred_element_type=F32
@@ -136,9 +187,8 @@
     target_wide = jnp.sum(partial.astype(F32), axis=0)
     target_wide = target_wide.reshape(sub, N_NEAR, columns).transpose(1, 0, 2)
 
-    gain_wide = student_gain.reshape(N_ZH, N_NEAR, N_XL, columns)
-    gain_wide = gain_wide.transpose(0, 2, 1, 3).reshape(N_FAR, N_NEAR, columns)
-    gain_wide = lax.dynamic_index_in_dim(gain_wide, far, 0, keepdims=False)[:, None]
+    gain_wide = student_gain.reshape(N_NEAR, N_FAR, columns)
+    gain_wide = lax.dynamic_slice_in_dim(gain_wide, far, 1, 1)
     gained = state_wide * gain_wide
     sums = jnp.stack(
         [
@@ -147,20 +197,19 @@
             jnp.sum(target_wide * gained, axis=(0, 2)),
         ]
     )
-    sums = jnp.stack(split(sums)).reshape(1, 6 * sub)
-    sums = jnp.pad(sums, ((0, 7), (0, columns - 6 * sub)))
-    here = (lax.iota(jnp.int32, N_FAR) == far)[:, None, None, None]
-    sent = jnp.where(here, target_wide.astype(BF)[None], jnp.zeros((), BF))
-    sums = jnp.broadcast_to(sums, (N_FAR, N_NEAR, 8, columns))
+    sums = jnp.stack(split(sums)).reshape(6 * sub)
+    sums = jnp.pad(sums, (0, 8 * columns - 6 * sub)).reshape(8, columns)
+    here = (lax.iota(jnp.int32, N_FAR) == far)[None, :, None, None]
+    sent = jnp.where(here, target_wide.astype(BF)[:, None], jnp.zeros((), BF))
+    sums = jnp.broadcast_to(sums, (N_NEAR, N_FAR, 8, columns))
     sent = jnp.concatenate([sent, sums], axis=2)
-    sent = sent.reshape(N_ZH, N_XL, N_NEAR, sub + 8, columns)
-    sent = sent.transpose(0, 2, 1, 3, 4)
     got = exchange(sent.reshape(N_FAR * N_NEAR, sub + 8, columns), DP)
-    got = got.reshape(N_ZH, N_NEAR, N_XL, sub + 8, columns)
-    got = jnp.sum(got.astype(F32), axis=(0, 2))
+    got = got.reshape(N_NEAR, N_FAR, sub + 8, columns)
+    got = jnp.sum(got.astype(F32), axis=1)
     target = got[:, :sub].reshape(N_NEAR, N_XL, few, columns)
     target = target.transpose(1, 0, 2, 3).reshape(rows, columns)
-    sums = got[:, sub, : 6 * sub].reshape(N_NEAR, 2, 3, N_XL, few).sum(axis=1)
+    sums = got[:, sub:].reshape(N_NEAR, 8 * columns)[:, : 6 * sub]
+    sums = sums.reshape(N_NEAR, 2, 3, N_XL, few).sum(axis=1)
     sums = sums.transpose(1, 2, 0, 3).reshape(3, rows)
 
     grad_scale = total ** (-0.5)

time: 283 us -> 248 us (0.88)
  the two profiles are of different devices: /device:TPU:2 before, /device:TPU:1 now
where the time goes in v3:
time: 248 us; the launch traced here: 247 us
  waiting for transfers between devices  85.6 us (35%)
  blocking collectives  57.8 us (23%)
  starting transfers between devices  50 us (20%)
  local copies, waits for them, and re-layouts  21.8 us (9%)
  between operations  14.5 us (6%)
  matrix products  8.11 us (3%)
  other arithmetic  5.78 us (2%)
  Pallas kernels  3.09 us (1%)
    all_to_all x7, waiting for transfers between devices, exchange(): return lax.all_to_all(pieces, axes, 0, 0, tiled=True)  85.6 us
    all_to_all x2, blocking collectives, exchange(): return lax.all_to_all(pieces, axes, 0, 0, tiled=True)  57.8 us
    all_to_all x7, starting transfers between devices, exchange(): return lax.all_to_all(pieces, axes, 0, 0, tiled=True)  49.9 us
  transfers between devices with their start and end apart: 9, of which 7 were waited for; matrix products, arithmetic and copies ran while one was open for 9% of the time, Pallas kernels for 0%

profile of v3, /device:TPU:1, one launch (start us, length us, event | category | flops | bytes accessed | tf_op | source)
XLA Modules:
  0.0 246.9 jit_solution(8493548200445140276)
XLA Ops:
  8.3 1.8 pad_maximum_fusion.1
  12.1 10.5 %all-to-all-start = ((bf16[16,128,256]{2,1,0:T(8,128)(2,1)}), bf16[16,128,256]{2,1,0:T(8,128)(2,1)S(1)}, u32[]{:S(2)}, u32[]{:S(2)}) async-start(bf16[16,128,256]{2,1,0:T(8,128)(2,1)} %broadcast_in_dim.48), calls=%async_computation | async-start | bytes 2097152 | tf_op jit(solution)/shard_map/all_to_all | solution.py:31
  24.2 15.7 %all-to-all-done = bf16[16,128,256]{2,1,0:T(8,128)(2,1)S(1)} async-done(((bf16[16,128,256]{2,1,0:T(8,128)(2,1)}), bf16[16,128,256]{2,1,0:T(8,128)(2,1)S(1)}, u32[]{:S(2)}, u32[]{:S(2)}) %all-to-all-start) | async-done | bytes 1048608 | tf_op jit(solution)/shard_map/all_to_all | solution.py:31
  40.8 2.1 fusion.6
  43.8 12.8 %all-to-all-start.1 = ((bf16[8,32,256]{2,1,0:T(8,128)(2,1)}), bf16[8,32,256]{2,1,0:T(8,128)(2,1)S(1)}, u32[]{:S(2)}, u32[]{:S(2)}) async-start(bf16[8,32,256]{2,1,0:T(8,128)(2,1)} %pad_maximum_fusion.3), calls=%async_computation.1 | async-start | bytes 262144 | tf_op jit(solution)/shard_map/all_to_all | solution.py:31
  57.3 23.4 %all-to-all-done.1 = bf16[8,32,256]{2,1,0:T(8,128)(2,1)S(1)} async-done(((bf16[8,32,256]{2,1,0:T(8,128)(2,1)}), bf16[8,32,256]{2,1,0:T(8,128)(2,1)S(1)}, u32[]{:S(2)}, u32[]{:S(2)}) %all-to-all-start.1) | async-done | bytes 131104 | tf_op jit(solution)/shard_map/all_to_all | solution.py:31
  81.4 32.2 %all_to_all.45 = bf16[16,256,256]{1,2,0:T(8,128)(2,1)} all-to-all(bf16[16,256,256]{1,2,0:T(8,128)(2,1)S(1)} %pad_maximum_fusion), channel_id=1, replica_groups=mesh['zn'=8,'zf'=2,'xl'=2,'xh'=2,'y'=4,'core'=2] {'xh','y','core'}, dimensions={0} | all-to-all | bytes 4194304 | tf_op jit(solution)/shard_map/all_to_all | solution.py:31
  113.5 2.8 %copy.97 = bf16[16,256,256]{2,1,0:T(8,128)(2,1)S(1)} copy(bf16[16,256,256]{1,2,0:T(8,128)(2,1)} %all_to_all.45) | data formatting | bytes 4194304 | tf_op jit(solution)/shard_map/all_to_all | solution.py:31
  116.4 2.0 copy-done.1
  118.5 3.1 %shard_map.121 = bf16[4,64,512]{2,1,0:T(8,128)(2,1)} custom-call(bf16[16,16,16,256]{3,2,1,0:T(8,128)(2,1)S(1)} %bitcast.159, bf16[8,448,512]{2,1,0:T(8,128)(2,1)S(1)} %bitcast.162), custom_call_target="tpu_custom_call" | custom-call | flops 536870912 | bytes 4194304 | tf_op jit(solution)/shard_map/pallas_call | solution.py:74
  121.6 3.4 %all-to-all-start.3 = ((bf16[4,64,512]{2,1,0:T(8,128)(2,1)}), bf16[4,64,512]{2,1,0:T(8,128)(2,1)S(1)}, u32[]{:S(2)}, u32[]{:S(2)}) async-start(bf16[4,64,512]{2,1,0:T(8,128)(2,1)} %shard_map.121), calls=%async_computation.3 | async-start | bytes 524288 | tf_op jit(solution)/shard_map/all_to_all | solution.py:31
  126.1 3.1 %all-to-all-done.3 = bf16[4,64,512]{2,1,0:T(8,128)(2,1)S(1)} async-done(((bf16[4,64,512]{2,1,0:T(8,128)(2,1)}), bf16[4,64,512]{2,1,0:T(8,128)(2,1)S(1)}, u32[]{:S(2)}, u32[]{:S(2)}) %all-to-all-start.3) | async-done | bytes 262176 | tf_op jit(solution)/shard_map/all_to_all | solution.py:31
  129.9 4.1 %all-to-all-start.4 = ((bf16[4,64,512]{2,1,0:T(8,128)(2,1)}), bf16[4,64,512]{2,1,0:T(8,128)(2,1)}, u32[]{:S(2)}, u32[]{:S(2)}) async-start(bf16[4,64,512]{2,1,0:T(8,128)(2,1)} %broadcast_in_dim.87), calls=%async_computation.4 | async-start | bytes 524288 | tf_op jit(solution)/shard_map/all_to_all | solution.py:31
  134.0 1.3 slice.88
  136.0 2.3 all-to-all-done.4
  141.1 7.3 %all-to-all-start.5 = ((bf16[16,16,1024]{2,1,0:T(8,128)(2,1)}), bf16[16,16,1024]{2,1,0:T(8,128)(2,1)S(1)}, u32[]{:S(2)}, u32[]{:S(2)}) async-start(bf16[16,16,1024]{2,1,0:T(8,128)(2,1)} %reshape.307), calls=%async_computation.5 | async-start | bytes 1048576 | tf_op jit(solution)/shard_map/all_to_all | solution.py:31
  149.2 10.5 %all-to-all-done.5 = bf16[16,16,1024]{2,1,0:T(8,128)(2,1)S(1)} async-done(((bf16[16,16,1024]{2,1,0:T(8,128)(2,1)}), bf16[16,16,1024]{2,1,0:T(8,128)(2,1)S(1)}, u32[]{:S(2)}, u32[]{:S(2)}) %all-to-all-start.5) | async-done | bytes 524320 | tf_op jit(solution)/shard_map/all_to_all | solution.py:31
  160.9 8.0 %all-to-all-start.6 = ((bf16[32,24,128]{2,1,0:T(8,128)(2,1)}), bf16[32,24,128]{2,1,0:T(8,128)(2,1)S(1)}, u32[]{:S(2)}, u32[]{:S(2)}) async-start(bf16[32,24,128]{2,1,0:T(8,128)(2,1)} %pad_maximum_fusion.2), calls=%async_computation.6 | async-start | bytes 393216 | tf_op jit(solution)/shard_map/all_to_all | solution.py:31
  169.8 16.0 %all-to-all-done.6 = bf16[32,24,128]{2,1,0:T(8,128)(2,1)S(1)} async-done(((bf16[32,24,128]{2,1,0:T(8,128)(2,1)}), bf16[32,24,128]{2,1,0:T(8,128)(2,1)S(1)}, u32[]{:S(2)}, u32[]{:S(2)}) %all-to-all-start.6) | async-done | bytes 196640 | tf_op jit(solution)/shard_map/all_to_all | solution.py:31
  187.0 25.7 %all_to_all.46 = bf16[16,136,256]{2,1,0:T(8,128)(2,1)S(1)} all-to-all(bf16[16,136,256]{2,1,0:T(8,128)(2,1)S(1)} %broadcast_in_dim.92), channel_id=1, replica_groups=mesh['zn'=8,'zf'=2,'xl'=2,'xh'=2,'y'=4,'core'=2] {'xh','y','core'}, dimensions={0} | all-to-all | bytes 2228224 | tf_op jit(solution)/shard_map/all_to_all | solution.py:31
  213.7 1.2 broadcast_in_dim.93
  214.8 3.9 %all-to-all-start.8 = ((bf16[16,256,128]{2,1,0:T(8,128)(2,1)}), bf16[16,256,128]{2,1,0:T(8,128)(2,1)S(1)}, u32[]{:S(2)}, u32[]{:S(2)}) async-start(bf16[16,256,128]{2,1,0:T(8,128)(2,1)} %broadcast_in_dim.93), calls=%async_computation.8 | async-start | bytes 2097152 | tf_op jit(solution)/shard_map/all_to_all | solution.py:31
  221.3 14.7 %all-to-all-done.8 = bf16[16,256,128]{2,1,0:T(8,128)(2,1)S(1)} async-done(((bf16[16,256,128]{2,1,0:T(8,128)(2,1)}), bf16[16,256,128]{2,1,0:T(8,128)(2,1)S(1)}, u32[]{:S(2)}, u32[]{:S(2)}) %all-to-all-start.8) | async-done | bytes 1048608 | tf_op jit(solution)/shard_map/all_to_all | solution.py:31
  236.0 3.0 %convolution_negate_fusion = f32[512,128]{1,0:T(8,128)} fusion(bf16[2048,512]{1,0:T(8,128)(2,1)} %all-gather.4.cloned.1.call-done, bf16[2048,128]{1,0:T(8,128)(2,1)S(1)} %bitcast.168), kind=kOutput, calls=%fused_computation.9 | convolution fusion | flops 268500992 | bytes 2883584 | tf_op jit(solution)/shard_map/dot_general | solution.py:239
  (98 shorter events, 21.5 us)
Async XLA Ops:
  7.2 15.5 %copy-start = (bf16[4096,128]{1,0:T(8,128)(2,1)S(1)}, bf16[4096,128]{1,0:T(8,128)(2,1)}, u32[]{:S(2)}) copy-start(bf16[4096,128]{1,0:T(8,128)(2,1)} %param.18) | copy-start | bytes 3145732
  7.2 109.2 %all-gather.6.cloned.1.call-start = ((), (), s32[]{:S(2)}) async-start(), calls=%async_computation.10 | async-start | bytes 4128768 | tf_op jit(solution)/shard_map/all_gather | solution.py:122
  10.1 12.5 %copy-start.7 = (bf16[128,128]{1,0:T(8,128)(2,1)S(1)}, bf16[128,128]{1,0:T(8,128)(2,1)}, u32[]{:S(2)}) copy-start(bf16[128,128]{1,0:T(8,128)(2,1)} %param.17) | copy-start | bytes 98308
  10.1 12.6 %copy-start.3 = (bf16[128,4096]{1,0:T(8,128)(2,1)S(1)}, bf16[128,4096]{1,0:T(8,128)(2,1)}, u32[]{:S(2)}) copy-start(bf16[128,4096]{1,0:T(8,128)(2,1)} %param.16) | copy-start | bytes 3145732
  12.1 27.7 %copy-start.8 = (bf16[128,256]{1,0:T(8,128)(2,1)S(1)}, bf16[128,256]{1,0:T(8,128)(2,1)}, u32[]{:S(2)}) copy-start(bf16[128,256]{1,0:T(8,128)(2,1)} %param.10) | copy-start | bytes 196612
  12.1 27.7 %all-to-all-start = ((bf16[16,128,256]{2,1,0:T(8,128)(2,1)}), bf16[16,128,256]{2,1,0:T(8,128)(2,1)S(1)}, u32[]{:S(2)}, u32[]{:S(2)}) async-start(bf16[16,128,256]{2,1,0:T(8,128)(2,1)} %broadcast_in_dim.48), calls=%async_computation | async-start | bytes 2097152 | tf_op jit(solution)/shard_map/all_to_all | solution.py:31
  43.8 36.9 %all-to-all-start.1 = ((bf16[8,32,256]{2,1,0:T(8,128)(2,1)}), bf16[8,32,256]{2,1,0:T(8,128)(2,1)S(1)}, u32[]{:S(2)}, u32[]{:S(2)}) async-start(bf16[8,32,256]{2,1,0:T(8,128)(2,1)} %pad_maximum_fusion.3), calls=%async_computation.1 | async-start | bytes 262144 | tf_op jit(solution)/shard_map/all_to_all | solution.py:31
  116.4 2.0 copy-start.1
  121.6 7.6 %all-to-all-start.3 = ((bf16[4,64,512]{2,1,0:T(8,128)(2,1)}), bf16[4,64,512]{2,1,0:T(8,128)(2,1)S(1)}, u32[]{:S(2)}, u32[]{:S(2)}) async-start(bf16[4,64,512]{2,1,0:T(8,128)(2,1)} %shard_map.121), calls=%async_computation.3 | async-start | bytes 524288 | tf_op jit(solution)/shard_map/all_to_all | solution.py:31
  129.9 8.3 %all-to-all-start.4 = ((bf16[4,64,512]{2,1,0:T(8,128)(2,1)}), bf16[4,64,512]{2,1,0:T(8,128)(2,1)}, u32[]{:S(2)}, u32[]{:S(2)}) async-start(bf16[4,64,512]{2,1,0:T(8,128)(2,1)} %broadcast_in_dim.87), calls=%async_computation.4 | async-start | bytes 524288 | tf_op jit(solution)/shard_map/all_to_all | solution.py:31
  139.3 1.8 copy-start.5
  141.1 45.3 %copy-start.6 = (f32[128,128]{0,1:T(8,128)S(1)}, f32[128,128]{0,1:T(8,128)}, u32[]{:S(2)}) copy-start(f32[128,128]{0,1:T(8,128)} %get-tuple-element.18) | copy-start | bytes 196612
  141.1 18.6 %all-to-all-start.5 = ((bf16[16,16,1024]{2,1,0:T(8,128)(2,1)}), bf16[16,16,1024]{2,1,0:T(8,128)(2,1)S(1)}, u32[]{:S(2)}, u32[]{:S(2)}) async-start(bf16[16,16,1024]{2,1,0:T(8,128)(2,1)} %reshape.307), calls=%async_computation.5 | async-start | bytes 1048576 | tf_op jit(solution)/shard_map/all_to_all | solution.py:31
  160.9 24.9 %all-to-all-start.6 = ((bf16[32,24,128]{2,1,0:T(8,128)(2,1)}), bf16[32,24,128]{2,1,0:T(8,128)(2,1)S(1)}, u32[]{:S(2)}, u32[]{:S(2)}) async-start(bf16[32,24,128]{2,1,0:T(8,128)(2,1)} %pad_maximum_fusion.2), calls=%async_computation.6 | async-start | bytes 393216 | tf_op jit(solution)/shard_map/all_to_all | solution.py:31
  168.9 67.1 %all-gather.4.cloned.1.call-start = ((), (), s32[]{:S(2)}) async-start(), calls=%async_computation.9 | async-start | bytes 2359296 | tf_op jit(solution)/shard_map/all_gather | solution.py:236
  186.4 26.3 %copy-start.2 = (bf16[16,256,256]{1,2,0:T(8,128)(2,1)S(1)}, bf16[16,256,256]{1,2,0:T(8,128)(2,1)}, u32[]{:S(2)}) copy-start(bf16[16,256,256]{1,2,0:T(8,128)(2,1)} %all_to_all.45) | copy-start | bytes 6291460
  212.7 1.0 copy-start.4
  214.8 21.2 %all-to-all-start.8 = ((bf16[16,256,128]{2,1,0:T(8,128)(2,1)}), bf16[16,256,128]{2,1,0:T(8,128)(2,1)S(1)}, u32[]{:S(2)}, u32[]{:S(2)}) async-start(bf16[16,256,128]{2,1,0:T(8,128)(2,1)} %broadcast_in_dim.93), calls=%async_computation.8 | async-start | bytes 2097152 | tf_op jit(solution)/shard_map/all_to_all | solution.py:31
Sparse Core Ops, SparseCore 0:
  10.3 100.3 all-gather.5
  172.4 61.0 all-gather.3

commit v4 on v3

--- a/solution.py
+++ b/solution.py
@@ -21,6 +21,7 @@
 N_NEAR, N_XL, N_MP = 8, 2, 16
 N_ZF = 16 // N_NEAR
 N_FAR = N_ZF * N_XL
+AT_ONCE = 4
 SIZES = (N_NEAR, N_ZF, N_XL, 2, 4, 2)
 
 BF = jnp.bfloat16
@@ -44,10 +45,13 @@
     step = pl.program_id(0)
     context = context_ref[...]
     rows = context.shape[0] * context.shape[2]
-    part = jnp.dot(
-        context.reshape(rows, context.shape[3]),
-        out_ref[0],
-        preferred_element_type=F32,
+    part = sum(
+        jnp.dot(
+            context[:, device].reshape(rows, context.shape[3]),
+            out_ref[device],
+            preferred_element_type=F32,
+        )
+        for device in range(AT_ONCE)
     )
 
     @pl.when(step == 0)
@@ -58,7 +62,7 @@
     def _():
         total[...] += part
 
-    @pl.when(step == N_NEAR - 1)
+    @pl.when(step == N_NEAR // AT_ONCE - 1)
     def _():
         for far in range(N_FAR):
             pieces = []
@@ -73,21 +77,70 @@
     d_cols = packed.shape[2]
     return pl.pallas_call(
         functools.partial(head_sum_kernel, few),
-        grid=(N_NEAR,),
+        grid=(N_NEAR // AT_ONCE,),
         in_specs=[
-            pl.BlockSpec((n_mp, 1, sub, features), lambda g: (0, g, 0, 0)),
-            pl.BlockSpec((1, head_rows, d_cols), lambda g: (g, 0, 0)),
+            pl.BlockSpec((n_mp, AT_ONCE, sub, features), lambda g: (0, g, 0, 0)),
+            pl.BlockSpec((AT_ONCE, head_rows, d_cols), lambda g: (g, 0, 0)),
         ],
         out_specs=pl.BlockSpec((N_FAR, N_NEAR * few, d_cols), lambda g: (0, 0, 0)),
         out_shape=jax.ShapeDtypeStruct((N_FAR, N_NEAR * few, d_cols), BF),
         scratch_shapes=[pltpu.VMEM((n_mp * sub, d_cols), F32)],
-        compiler_params=pltpu.CompilerParams(vmem_limit_bytes=24 * 2**20),
+        compiler_params=pltpu.CompilerParams(vmem_limit_bytes=60 * 2**20),
         cost_estimate=pl.CostEstimate(
             flops=2 * n_mp * sub * features * N_NEAR * d_cols,
             bytes_accessed=4 * 2**20,
             transcendentals=0,
         ),
     )(context, packed)
+
+
+def project_kernel(hidden_ref, map_ref, out_ref, ordered):
+    columns = out_ref.shape[2] // AT_ONCE
+
+    @pl.when(pl.program_id(0) == 0)
+    def _():
+        few = hidden_ref.shape[1] // N_NEAR
+        hidden = hidden_ref[...].astype(F32)
+        pieces = []
+        for block in range(N_NEAR):
+            for far in range(N_FAR):
+                pieces.append(hidden[far, block * few : (block + 1) * few])
+        ordered[...] = jnp.concatenate(pieces, axis=0).astype(BF)
+
+    folds = map_ref.shape[2] // columns
+    for device in range(AT_ONCE):
+        folded = map_ref[device]
+        weights = jnp.concatenate(
+            [folded[:, f * columns : (f + 1) * columns] for f in range(folds)], axis=0
+        )
+        part = jnp.dot(ordered[...], weights, preferred_element_type=F32)
+        out_ref[:, :, device * columns : (device + 1) * columns] = part.astype(
+            BF
+        ).reshape(out_ref.shape[:2] + (columns,))
+
+
+def project(hidden, packed, first, sub, columns):
+    rows = hidden.shape[0] * hidden.shape[1]
+    d_cols = hidden.shape[2]
+    return pl.pallas_call(
+        project_kernel,
+        grid=(N_NEAR // AT_ONCE,),
+        in_specs=[
+            pl.BlockSpec(hidden.shape, lambda g: (0, 0, 0)),
+            pl.BlockSpec((AT_ONCE, columns, d_cols), lambda g: (g, first // columns, 0)),
+        ],
+        out_specs=pl.BlockSpec(
+            (rows // sub, sub, AT_ONCE * columns), lambda g: (0, 0, g)
+        ),
+        out_shape=jax.ShapeDtypeStruct((rows // sub, sub, N_NEAR * columns), BF),
+        scratch_shapes=[pltpu.VMEM((rows, d_cols), BF)],
+        compiler_params=pltpu.CompilerParams(vmem_limit_bytes=60 * 2**20),
+        cost_estimate=pl.CostEstimate(
+            flops=2 * rows * d_cols * N_NEAR * columns,
+            bytes_accessed=2 * 2**20,
+            transcendentals=0,
+        ),
+    )(hidden, packed)
 
 
 def on_device(
@@ -113,18 +166,16 @@
     columns = student_out.shape[1]
     width = student_context.shape[1]
     head_rows, d_cols = teacher_out.shape
-    resid_rows = teacher_resid.shape[0]
     few = sub // N_XL
 
-    packed = jnp.concatenate(
-        [teacher_out, teacher_resid, distill_proj.reshape(-1, d_cols)], axis=0
-    )
+    folds = d_cols // columns
+    folded = distill_proj.reshape(folds, columns, columns)
+    folded = folded.transpose(1, 0, 2).reshape(columns, d_cols)
+    packed = jnp.concatenate([teacher_out, folded, teacher_resid], axis=0)
     packed_all = lax.all_gather(packed, NEAR, axis=0, tiled=False)
-    resid_near = packed_all[:, head_rows : head_rows + resid_rows]
+    resid_near = packed_all[:, head_rows + columns :]
     resid_near = resid_near.reshape(N_NEAR, N_NEAR, few, d_cols)
     resid_mine = lax.dynamic_index_in_dim(resid_near, near, 1, keepdims=False)
-    proj_near = packed_all[:, head_rows + resid_rows :]
-    proj_near = proj_near.reshape(N_NEAR, d_cols, columns)
 
     def by_near(values):
         values = values.reshape(N_XL, N_NEAR, few, values.shape[-1])
@@ -177,13 +228,8 @@
     resid_mine = resid_mine.reshape(N_NEAR * few, d_cols).astype(F32)
     hidden = (resid_mine + summed).astype(BF)
     hidden_near = to_all(hidden, FAR, N_FAR)
-    hidden_near = hidden_near.reshape(N_FAR, N_NEAR, few, d_cols)
-    hidden_near = hidden_near.transpose(1, 0, 2, 3).reshape(N_MP * sub, d_cols)
-
-    partial = jnp.einsum(
-        "tk,gkc->tgc", hidden_near, proj_near, preferred_element_type=F32
-    ).astype(BF)
-    partial = exchange(partial.reshape(N_MP, sub, N_NEAR * columns), MP)
+
+    partial = exchange(project(hidden_near, packed_all, head_rows, sub, columns), MP)
     target_wide = jnp.sum(partial.astype(F32), axis=0)
     target_wide = target_wide.reshape(sub, N_NEAR, columns).transpose(1, 0, 2)
 
@@ -221,6 +267,7 @@
     gain_part = jnp.sum(error * state * inverse, axis=0)[None]
     gain_part = jnp.pad(jnp.concatenate(split(gain_part), axis=1), ((0, 7), (0, 0)))
     sent = jnp.concatenate([error.astype(BF), grad_state.astype(BF)], axis=1)
+    sent, context_cols = lax.optimization_barrier((sent, context_cols))
     got = to_all(jnp.concatenate([sent, gain_part], axis=0), MP, N_MP)
     error_all = got[:, :rows, :columns]
     grad_all = got[:, :rows, columns:].reshape(total, columns)
@@ -233,9 +280,10 @@
     ).astype(BF)
     grad_wo = to_all(grad_wo, MP, N_MP).reshape(width, columns)
 
+    hidden_near = hidden_near.reshape(N_MP * sub, d_cols)
     hidden_all = lax.all_gather(hidden_near, NEAR, axis=0, tiled=True)
-    error_all = error_all.reshape(N_MP, N_XL, N_NEAR, few, columns)
-    error_all = error_all.transpose(2, 0, 1, 3, 4).reshape(total, columns)
+    error_all = error_all.reshape(N_NEAR, N_ZF, N_XL, N_NEAR, few, columns)
+    error_all = error_all.transpose(3, 1, 2, 0, 4, 5).reshape(total, columns)
     grad_proj = -lax.dot_general(
         hidden_all, error_all, contract_rows, preferred_element_type=F32
     )

time: 248 us -> 245 us (0.988)
  blocking collectives: 57.8 us -> 70.5 us
  local copies, waits for them, and re-layouts: 21.8 us -> 14.3 us
  waiting for transfers between devices: 85.6 us -> 78.1 us
  starting transfers between devices: 50 us -> 46.2 us
  Pallas kernels: 3.09 us -> 5.77 us
    all_to_all x2 -> x3, blocking collectives: 57.8 us -> 70.5 us  [exchange(): return lax.all_to_all(pieces, axes, 0, 0, tiled=True)]
    all_to_all x7 -> x6, waiting for transfers between devices: 85.6 us -> 78.1 us  [exchange(): return lax.all_to_all(pieces, axes, 0, 0, tiled=True)]
    all_to_all x7 -> x6, starting transfers between devices: 49.9 us -> 46.1 us  [exchange(): return lax.all_to_all(pieces, axes, 0, 0, tiled=True)]
    unnamed x23 -> x14, local copies, waits for them, and re-layouts: 4.41 us -> 1.12 us
    all_to_all x1 -> x0, local copies, waits for them, and re-layouts: 2.85 us -> none  [exchange(): return lax.all_to_all(pieces, axes, 0, 0, tiled=True)]
    pallas_call x1 -> x2, Pallas kernels: 3.09 us -> 5.77 us  [the longest x1 3.08 us: head_sum(): pl.pallas_call(functools.partial(head_sum_kernel, few), grid=(N_NEAR // A...]
  transfers between devices with their start and end apart: 9 -> 8, of which waited for: 7 -> 6; matrix products, arithmetic and copies ran while one was open for 9% -> 8% of each run, Pallas kernels for 0% -> 0%
where the time goes in v4:
time: 245 us; the launch traced here: 244 us
  waiting for transfers between devices  78.1 us (32%)
  blocking collectives  70.5 us (29%)
  starting transfers between devices  46.2 us (19%)
  between operations  14.5 us (6%)
  local copies, waits for them, and re-layouts  14.3 us (6%)
  matrix products  8.65 us (4%)
  other arithmetic  5.88 us (2%)
  Pallas kernels  5.77 us (2%)
    all_to_all x6, waiting for transfers between devices, exchange(): return lax.all_to_all(pieces, axes, 0, 0, tiled=True)  78.1 us
    all_to_all x3, blocking collectives, exchange(): return lax.all_to_all(pieces, axes, 0, 0, tiled=True)  70.5 us
    all_to_all x6, starting transfers between devices, exchange(): return lax.all_to_all(pieces, axes, 0, 0, tiled=True)  46.1 us
  transfers between devices with their start and end apart: 8, of which 6 were waited for; matrix products, arithmetic and copies ran while one was open for 8% of the time, Pallas kernels for 0%

profile of v4, /device:TPU:1, one launch (start us, length us, event | category | flops | bytes accessed | tf_op | source)
XLA Modules:
  0.0 243.9 jit_solution(9040128121343703954)
XLA Ops:
  8.2 1.8 pad_maximum_fusion.1
  12.0 10.3 %all-to-all-start = ((bf16[16,128,256]{2,1,0:T(8,128)(2,1)}), bf16[16,128,256]{2,1,0:T(8,128)(2,1)S(1)}, u32[]{:S(2)}, u32[]{:S(2)}) async-start(bf16[16,128,256]{2,1,0:T(8,128)(2,1)} %broadcast_in_dim.82), calls=%async_computation | async-start | bytes 2097152 | tf_op jit(solution)/shard_map/all_to_all | solution.py:32
  23.3 16.3 %all-to-all-done = bf16[16,128,256]{2,1,0:T(8,128)(2,1)S(1)} async-done(((bf16[16,128,256]{2,1,0:T(8,128)(2,1)}), bf16[16,128,256]{2,1,0:T(8,128)(2,1)S(1)}, u32[]{:S(2)}, u32[]{:S(2)}) %all-to-all-start) | async-done | bytes 1048608 | tf_op jit(solution)/shard_map/all_to_all | solution.py:32
  39.7 1.8 fusion.42
  41.5 2.8 %fusion.5 = bf16[128,2,128]{0,2,1:T(8,128)(2,1)} fusion(f32[2,128]{1,0:T(2,128)S(1)} %fusion.42, bf16[2048,256]{1,0:T(8,128)(2,1)S(1)} %bitcast.176, pred[128,2048]{0,1:T(8,128)(4,1)S(1)} %iota_compare_fusion, bf16[128,256]{1,0:T(8,128)(2,1)} %param.10), kind=kOutput, calls=%fused_computation.11 | convolution fusion | flops 271091968 | bytes 1442816 | tf_op jit(solution)/shard_map/rqk,kd->qrd/dot_general | solution.py:202
  45.9 12.9 %all-to-all-start.1 = ((bf16[8,32,256]{2,1,0:T(8,128)(2,1)}), bf16[8,32,256]{2,1,0:T(8,128)(2,1)S(1)}, u32[]{:S(2)}, u32[]{:S(2)}) async-start(bf16[8,32,256]{2,1,0:T(8,128)(2,1)} %pad_maximum_fusion.3), calls=%async_computation.1 | async-start | bytes 262144 | tf_op jit(solution)/shard_map/all_to_all | solution.py:32
  58.9 18.4 %all-to-all-done.1 = bf16[8,32,256]{2,1,0:T(8,128)(2,1)S(1)} async-done(((bf16[8,32,256]{2,1,0:T(8,128)(2,1)}), bf16[8,32,256]{2,1,0:T(8,128)(2,1)S(1)}, u32[]{:S(2)}, u32[]{:S(2)}) %all-to-all-start.1) | async-done | bytes 131104 | tf_op jit(solution)/shard_map/all_to_all | solution.py:32
  77.6 37.5 %all_to_all.45 = bf16[16,256,256]{2,1,0:T(8,128)(2,1)} all-to-all(bf16[16,256,256]{2,1,0:T(8,128)(2,1)S(1)} %pad_maximum_fusion), channel_id=1, replica_groups=mesh['zn'=8,'zf'=2,'xl'=2,'xh'=2,'y'=4,'core'=2] {'xh','y','core'}, dimensions={0} | all-to-all | bytes 4194304 | tf_op jit(solution)/shard_map/all_to_all | solution.py:32
  115.1 3.1 %shard_map.121 = bf16[4,64,512]{2,1,0:T(8,128)(2,1)} custom-call(bf16[16,16,16,256]{3,2,1,0:T(8,128)(2,1)} %bitcast.166, bf16[8,448,512]{2,1,0:T(8,128)(2,1)} %bitcast.163), custom_call_target="tpu_custom_call" | custom-call | flops 536870912 | bytes 4194304 | tf_op jit(solution)/shard_map/pallas_call | solution.py:78
  118.2 3.4 %all-to-all-start.3 = ((bf16[4,64,512]{2,1,0:T(8,128)(2,1)}), bf16[4,64,512]{2,1,0:T(8,128)(2,1)S(1)}, u32[]{:S(2)}, u32[]{:S(2)}) async-start(bf16[4,64,512]{2,1,0:T(8,128)(2,1)} %shard_map.121), calls=%async_computation.3 | async-start | bytes 524288 | tf_op jit(solution)/shard_map/all_to_all | solution.py:32
  122.7 3.1 %all-to-all-done.3 = bf16[4,64,512]{2,1,0:T(8,128)(2,1)S(1)} async-done(((bf16[4,64,512]{2,1,0:T(8,128)(2,1)}), bf16[4,64,512]{2,1,0:T(8,128)(2,1)S(1)}, u32[]{:S(2)}, u32[]{:S(2)}) %all-to-all-start.3) | async-done | bytes 262176 | tf_op jit(solution)/shard_map/all_to_all | solution.py:32
  125.9 7.6 %all_to_all.46.hidden_ref = bf16[4,64,512]{2,1,0:T(8,128)(2,1)} all-to-all(bf16[4,64,512]{2,1,0:T(8,128)(2,1)S(1)} %broadcast_in_dim.87), channel_id=1, replica_groups=mesh['zn'=8,'zf'=2,'xl'=2,'xh'=2,'y'=4,'core'=2] {'zf','xl'}, dimensions={0} | all-to-all | bytes 524288 | tf_op jit(solution)/shard_map/all_to_all | solution.py:32
  133.5 2.7 %shard_map.122 = bf16[16,16,1024]{2,1,0:T(8,128)(2,1)} custom-call(bf16[4,64,512]{2,1,0:T(8,128)(2,1)} %all_to_all.46.hidden_ref, bf16[8,448,512]{2,1,0:T(8,128)(2,1)} %bitcast.165), custom_call_target="tpu_custom_call" | custom-call | flops 268435456 | bytes 2097152 | tf_op jit(solution)/shard_map/pallas_call | solution.py:125
  136.2 8.0 %all-to-all-start.5 = ((bf16[16,16,1024]{2,1,0:T(8,128)(2,1)}), bf16[16,16,1024]{2,1,0:T(8,128)(2,1)}, u32[]{:S(2)}, u32[]{:S(2)}) async-start(bf16[16,16,1024]{2,1,0:T(8,128)(2,1)} %shard_map.122), calls=%async_computation.5 | async-start | bytes 1048576 | tf_op jit(solution)/shard_map/all_to_all | solution.py:32
  145.0 10.6 %all-to-all-done.5 = bf16[16,16,1024]{2,1,0:T(8,128)(2,1)} async-done(((bf16[16,16,1024]{2,1,0:T(8,128)(2,1)}), bf16[16,16,1024]{2,1,0:T(8,128)(2,1)}, u32[]{:S(2)}, u32[]{:S(2)}) %all-to-all-start.5) | async-done | bytes 524320 | tf_op jit(solution)/shard_map/all_to_all | solution.py:32
  155.6 1.1 convert_reduce_fusion
  157.9 7.7 %all-to-all-start.6 = ((bf16[32,24,128]{2,1,0:T(8,128)(2,1)}), bf16[32,24,128]{2,1,0:T(8,128)(2,1)S(1)}, u32[]{:S(2)}, u32[]{:S(2)}) async-start(bf16[32,24,128]{2,1,0:T(8,128)(2,1)} %pad_maximum_fusion.2), calls=%async_computation.6 | async-start | bytes 393216 | tf_op jit(solution)/shard_map/all_to_all | solution.py:32
  167.4 14.9 %all-to-all-done.6 = bf16[32,24,128]{2,1,0:T(8,128)(2,1)S(1)} async-done(((bf16[32,24,128]{2,1,0:T(8,128)(2,1)}), bf16[32,24,128]{2,1,0:T(8,128)(2,1)S(1)}, u32[]{:S(2)}, u32[]{:S(2)}) %all-to-all-start.6) | async-done | bytes 196640 | tf_op jit(solution)/shard_map/all_to_all | solution.py:32
  183.6 25.4 %all_to_all.47 = bf16[16,136,256]{2,1,0:T(8,128)(2,1)S(1)} all-to-all(bf16[16,136,256]{2,1,0:T(8,128)(2,1)S(1)} %broadcast_in_dim.92), channel_id=1, replica_groups=mesh['zn'=8,'zf'=2,'xl'=2,'xh'=2,'y'=4,'core'=2] {'xh','y','core'}, dimensions={0} | all-to-all | bytes 2228224 | tf_op jit(solution)/shard_map/all_to_all | solution.py:32
  210.6 1.2 broadcast_in_dim.93
  211.8 3.9 %all-to-all-start.8 = ((bf16[16,256,128]{2,1,0:T(8,128)(2,1)}), bf16[16,256,128]{2,1,0:T(8,128)(2,1)S(1)}, u32[]{:S(2)}, u32[]{:S(2)}) async-start(bf16[16,256,128]{2,1,0:T(8,128)(2,1)} %broadcast_in_dim.93), calls=%async_computation.8 | async-start | bytes 2097152 | tf_op jit(solution)/shard_map/all_to_all | solution.py:32
  215.7 2.0 copy.109
  218.2 14.8 %all-to-all-done.8 = bf16[16,256,128]{2,1,0:T(8,128)(2,1)S(1)} async-done(((bf16[16,256,128]{2,1,0:T(8,128)(2,1)}), bf16[16,256,128]{2,1,0:T(8,128)(2,1)S(1)}, u32[]{:S(2)}, u32[]{:S(2)}) %all-to-all-start.8) | async-done | bytes 1048608 | tf_op jit(solution)/shard_map/all_to_all | solution.py:32
  233.0 3.1 %convolution_negate_fusion = f32[512,128]{1,0:T(8,128)} fusion(bf16[2048,512]{1,0:T(8,128)(2,1)} %all-gather.4.cloned.1.call-done, bf16[2048,128]{1,0:T(8,128)(2,1)} %bitcast.173), kind=kOutput, calls=%fused_computation.8 | convolution fusion | flops 268500992 | bytes 2883584 | tf_op jit(solution)/shard_map/dot_general | solution.py:287
  (84 shorter events, 15.1 us)
Async XLA Ops:
  7.2 15.3 %copy-start = (bf16[4096,128]{1,0:T(8,128)(2,1)S(1)}, bf16[4096,128]{1,0:T(8,128)(2,1)}, u32[]{:S(2)}) copy-start(bf16[4096,128]{1,0:T(8,128)(2,1)} %param.18) | copy-start | bytes 3145732
  7.2 107.9 %all-gather.6.cloned.1.call-start = ((), (), s32[]{:S(2)}) async-start(), calls=%async_computation.10 | async-start | bytes 4128768 | tf_op jit(solution)/shard_map/all_gather | solution.py:175
  10.0 12.3 %copy-start.4 = (bf16[128,128]{1,0:T(8,128)(2,1)S(1)}, bf16[128,128]{1,0:T(8,128)(2,1)}, u32[]{:S(2)}) copy-start(bf16[128,128]{1,0:T(8,128)(2,1)} %param.17) | copy-start | bytes 98308
  10.0 12.5 %copy-start.2 = (bf16[128,4096]{1,0:T(8,128)(2,1)S(1)}, bf16[128,4096]{1,0:T(8,128)(2,1)}, u32[]{:S(2)}) copy-start(bf16[128,4096]{1,0:T(8,128)(2,1)} %param.16) | copy-start | bytes 3145732
  12.0 27.6 %all-to-all-start = ((bf16[16,128,256]{2,1,0:T(8,128)(2,1)}), bf16[16,128,256]{2,1,0:T(8,128)(2,1)S(1)}, u32[]{:S(2)}, u32[]{:S(2)}) async-start(bf16[16,128,256]{2,1,0:T(8,128)(2,1)} %broadcast_in_dim.82), calls=%async_computation | async-start | bytes 2097152 | tf_op jit(solution)/shard_map/all_to_all | solution.py:32
  45.9 31.4 %all-to-all-start.1 = ((bf16[8,32,256]{2,1,0:T(8,128)(2,1)}), bf16[8,32,256]{2,1,0:T(8,128)(2,1)S(1)}, u32[]{:S(2)}, u32[]{:S(2)}) async-start(bf16[8,32,256]{2,1,0:T(8,128)(2,1)} %pad_maximum_fusion.3), calls=%async_computation.1 | async-start | bytes 262144 | tf_op jit(solution)/shard_map/all_to_all | solution.py:32
  118.2 7.6 %all-to-all-start.3 = ((bf16[4,64,512]{2,1,0:T(8,128)(2,1)}), bf16[4,64,512]{2,1,0:T(8,128)(2,1)S(1)}, u32[]{:S(2)}, u32[]{:S(2)}) async-start(bf16[4,64,512]{2,1,0:T(8,128)(2,1)} %shard_map.121), calls=%async_computation.3 | async-start | bytes 524288 | tf_op jit(solution)/shard_map/all_to_all | solution.py:32
  136.2 30.2 %copy-start.1 = (bf16[16,256,256]{2,1,0:T(8,128)(2,1)S(1)}, bf16[16,256,256]{2,1,0:T(8,128)(2,1)}, u32[]{:S(2)}) copy-start(bf16[16,256,256]{2,1,0:T(8,128)(2,1)} %all_to_all.45) | copy-start | bytes 6291460
  136.2 19.4 %all-to-all-start.5 = ((bf16[16,16,1024]{2,1,0:T(8,128)(2,1)}), bf16[16,16,1024]{2,1,0:T(8,128)(2,1)}, u32[]{:S(2)}, u32[]{:S(2)}) async-start(bf16[16,16,1024]{2,1,0:T(8,128)(2,1)} %shard_map.122), calls=%async_computation.5 | async-start | bytes 1048576 | tf_op jit(solution)/shard_map/all_to_all | solution.py:32
  157.9 24.5 %all-to-all-start.6 = ((bf16[32,24,128]{2,1,0:T(8,128)(2,1)}), bf16[32,24,128]{2,1,0:T(8,128)(2,1)S(1)}, u32[]{:S(2)}, u32[]{:S(2)}) async-start(bf16[32,24,128]{2,1,0:T(8,128)(2,1)} %pad_maximum_fusion.2), calls=%async_computation.6 | async-start | bytes 393216 | tf_op jit(solution)/shard_map/all_to_all | solution.py:32
  165.6 67.4 %all-gather.4.cloned.1.call-start = ((), (), s32[]{:S(2)}) async-start(), calls=%async_computation.9 | async-start | bytes 2359296 | tf_op jit(solution)/shard_map/all_gather | solution.py:284
  183.6 26.5 %copy-start.3 = (bf16[16,128,256]{2,1,0:T(8,128)(2,1)S(1)}, bf16[16,128,256]{2,1,0:T(8,128)(2,1)}, u32[]{:S(2)}) copy-start(bf16[16,128,256]{2,1,0:T(8,128)(2,1)} %slice.92) | copy-start | bytes 3145732
  211.8 21.2 %all-to-all-start.8 = ((bf16[16,256,128]{2,1,0:T(8,128)(2,1)}), bf16[16,256,128]{2,1,0:T(8,128)(2,1)S(1)}, u32[]{:S(2)}, u32[]{:S(2)}) async-start(bf16[16,256,128]{2,1,0:T(8,128)(2,1)} %broadcast_in_dim.93), calls=%async_computation.8 | async-start | bytes 2097152 | tf_op jit(solution)/shard_map/all_to_all | solution.py:32
Sparse Core Ops, SparseCore 0:
  10.2 101.4 all-gather.5
  168.5 61.2 all-gather.3

commit v5 on v4

--- a/solution.py
+++ b/solution.py
@@ -141,6 +141,89 @@
             transcendentals=0,
         ),
     )(hidden, packed)
+
+
+def attend_kernel(few, place_ref, query_ref, kv_ref, state_ref, out_ref):
+    rows = query_ref.shape[0]
+    heads = query_ref.shape[1] // HEAD
+    total = kv_ref.shape[0] * kv_ref.shape[1]
+    sub = N_XL * few
+    kv = kv_ref[...].reshape(total, 2 * HEAD)
+    keys, values = kv[:, :HEAD], kv[:, HEAD:]
+    query_pos = place_ref[0] * rows + lax.broadcasted_iota(
+        jnp.int32, (rows, total), 0
+    )
+    allowed = query_pos >= lax.broadcasted_iota(jnp.int32, (rows, total), 1)
+    found = []
+    for head in range(heads):
+        scores = lax.dot_general(
+            query_ref[:, head * HEAD : (head + 1) * HEAD],
+            keys,
+            (((1,), (1,)), ((), ())),
+            preferred_element_type=F32,
+        ) * HEAD ** (-0.5)
+        scores = jnp.where(allowed, scores, -jnp.inf)
+        weights = jnp.exp(scores - jnp.max(scores, axis=1, keepdims=True))
+        probs = (weights / jnp.sum(weights, axis=1, keepdims=True)).astype(BF)
+        found.append(jnp.dot(probs, values, preferred_element_type=F32))
+    context = jnp.concatenate(found, axis=1)
+    for device in range(N_NEAR):
+        pieces = []
+        for xl in range(N_XL):
+            first = (xl * N_NEAR + device) * few
+            pieces.append(context[first : first + few])
+        out_ref[device, :sub] = jnp.concatenate(pieces, axis=0).astype(BF)
+        out_ref[device, sub:] = state_ref[device]
+
+
+def attend(place, query, kv, state_parts, few):
+    near, sub, features = state_parts.shape
+    total = kv.shape[0] * kv.shape[1]
+    vmem = pl.BlockSpec(memory_space=pltpu.VMEM)
+    return pl.pallas_call(
+        functools.partial(attend_kernel, few),
+        in_specs=[pl.BlockSpec(memory_space=pltpu.SMEM), vmem, vmem, vmem],
+        out_specs=vmem,
+        out_shape=jax.ShapeDtypeStruct((near, 2 * sub, features), BF),
+        compiler_params=pltpu.CompilerParams(vmem_limit_bytes=40 * 2**20),
+        cost_estimate=pl.CostEstimate(
+            flops=4 * query.shape[0] * query.shape[1] * total,
+            bytes_accessed=2 * 2**20,
+            transcendentals=query.shape[0] * query.shape[1] // HEAD * total,
+        ),
+    )(place, query, kv, state_parts)
+
+
+def weight_kernel(context_ref, grad_ref, out_ref):
+    blocks, rows, part = context_ref.shape
+    columns = out_ref.shape[2]
+    grad = lax.dot_general(
+        context_ref[...].reshape(blocks * rows, part),
+        grad_ref[:, :, columns:].reshape(blocks * rows, columns),
+        (((0,), (0,)), ((), ())),
+        preferred_element_type=F32,
+    )
+    out_ref[...] = jnp.broadcast_to(grad.astype(BF)[None], out_ref.shape)
+
+
+def weight_grad(got, sent, rows, columns):
+    blocks, _, part = got.shape
+    return pl.pallas_call(
+        weight_kernel,
+        grid=(1,),
+        in_specs=[
+            pl.BlockSpec((blocks, rows, part), lambda g: (0, 1, 0)),
+            pl.BlockSpec((blocks, rows, 2 * columns), lambda g: (0, 0, 0)),
+        ],
+        out_specs=pl.BlockSpec((blocks, part, columns), lambda g: (0, 0, 0)),
+        out_shape=jax.ShapeDtypeStruct((blocks, part, columns), BF),
+        compiler_params=pltpu.CompilerParams(vmem_limit_bytes=40 * 2**20),
+        cost_estimate=pl.CostEstimate(
+            flops=2 * blocks * rows * part * columns,
+            bytes_accessed=3 * 2**20,
+            transcendentals=0,
+        ),
+    )(got, sent)
 
 
 def on_device(
@@ -185,23 +268,6 @@
     key_mine = lax.dynamic_slice_in_dim(teacher_keys, kv_start * HEAD, HEAD, 1)
     value_mine = lax.dynamic_slice_in_dim(teacher_values, kv_start * HEAD, HEAD, 1)
     kv_all = to_all(jnp.concatenate([key_mine, value_mine], axis=1), MP, N_MP)
-    kv_all = kv_all.reshape(total, 2 * HEAD)
-    keyed = kv_all[:, :HEAD]
-    valued = kv_all[:, HEAD:]
-    queries = teacher_query.reshape(rows, local_heads, HEAD)
-    scores = jnp.einsum(
-        "qrd,kd->rqk", queries, keyed, preferred_element_type=F32
-    ) * HEAD ** (-0.5)
-    query_pos = mp_index * rows + lax.iota(jnp.int32, rows)
-    key_pos = lax.iota(jnp.int32, total)
-    allowed = query_pos[:, None] >= key_pos[None, :]
-    scores = jnp.where(allowed, scores, -jnp.inf)
-    top = jnp.max(scores, axis=-1, keepdims=True)
-    weights = jnp.exp(scores - top)
-    probs = (weights / jnp.sum(weights, axis=-1, keepdims=True)).astype(BF)
-    context = jnp.einsum("rqk,kd->qrd", probs, valued, preferred_element_type=F32)
-    context = by_near(context.astype(BF).reshape(rows, query_width))
-
     state = student_resid.astype(F32) + jnp.dot(
         student_context, student_out, preferred_element_type=F32
     )
@@ -210,7 +276,8 @@
     state_high, state_low = split(state)
     state_parts = jnp.concatenate([state_high, state_low], axis=1)
     state_parts = by_near(state_parts)
-    got = exchange(jnp.concatenate([context, state_parts], axis=1), NEAR)
+    place = jnp.full((1,), mp_index, jnp.int32)
+    got = exchange(attend(place, teacher_query, kv_all, state_parts, few), NEAR)
     state_parts = got[:, sub:].astype(F32)
     state_wide = state_parts[:, :, :columns] + state_parts[:, :, columns:]
     part = width // N_MP
@@ -218,7 +285,7 @@
     context = jnp.broadcast_to(context[None], (N_MP, rows, query_width))
     sent = student_context.reshape(rows, N_MP, part).transpose(1, 0, 2)
     got = exchange(jnp.concatenate([context, sent], axis=1), MP)
-    context_cols = got[:, rows:].reshape(total, part)
+    context_cols = got
 
     head_terms = head_sum(
         got.reshape(N_MP, 2 * N_NEAR, sub, query_width), packed_all, few, head_rows
@@ -267,18 +334,14 @@
     gain_part = jnp.sum(error * state * inverse, axis=0)[None]
     gain_part = jnp.pad(jnp.concatenate(split(gain_part), axis=1), ((0, 7), (0, 0)))
     sent = jnp.concatenate([error.astype(BF), grad_state.astype(BF)], axis=1)
-    sent, context_cols = lax.optimization_barrier((sent, context_cols))
     got = to_all(jnp.concatenate([sent, gain_part], axis=0), MP, N_MP)
     error_all = got[:, :rows, :columns]
-    grad_all = got[:, :rows, columns:].reshape(total, columns)
     grad_gain = jnp.sum(got[:, rows].astype(F32), axis=0)
     grad_gain = grad_gain[:columns] + grad_gain[columns:]
 
     contract_rows = (((0,), (0,)), ((), ()))
-    grad_wo = lax.dot_general(
-        context_cols, grad_all, contract_rows, preferred_element_type=F32
-    ).astype(BF)
-    grad_wo = to_all(grad_wo, MP, N_MP).reshape(width, columns)
+    grad_wo = weight_grad(context_cols, got, rows, columns)
+    grad_wo = exchange(grad_wo, MP).reshape(width, columns)
 
     hidden_near = hidden_near.reshape(N_MP * sub, d_cols)
     hidden_all = lax.all_gather(hidden_near, NEAR, axis=0, tiled=True)
@@ -287,6 +350,7 @@
     grad_proj = -lax.dot_general(
         hidden_all, error_all, contract_rows, preferred_element_type=F32
     )
+    grad_wo, grad_proj = lax.optimization_barrier((grad_wo, grad_proj))
     return (grad_wo, grad_gain, grad_proj)
 
 

time: 245 us -> 241 us (0.984)
  matrix products: 8.65 us -> 3.53 us
  starting transfers between devices: 46.2 us -> 50 us
  Pallas kernels: 5.77 us -> 8.59 us
  blocking collectives: 70.5 us -> 67.7 us
    all_to_all x6, waiting for transfers between devices: 78.1 us -> 65.6 us  [exchange(): return lax.all_to_all(pieces, axes, 0, 0, tiled=True)]
    all_gather x1, waiting for transfers between devices: 0.01 us -> 12.1 us  [on_device(): hidden_all = lax.all_gather(hidden_near, NEAR, axis=0, tiled=True)]
    all_to_all x6, starting transfers between devices: 46.1 us -> 49.9 us  [exchange(): return lax.all_to_all(pieces, axes, 0, 0, tiled=True)]
    dot_general x2 -> x0, matrix products: 3.23 us -> none  [the longest x1 2.75 us: on_device(): jnp.einsum('rqk,kd->qrd', probs, valued, preferred_element_type=F32)]
    all_to_all x3, blocking collectives: 70.5 us -> 67.7 us  [exchange(): return lax.all_to_all(pieces, axes, 0, 0, tiled=True)]
    pallas_call x0 -> x2, Pallas kernels: none -> 2.82 us  [the longest x1 2.29 us: attend(): pl.pallas_call(functools.partial(attend_kernel, few), in_specs=[pl.BlockS...]
    unnamed x14 -> x19, local copies, waits for them, and re-layouts: 1.12 us -> 3.74 us
  transfers between devices with their start and end apart: 8 -> 8, of which waited for: 6 -> 7; matrix products, arithmetic and copies ran while one was open for 8% -> 6% of each run, Pallas kernels for 0% -> 1%
where the time goes in v5:
time: 241 us; the launch traced here: 239 us
  waiting for transfers between devices  78.1 us (32%)
  blocking collectives  67.7 us (28%)
  starting transfers between devices  50 us (21%)
  between operations  14.5 us (6%)
  local copies, waits for them, and re-layouts  12.2 us (5%)
  Pallas kernels  8.59 us (4%)
  other arithmetic  4.81 us (2%)
  matrix products  3.53 us (1%)
    all_to_all x3, blocking collectives, exchange(): return lax.all_to_all(pieces, axes, 0, 0, tiled=True)  67.7 us
    all_to_all x6, waiting for transfers between devices, exchange(): return lax.all_to_all(pieces, axes, 0, 0, tiled=True)  65.6 us
    all_to_all x6, starting transfers between devices, exchange(): return lax.all_to_all(pieces, axes, 0, 0, tiled=True)  49.9 us
    all_gather x1, waiting for transfers between devices, on_device(): hidden_all = lax.all_gather(hidden_near, NEAR, axis=0, tiled=True)  12.1 us
  transfers between devices with their start and end apart: 8, of which 7 were waited for; matrix products, arithmetic and copies ran while one was open for 6% of the time, Pallas kernels for 1%

profile of v5, /device:TPU:1, one launch (start us, length us, event | category | flops | bytes accessed | tf_op | source)
XLA Modules:
  0.0 239.5 jit_solution(7667273148626332056)
XLA Ops:
  7.2 1.0 copy.84
  8.2 1.8 pad_maximum_fusion.1
  11.0 1.1 broadcast_in_dim.65
  12.0 10.5 %all-to-all-start = ((bf16[16,128,256]{2,1,0:T(8,128)(2,1)}), bf16[16,128,256]{2,1,0:T(8,128)(2,1)S(1)}, u32[]{:S(2)}, u32[]{:S(2)}) async-start(bf16[16,128,256]{2,1,0:T(8,128)(2,1)} %broadcast_in_dim.65), calls=%async_computation | async-start | bytes 2097152 | tf_op jit(solution)/shard_map/all_to_all | solution.py:32
  23.3 16.5 %all-to-all-done.kv_ref = bf16[16,128,256]{2,1,0:T(8,128)(2,1)S(1)} async-done(((bf16[16,128,256]{2,1,0:T(8,128)(2,1)}), bf16[16,128,256]{2,1,0:T(8,128)(2,1)S(1)}, u32[]{:S(2)}, u32[]{:S(2)}) %all-to-all-start) | async-done | bytes 1048608 | tf_op jit(solution)/shard_map/all_to_all | solution.py:32
  39.8 2.3 shard_map.121
  42.1 12.9 %all-to-all-start.1 = ((bf16[8,32,256]{2,1,0:T(8,128)(2,1)}), bf16[8,32,256]{2,1,0:T(8,128)(2,1)S(1)}, u32[]{:S(2)}, u32[]{:S(2)}) async-start(bf16[8,32,256]{2,1,0:T(8,128)(2,1)} %shard_map.121), calls=%async_computation.1 | async-start | bytes 262144 | tf_op jit(solution)/shard_map/all_to_all | solution.py:32
  56.1 19.1 %all-to-all-done.1 = bf16[8,32,256]{2,1,0:T(8,128)(2,1)S(1)} async-done(((bf16[8,32,256]{2,1,0:T(8,128)(2,1)}), bf16[8,32,256]{2,1,0:T(8,128)(2,1)S(1)}, u32[]{:S(2)}, u32[]{:S(2)}) %all-to-all-start.1) | async-done | bytes 131104 | tf_op jit(solution)/shard_map/all_to_all | solution.py:32
  75.5 34.7 %all_to_all.45.context_ref = bf16[16,256,256]{2,1,0:T(8,128)(2,1)} all-to-all(bf16[16,256,256]{2,1,0:T(8,128)(2,1)S(1)} %pad_maximum_fusion), channel_id=1, replica_groups=mesh['zn'=8,'zf'=2,'xl'=2,'xh'=2,'y'=4,'core'=2] {'xh','y','core'}, dimensions={0} | all-to-all | bytes 4194304 | tf_op jit(solution)/shard_map/all_to_all | solution.py:32
  110.6 3.1 %shard_map.122 = bf16[4,64,512]{2,1,0:T(8,128)(2,1)} custom-call(bf16[16,16,16,256]{3,2,1,0:T(8,128)(2,1)} %bitcast.93, bf16[8,448,512]{2,1,0:T(8,128)(2,1)} %bitcast.95), custom_call_target="tpu_custom_call" | custom-call | flops 536870912 | bytes 4194304 | tf_op jit(solution)/shard_map/pallas_call | solution.py:78
  113.7 4.7 %all-to-all-start.3 = ((bf16[4,64,512]{2,1,0:T(8,128)(2,1)}), bf16[4,64,512]{2,1,0:T(8,128)(2,1)S(1)}, u32[]{:S(2)}, u32[]{:S(2)}) async-start(bf16[4,64,512]{2,1,0:T(8,128)(2,1)} %shard_map.122), calls=%async_computation.3 | async-start | bytes 524288 | tf_op jit(solution)/shard_map/all_to_all | solution.py:32
  118.3 1.1 slice_bitcast_fusion
  119.4 3.6 %all-to-all-done.3 = bf16[4,64,512]{2,1,0:T(8,128)(2,1)S(1)} async-done(((bf16[4,64,512]{2,1,0:T(8,128)(2,1)}), bf16[4,64,512]{2,1,0:T(8,128)(2,1)S(1)}, u32[]{:S(2)}, u32[]{:S(2)}) %all-to-all-start.3) | async-done | bytes 262176 | tf_op jit(solution)/shard_map/all_to_all | solution.py:32
  123.1 7.6 %all_to_all.46.hidden_ref = bf16[4,64,512]{2,1,0:T(8,128)(2,1)} all-to-all(bf16[4,64,512]{2,1,0:T(8,128)(2,1)S(1)} %broadcast_in_dim.71), channel_id=1, replica_groups=mesh['zn'=8,'zf'=2,'xl'=2,'xh'=2,'y'=4,'core'=2] {'zf','xl'}, dimensions={0} | all-to-all | bytes 524288 | tf_op jit(solution)/shard_map/all_to_all | solution.py:32
  130.8 2.7 %shard_map.123 = bf16[16,16,1024]{2,1,0:T(8,128)(2,1)} custom-call(bf16[4,64,512]{2,1,0:T(8,128)(2,1)} %all_to_all.46.hidden_ref, bf16[8,448,512]{2,1,0:T(8,128)(2,1)} %bitcast.97), custom_call_target="tpu_custom_call" | custom-call | flops 268435456 | bytes 2097152 | tf_op jit(solution)/shard_map/pallas_call | solution.py:125
  133.4 9.7 %all-to-all-start.5 = ((bf16[16,16,1024]{2,1,0:T(8,128)(2,1)}), bf16[16,16,1024]{2,1,0:T(8,128)(2,1)S(1)}, u32[]{:S(2)}, u32[]{:S(2)}) async-start(bf16[16,16,1024]{2,1,0:T(8,128)(2,1)} %shard_map.123), calls=%async_computation.5 | async-start | bytes 1048576 | tf_op jit(solution)/shard_map/all_to_all | solution.py:32
  144.0 10.5 %all-to-all-done.5 = bf16[16,16,1024]{2,1,0:T(8,128)(2,1)S(1)} async-done(((bf16[16,16,1024]{2,1,0:T(8,128)(2,1)}), bf16[16,16,1024]{2,1,0:T(8,128)(2,1)S(1)}, u32[]{:S(2)}, u32[]{:S(2)}) %all-to-all-start.5) | async-done | bytes 524320 | tf_op jit(solution)/shard_map/all_to_all | solution.py:32
  155.7 8.3 %all-to-all-start.6 = ((bf16[32,24,128]{2,1,0:T(8,128)(2,1)}), bf16[32,24,128]{2,1,0:T(8,128)(2,1)S(1)}, u32[]{:S(2)}, u32[]{:S(2)}) async-start(bf16[32,24,128]{2,1,0:T(8,128)(2,1)} %pad_maximum_fusion.2), calls=%async_computation.6 | async-start | bytes 393216 | tf_op jit(solution)/shard_map/all_to_all | solution.py:32
  164.9 16.0 %all-to-all-done.6 = bf16[32,24,128]{2,1,0:T(8,128)(2,1)S(1)} async-done(((bf16[32,24,128]{2,1,0:T(8,128)(2,1)}), bf16[32,24,128]{2,1,0:T(8,128)(2,1)S(1)}, u32[]{:S(2)}, u32[]{:S(2)}) %all-to-all-start.6) | async-done | bytes 196640 | tf_op jit(solution)/shard_map/all_to_all | solution.py:32
  182.1 25.3 %all_to_all.47.grad_ref = bf16[16,136,256]{2,1,0:T(8,128)(2,1)S(1)} all-to-all(bf16[16,136,256]{2,1,0:T(8,128)(2,1)S(1)} %broadcast_in_dim.76), channel_id=1, replica_groups=mesh['zn'=8,'zf'=2,'xl'=2,'xh'=2,'y'=4,'core'=2] {'xh','y','core'}, dimensions={0} | all-to-all | bytes 2228224 | tf_op jit(solution)/shard_map/all_to_all | solution.py:32
  209.9 3.9 %all-to-all-start.8 = ((bf16[16,256,128]{2,1,0:T(8,128)(2,1)}), bf16[16,256,128]{2,1,0:T(8,128)(2,1)S(1)}, u32[]{:S(2)}, u32[]{:S(2)}) async-start(bf16[16,256,128]{2,1,0:T(8,128)(2,1)} %copy-done.3), calls=%async_computation.8 | async-start | bytes 2097152 | tf_op jit(solution)/shard_map/all_to_all | solution.py:32
  213.8 1.1 slice.74
  216.5 12.1 %all-gather.4.cloned.1.call-done = bf16[2048,512]{1,0:T(8,128)(2,1)} async-done(((bf16[256,512]{1,0:T(8,128)(2,1)}), bf16[2048,512]{1,0:T(8,128)(2,1)}) %all-gather.4.cloned.1.call-update) | async-done | bytes 2097168 | tf_op jit(solution)/shard_map/all_gather | solution.py:347
  228.6 3.0 %convolution_negate_fusion = f32[512,128]{1,0:T(8,128)} fusion(bf16[2048,512]{1,0:T(8,128)(2,1)} %all-gather.4.cloned.1.call-done, bf16[2048,128]{1,0:T(8,128)(2,1)S(1)} %bitcast.103), kind=kOutput, calls=%fused_computation.1 | convolution fusion | flops 268500992 | bytes 2883584 | tf_op jit(solution)/shard_map/dot_general | solution.py:350
  (79 shorter events, 12.5 us)
Async XLA Ops:
  7.2 15.5 %copy-start = (bf16[4096,128]{1,0:T(8,128)(2,1)S(1)}, bf16[4096,128]{1,0:T(8,128)(2,1)}, u32[]{:S(2)}) copy-start(bf16[4096,128]{1,0:T(8,128)(2,1)} %param.18) | copy-start | bytes 3145732
  7.2 103.4 %all-gather.6.cloned.1.call-start = ((), (), s32[]{:S(2)}) async-start(), calls=%async_computation.10 | async-start | bytes 4128768 | tf_op jit(solution)/shard_map/all_gather | solution.py:258
  10.0 12.5 %copy-start.6 = (bf16[128,128]{1,0:T(8,128)(2,1)S(1)}, bf16[128,128]{1,0:T(8,128)(2,1)}, u32[]{:S(2)}) copy-start(bf16[128,128]{1,0:T(8,128)(2,1)} %param.17) | copy-start | bytes 98308
  10.0 12.6 %copy-start.5 = (bf16[128,4096]{1,0:T(8,128)(2,1)S(1)}, bf16[128,4096]{1,0:T(8,128)(2,1)}, u32[]{:S(2)}) copy-start(bf16[128,4096]{1,0:T(8,128)(2,1)} %param.16) | copy-start | bytes 3145732
  12.0 27.7 %copy-start.4 = (bf16[128,256]{1,0:T(8,128)(2,1)S(1)}, bf16[128,256]{1,0:T(8,128)(2,1)}, u32[]{:S(2)}) copy-start(bf16[128,256]{1,0:T(8,128)(2,1)} %query_ref.1) | copy-start | bytes 196612
  12.0 27.7 %all-to-all-start = ((bf16[16,128,256]{2,1,0:T(8,128)(2,1)}), bf16[16,128,256]{2,1,0:T(8,128)(2,1)S(1)}, u32[]{:S(2)}, u32[]{:S(2)}) async-start(bf16[16,128,256]{2,1,0:T(8,128)(2,1)} %broadcast_in_dim.65), calls=%async_computation | async-start | bytes 2097152 | tf_op jit(solution)/shard_map/all_to_all | solution.py:32
  42.1 33.2 %all-to-all-start.1 = ((bf16[8,32,256]{2,1,0:T(8,128)(2,1)}), bf16[8,32,256]{2,1,0:T(8,128)(2,1)S(1)}, u32[]{:S(2)}, u32[]{:S(2)}) async-start(bf16[8,32,256]{2,1,0:T(8,128)(2,1)} %shard_map.121), calls=%async_computation.1 | async-start | bytes 262144 | tf_op jit(solution)/shard_map/all_to_all | solution.py:32
  113.7 9.4 %all-to-all-start.3 = ((bf16[4,64,512]{2,1,0:T(8,128)(2,1)}), bf16[4,64,512]{2,1,0:T(8,128)(2,1)S(1)}, u32[]{:S(2)}, u32[]{:S(2)}) async-start(bf16[4,64,512]{2,1,0:T(8,128)(2,1)} %shard_map.122), calls=%async_computation.3 | async-start | bytes 524288 | tf_op jit(solution)/shard_map/all_to_all | solution.py:32
  133.4 21.0 %all-to-all-start.5 = ((bf16[16,16,1024]{2,1,0:T(8,128)(2,1)}), bf16[16,16,1024]{2,1,0:T(8,128)(2,1)S(1)}, u32[]{:S(2)}, u32[]{:S(2)}) async-start(bf16[16,16,1024]{2,1,0:T(8,128)(2,1)} %shard_map.123), calls=%async_computation.5 | async-start | bytes 1048576 | tf_op jit(solution)/shard_map/all_to_all | solution.py:32
  155.7 25.2 %all-to-all-start.6 = ((bf16[32,24,128]{2,1,0:T(8,128)(2,1)}), bf16[32,24,128]{2,1,0:T(8,128)(2,1)S(1)}, u32[]{:S(2)}, u32[]{:S(2)}) async-start(bf16[32,24,128]{2,1,0:T(8,128)(2,1)} %pad_maximum_fusion.2), calls=%async_computation.6 | async-start | bytes 393216 | tf_op jit(solution)/shard_map/all_to_all | solution.py:32
  164.0 64.6 %all-gather.4.cloned.1.call-start = ((), (), s32[]{:S(2)}) async-start(), calls=%async_computation.9 | async-start | bytes 2359296 | tf_op jit(solution)/shard_map/all_gather | solution.py:347
  181.5 25.9 %copy-start.1 = (bf16[16,256,256]{2,1,0:T(8,128)(2,1)S(1)}, bf16[16,256,256]{2,1,0:T(8,128)(2,1)}, u32[]{:S(2)}) copy-start(bf16[16,256,256]{2,1,0:T(8,128)(2,1)} %all_to_all.45.context_ref) | copy-start | bytes 6291460
  208.0 1.0 copy-start.2
  209.0 1.0 copy-start.3
  209.9 21.7 %all-to-all-start.8 = ((bf16[16,256,128]{2,1,0:T(8,128)(2,1)}), bf16[16,256,128]{2,1,0:T(8,128)(2,1)S(1)}, u32[]{:S(2)}, u32[]{:S(2)}) async-start(bf16[16,256,128]{2,1,0:T(8,128)(2,1)} %copy-done.3), calls=%async_computation.8 | async-start | bytes 2097152 | tf_op jit(solution)/shard_map/all_to_all | solution.py:32
Sparse Core Ops, SparseCore 0:
  10.2 100.3 all-gather.5
  167.0 61.6 all-gather.3

commit v6 on v5

--- a/solution.py
+++ b/solution.py
@@ -143,11 +143,10 @@
     )(hidden, packed)
 
 
-def attend_kernel(few, place_ref, query_ref, kv_ref, state_ref, out_ref):
+def attend_kernel(few, place_ref, query_ref, kv_ref, more_ref, out_ref):
     rows = query_ref.shape[0]
     heads = query_ref.shape[1] // HEAD
     total = kv_ref.shape[0] * kv_ref.shape[1]
-    sub = N_XL * few
     kv = kv_ref[...].reshape(total, 2 * HEAD)
     keys, values = kv[:, :HEAD], kv[:, HEAD:]
     query_pos = place_ref[0] * rows + lax.broadcasted_iota(
@@ -172,58 +171,83 @@
         for xl in range(N_XL):
             first = (xl * N_NEAR + device) * few
             pieces.append(context[first : first + few])
-        out_ref[device, :sub] = jnp.concatenate(pieces, axis=0).astype(BF)
-        out_ref[device, sub:] = state_ref[device]
-
-
-def attend(place, query, kv, state_parts, few):
-    near, sub, features = state_parts.shape
+        out_ref[device, :, : heads * HEAD] = jnp.concatenate(pieces, axis=0).astype(BF)
+        out_ref[device, :, heads * HEAD :] = more_ref[device]
+
+
+def attend(place, query, kv, more, few):
+    near, sub, extra = more.shape
     total = kv.shape[0] * kv.shape[1]
     vmem = pl.BlockSpec(memory_space=pltpu.VMEM)
     return pl.pallas_call(
         functools.partial(attend_kernel, few),
         in_specs=[pl.BlockSpec(memory_space=pltpu.SMEM), vmem, vmem, vmem],
         out_specs=vmem,
-        out_shape=jax.ShapeDtypeStruct((near, 2 * sub, features), BF),
+        out_shape=jax.ShapeDtypeStruct((near, sub, query.shape[1] + extra), BF),
         compiler_params=pltpu.CompilerParams(vmem_limit_bytes=40 * 2**20),
         cost_estimate=pl.CostEstimate(
             flops=4 * query.shape[0] * query.shape[1] * total,
             bytes_accessed=2 * 2**20,
             transcendentals=query.shape[0] * query.shape[1] // HEAD * total,
         ),
-    )(place, query, kv, state_parts)
-
-
-def weight_kernel(context_ref, grad_ref, out_ref):
-    blocks, rows, part = context_ref.shape
-    columns = out_ref.shape[2]
-    grad = lax.dot_general(
-        context_ref[...].reshape(blocks * rows, part),
-        grad_ref[:, :, columns:].reshape(blocks * rows, columns),
-        (((0,), (0,)), ((), ())),
-        preferred_element_type=F32,
-    )
-    out_ref[...] = jnp.broadcast_to(grad.astype(BF)[None], out_ref.shape)
-
-
-def weight_grad(got, sent, rows, columns):
-    blocks, _, part = got.shape
+    )(place, query, kv, more)
+
+
+def weight_kernel(context_ref, grad_ref, tail_ref, out_ref):
+    blocks = out_ref.shape[0]
+    part = context_ref.shape[1] // blocks
+    for block in range(blocks):
+        out_ref[block, :part] = lax.dot_general(
+            context_ref[:, block * part : (block + 1) * part],
+            grad_ref[...],
+            (((0,), (0,)), ((), ())),
+            preferred_element_type=F32,
+        ).astype(BF)
+        out_ref[block, part:] = tail_ref[...]
+
+
+def weight_parts(context, grad, tail):
+    part = context.shape[1] // N_MP
+    vmem = pl.BlockSpec(memory_space=pltpu.VMEM)
     return pl.pallas_call(
         weight_kernel,
+        in_specs=[vmem] * 3,
+        out_specs=vmem,
+        out_shape=jax.ShapeDtypeStruct(
+            (N_MP, part + tail.shape[0], tail.shape[1]), BF
+        ),
+        compiler_params=pltpu.CompilerParams(vmem_limit_bytes=40 * 2**20),
+        cost_estimate=pl.CostEstimate(
+            flops=2 * context.shape[0] * context.shape[1] * grad.shape[1],
+            bytes_accessed=3 * 2**20,
+            transcendentals=0,
+        ),
+    )(context, grad, tail)
+
+
+def sum_kernel(parts_ref, out_ref):
+    total = parts_ref[0].astype(F32)
+    for block in range(1, parts_ref.shape[0]):
+        total += parts_ref[block].astype(F32)
+    out_ref[...] = jnp.broadcast_to(total.astype(BF)[None], out_ref.shape)
+
+
+def weight_sum(got, part):
+    blocks, _, columns = got.shape
+    whole = pl.BlockSpec((blocks, part, columns), lambda g: (0, 0, 0))
+    return pl.pallas_call(
+        sum_kernel,
         grid=(1,),
-        in_specs=[
-            pl.BlockSpec((blocks, rows, part), lambda g: (0, 1, 0)),
-            pl.BlockSpec((blocks, rows, 2 * columns), lambda g: (0, 0, 0)),
-        ],
-        out_specs=pl.BlockSpec((blocks, part, columns), lambda g: (0, 0, 0)),
+        in_specs=[whole],
+        out_specs=whole,
         out_shape=jax.ShapeDtypeStruct((blocks, part, columns), BF),
         compiler_params=pltpu.CompilerParams(vmem_limit_bytes=40 * 2**20),
         cost_estimate=pl.CostEstimate(
-            flops=2 * blocks * rows * part * columns,
-            bytes_accessed=3 * 2**20,
+            flops=blocks * part * columns,
+            bytes_accessed=2 * 2**20,
             transcendentals=0,
         ),
-    )(got, sent)
+    )(got)
 
 
 def on_device(
@@ -254,11 +278,8 @@
     folds = d_cols // columns
     folded = distill_proj.reshape(folds, columns, columns)
     folded = folded.transpose(1, 0, 2).reshape(columns, d_cols)
-    packed = jnp.concatenate([teacher_out, folded, teacher_resid], axis=0)
+    packed = jnp.concatenate([teacher_out, folded], axis=0)
     packed_all = lax.all_gather(packed, NEAR, axis=0, tiled=False)
-    resid_near = packed_all[:, head_rows + columns :]
-    resid_near = resid_near.reshape(N_NEAR, N_NEAR, few, d_cols)
-    resid_mine = lax.dynamic_index_in_dim(resid_near, near, 1, keepdims=False)
 
     def by_near(values):
         values = values.reshape(N_XL, N_NEAR, few, values.shape[-1])
@@ -273,22 +294,22 @@
     )
     gain = lax.dynamic_slice_in_dim(student_gain, dp_index * columns, columns, 0)
 
-    state_high, state_low = split(state)
-    state_parts = jnp.concatenate([state_high, state_low], axis=1)
-    state_parts = by_near(state_parts)
+    half = d_cols // 2
+    resid_parts = teacher_resid.reshape(N_NEAR, few, 2, half)
+    resid_parts = resid_parts.transpose(0, 2, 1, 3).reshape(N_NEAR, sub, half)
+    more = jnp.concatenate([by_near(state.astype(BF)), resid_parts], axis=2)
     place = jnp.full((1,), mp_index, jnp.int32)
-    got = exchange(attend(place, teacher_query, kv_all, state_parts, few), NEAR)
-    state_parts = got[:, sub:].astype(F32)
-    state_wide = state_parts[:, :, :columns] + state_parts[:, :, columns:]
+    got = exchange(attend(place, teacher_query, kv_all, more, few), NEAR)
+    state_wide = got[:, :, query_width : query_width + columns].astype(F32)
+    resid_mine = got[:, :, query_width + columns :]
+    resid_mine = resid_mine.reshape(N_NEAR, 2, few, half).transpose(0, 2, 1, 3)
+
     part = width // N_MP
-    context = got[:, :sub].reshape(rows, query_width)
-    context = jnp.broadcast_to(context[None], (N_MP, rows, query_width))
-    sent = student_context.reshape(rows, N_MP, part).transpose(1, 0, 2)
-    got = exchange(jnp.concatenate([context, sent], axis=1), MP)
-    context_cols = got
+    context = got[:, :, :query_width].reshape(rows, query_width)
+    got = to_all(context, MP, N_MP)
 
     head_terms = head_sum(
-        got.reshape(N_MP, 2 * N_NEAR, sub, query_width), packed_all, few, head_rows
+        got.reshape(N_MP, N_NEAR, sub, query_width), packed_all, few, head_rows
     )
     head_terms = exchange(head_terms, FAR)
     summed = jnp.sum(head_terms.astype(F32), axis=0)
@@ -332,16 +353,16 @@
     error = (state * inverse * gain - target) * grad_scale
     grad_state = inverse * error * gain - state * (inverse**3 * inner[:, None])
     gain_part = jnp.sum(error * state * inverse, axis=0)[None]
-    gain_part = jnp.pad(jnp.concatenate(split(gain_part), axis=1), ((0, 7), (0, 0)))
-    sent = jnp.concatenate([error.astype(BF), grad_state.astype(BF)], axis=1)
-    got = to_all(jnp.concatenate([sent, gain_part], axis=0), MP, N_MP)
-    error_all = got[:, :rows, :columns]
-    grad_gain = jnp.sum(got[:, rows].astype(F32), axis=0)
-    grad_gain = grad_gain[:columns] + grad_gain[columns:]
+    tail = jnp.concatenate(
+        [error.astype(BF), *split(gain_part), jnp.zeros((14, columns), BF)], axis=0
+    )
 
     contract_rows = (((0,), (0,)), ((), ()))
-    grad_wo = weight_grad(context_cols, got, rows, columns)
-    grad_wo = exchange(grad_wo, MP).reshape(width, columns)
+    got = exchange(weight_parts(student_context, grad_state.astype(BF), tail), MP)
+    grad_wo = exchange(weight_sum(got, part), MP).reshape(width, columns)
+    error_all = got[:, part : part + rows]
+    first = part + rows
+    grad_gain = jnp.sum(got[:, first : first + 2].astype(F32), axis=(0, 1))
 
     hidden_near = hidden_near.reshape(N_MP * sub, d_cols)
     hidden_all = lax.all_gather(hidden_near, NEAR, axis=0, tiled=True)

time: 241 us -> 240 us (level)
  blocking collectives: 67.7 us -> 106 us
  waiting for transfers between devices: 78.1 us -> 59.4 us
  starting transfers between devices: 50 us -> 35.2 us
  local copies, waits for them, and re-layouts: 12.2 us -> 8.66 us
    all_to_all x3 -> x5, blocking collectives: 67.7 us -> 106 us  [exchange(): return lax.all_to_all(pieces, axes, 0, 0, tiled=True)]
    all_to_all x6 -> x4, waiting for transfers between devices: 65.6 us -> 47.9 us  [exchange(): return lax.all_to_all(pieces, axes, 0, 0, tiled=True)]
    all_to_all x6 -> x4, starting transfers between devices: 49.9 us -> 35.1 us  [exchange(): return lax.all_to_all(pieces, axes, 0, 0, tiled=True)]
    all_gather x1, waiting for transfers between devices: 12.1 us -> 8.81 us  [on_device(): hidden_all = lax.all_gather(hidden_near, NEAR, axis=0, tiled=True)]
  transfers between devices with their start and end apart: 8 -> 6, of which waited for: 7 -> 6; matrix products, arithmetic and copies ran while one was open for 6% -> 4% of each run, Pallas kernels for 1% -> 1%
where the time goes in v6:
time: 240 us; the launch traced here: 239 us
  blocking collectives  106 us (44%)
  waiting for transfers between devices  59.4 us (25%)
  starting transfers between devices  35.2 us (15%)
  between operations  14.4 us (6%)
  local copies, waits for them, and re-layouts  8.66 us (4%)
  Pallas kernels  8.18 us (3%)
  other arithmetic  3.74 us (2%)
  matrix products  3.46 us (1%)
    all_to_all x5, blocking collectives, exchange(): return lax.all_to_all(pieces, axes, 0, 0, tiled=True)  106 us
    all_to_all x4, waiting for transfers between devices, exchange(): return lax.all_to_all(pieces, axes, 0, 0, tiled=True)  47.9 us
    all_to_all x4, starting transfers between devices, exchange(): return lax.all_to_all(pieces, axes, 0, 0, tiled=True)  35.1 us
    all_gather x1, waiting for transfers between devices, on_device(): hidden_all = lax.all_gather(hidden_near, NEAR, axis=0, tiled=True)  8.81 us
  transfers between devices with their start and end apart: 6, of which 6 were waited for; matrix products, arithmetic and copies ran while one was open for 4% of the time, Pallas kernels for 1%

profile of v6, /device:TPU:1, one launch (start us, length us, event | category | flops | bytes accessed | tf_op | source)
XLA Modules:
  0.0 238.8 jit_solution(16357017836892559340)
XLA Ops:
  7.2 1.0 copy.51
  8.2 1.7 pad_maximum_fusion
  10.9 1.1 broadcast_in_dim.65
  12.0 10.5 %all-to-all-start = ((bf16[16,128,256]{2,1,0:T(8,128)(2,1)}), bf16[16,128,256]{2,1,0:T(8,128)(2,1)S(1)}, u32[]{:S(2)}, u32[]{:S(2)}) async-start(bf16[16,128,256]{2,1,0:T(8,128)(2,1)} %broadcast_in_dim.65), calls=%async_computation | async-start | bytes 2097152 | tf_op jit(solution)/shard_map/all_to_all | solution.py:32
  22.9 16.8 %all-to-all-done.kv_ref = bf16[16,128,256]{2,1,0:T(8,128)(2,1)S(1)} async-done(((bf16[16,128,256]{2,1,0:T(8,128)(2,1)}), bf16[16,128,256]{2,1,0:T(8,128)(2,1)S(1)}, u32[]{:S(2)}, u32[]{:S(2)}) %all-to-all-start) | async-done | bytes 1048608 | tf_op jit(solution)/shard_map/all_to_all | solution.py:32
  39.7 1.6 shard_map.121
  41.3 36.9 %all_to_all.45 = bf16[8,16,640]{2,1,0:T(8,128)(2,1)S(1)} all-to-all(bf16[8,16,640]{2,1,0:T(8,128)(2,1)S(1)} %shard_map.121), channel_id=1, replica_groups=mesh['zn'=8,'zf'=2,'xl'=2,'xh'=2,'y'=4,'core'=2] {'zn'}, dimensions={0} | all-to-all | bytes 327680 | tf_op jit(solution)/shard_map/all_to_all | solution.py:32
  78.3 22.3 %all_to_all.46 = bf16[16,128,256]{2,1,0:T(8,128)(2,1)} all-to-all(bf16[16,128,256]{2,1,0:T(8,128)(2,1)S(1)} %broadcast_in_dim.67), channel_id=1, replica_groups=mesh['zn'=8,'zf'=2,'xl'=2,'xh'=2,'y'=4,'core'=2] {'xh','y','core'}, dimensions={0} | all-to-all | bytes 2097152 | tf_op jit(solution)/shard_map/all_to_all | solution.py:32
  100.6 2.6 %all-gather.6.cloned.1.call-done = bf16[3072,512]{1,0:T(8,128)(2,1)} async-done(((bf16[384,512]{1,0:T(8,128)(2,1)}), bf16[3072,512]{1,0:T(8,128)(2,1)}) %all-gather.6.cloned.1.call-update) | async-done | bytes 3145744 | tf_op jit(solution)/shard_map/all_gather | solution.py:282
  103.2 3.1 %shard_map.122 = bf16[4,64,512]{2,1,0:T(8,128)(2,1)} custom-call(bf16[16,8,16,256]{3,2,1,0:T(8,128)(2,1)} %bitcast.104, bf16[8,384,512]{2,1,0:T(8,128)(2,1)} %bitcast.102), custom_call_target="tpu_custom_call" | custom-call | flops 536870912 | bytes 4194304 | tf_op jit(solution)/shard_map/pallas_call | solution.py:78
  106.3 8.1 %all_to_all.47 = bf16[4,64,512]{2,1,0:T(8,128)(2,1)S(1)} all-to-all(bf16[4,64,512]{2,1,0:T(8,128)(2,1)} %shard_map.122), channel_id=1, replica_groups=mesh['zn'=8,'zf'=2,'xl'=2,'xh'=2,'y'=4,'core'=2] {'zf','xl'}, dimensions={0} | all-to-all | bytes 524288 | tf_op jit(solution)/shard_map/all_to_all | solution.py:32
  114.5 7.6 %all_to_all.48.hidden_ref = bf16[4,64,512]{2,1,0:T(8,128)(2,1)} all-to-all(bf16[4,64,512]{2,1,0:T(8,128)(2,1)S(1)} %broadcast_in_dim.68), channel_id=1, replica_groups=mesh['zn'=8,'zf'=2,'xl'=2,'xh'=2,'y'=4,'core'=2] {'zf','xl'}, dimensions={0} | all-to-all | bytes 524288 | tf_op jit(solution)/shard_map/all_to_all | solution.py:32
  122.1 2.7 %shard_map.123 = bf16[16,16,1024]{2,1,0:T(8,128)(2,1)} custom-call(bf16[4,64,512]{2,1,0:T(8,128)(2,1)} %all_to_all.48.hidden_ref, bf16[8,384,512]{2,1,0:T(8,128)(2,1)} %bitcast.103), custom_call_target="tpu_custom_call" | custom-call | flops 268435456 | bytes 2097152 | tf_op jit(solution)/shard_map/pallas_call | solution.py:125
  124.8 9.9 %all-to-all-start.5 = ((bf16[16,16,1024]{2,1,0:T(8,128)(2,1)}), bf16[16,16,1024]{2,1,0:T(8,128)(2,1)S(1)}, u32[]{:S(2)}, u32[]{:S(2)}) async-start(bf16[16,16,1024]{2,1,0:T(8,128)(2,1)} %shard_map.123), calls=%async_computation.5 | async-start | bytes 1048576 | tf_op jit(solution)/shard_map/all_to_all | solution.py:32
  135.5 10.5 %all-to-all-done.5 = bf16[16,16,1024]{2,1,0:T(8,128)(2,1)S(1)} async-done(((bf16[16,16,1024]{2,1,0:T(8,128)(2,1)}), bf16[16,16,1024]{2,1,0:T(8,128)(2,1)S(1)}, u32[]{:S(2)}, u32[]{:S(2)}) %all-to-all-start.5) | async-done | bytes 524320 | tf_op jit(solution)/shard_map/all_to_all | solution.py:32
  147.2 10.3 %all-to-all-start.6 = ((bf16[32,24,128]{2,1,0:T(8,128)(2,1)}), bf16[32,24,128]{2,1,0:T(8,128)(2,1)S(1)}, u32[]{:S(2)}, u32[]{:S(2)}) async-start(bf16[32,24,128]{2,1,0:T(8,128)(2,1)} %pad_maximum_fusion.1), calls=%async_computation.6 | async-start | bytes 393216 | tf_op jit(solution)/shard_map/all_to_all | solution.py:32
  158.4 15.9 %all-to-all-done.6 = bf16[32,24,128]{2,1,0:T(8,128)(2,1)S(1)} async-done(((bf16[32,24,128]{2,1,0:T(8,128)(2,1)}), bf16[32,24,128]{2,1,0:T(8,128)(2,1)S(1)}, u32[]{:S(2)}, u32[]{:S(2)}) %all-to-all-start.6) | async-done | bytes 196640 | tf_op jit(solution)/shard_map/all_to_all | solution.py:32
  175.6 30.9 %all_to_all.49.parts_ref = bf16[16,400,128]{2,1,0:T(8,128)(2,1)S(1)} all-to-all(bf16[16,400,128]{2,1,0:T(8,128)(2,1)S(1)} %shard_map.124), channel_id=1, replica_groups=mesh['zn'=8,'zf'=2,'xl'=2,'xh'=2,'y'=4,'core'=2] {'xh','y','core'}, dimensions={0} | all-to-all | bytes 3276800 | tf_op jit(solution)/shard_map/all_to_all | solution.py:32
  206.8 1.0 copy-done.2
  207.8 4.5 %all-to-all-start.8 = ((bf16[16,256,128]{2,1,0:T(8,128)(2,1)}), bf16[16,256,128]{2,1,0:T(8,128)(2,1)}, u32[]{:S(2)}, u32[]{:S(2)}) async-start(bf16[16,256,128]{2,1,0:T(8,128)(2,1)} %copy-done.2), calls=%async_computation.8 | async-start | bytes 2097152 | tf_op jit(solution)/shard_map/all_to_all | solution.py:32
  213.0 8.8 %all-gather.4.cloned.1.call-done = bf16[2048,512]{1,0:T(8,128)(2,1)} async-done(((bf16[256,512]{1,0:T(8,128)(2,1)}), bf16[2048,512]{1,0:T(8,128)(2,1)}) %all-gather.4.cloned.1.call-update) | async-done | bytes 2097168 | tf_op jit(solution)/shard_map/all_gather | solution.py:368
  221.8 3.0 %convolution_negate_fusion = f32[512,128]{1,0:T(8,128)} fusion(bf16[2048,512]{1,0:T(8,128)(2,1)} %all-gather.4.cloned.1.call-done, bf16[2048,128]{1,0:T(8,128)(2,1)S(1)} %bitcast.107), kind=kOutput, calls=%fused_computation | convolution fusion | flops 268500992 | bytes 2883584 | tf_op jit(solution)/shard_map/dot_general | solution.py:371
  224.9 4.8 %all-to-all-done.8 = bf16[16,256,128]{2,1,0:T(8,128)(2,1)} async-done(((bf16[16,256,128]{2,1,0:T(8,128)(2,1)}), bf16[16,256,128]{2,1,0:T(8,128)(2,1)}, u32[]{:S(2)}, u32[]{:S(2)}) %all-to-all-start.8) | async-done | bytes 1048608 | tf_op jit(solution)/shard_map/all_to_all | solution.py:32
  229.7 2.3 copy.56
  (66 shorter events, 6.7 us)
Async XLA Ops:
  7.2 15.3 %copy-start = (bf16[4096,128]{1,0:T(8,128)(2,1)S(1)}, bf16[4096,128]{1,0:T(8,128)(2,1)}, u32[]{:S(2)}) copy-start(bf16[4096,128]{1,0:T(8,128)(2,1)} %param.18) | copy-start | bytes 3145732
  7.2 96.1 %all-gather.6.cloned.1.call-start = ((), (), s32[]{:S(2)}) async-start(), calls=%async_computation.10 | async-start | bytes 3538944 | tf_op jit(solution)/shard_map/all_gather | solution.py:282
  10.0 12.5 %copy-start.1 = (bf16[128,4096]{1,0:T(8,128)(2,1)S(1)}, bf16[128,4096]{1,0:T(8,128)(2,1)}, u32[]{:S(2)}) copy-start(bf16[128,4096]{1,0:T(8,128)(2,1)} %context_ref.1) | copy-start | bytes 3145732
  10.0 12.5 %copy-start.5 = (bf16[128,128]{1,0:T(8,128)(2,1)S(1)}, bf16[128,128]{1,0:T(8,128)(2,1)}, u32[]{:S(2)}) copy-start(bf16[128,128]{1,0:T(8,128)(2,1)} %param.17) | copy-start | bytes 98308
  12.0 10.9 %copy-start.4 = (bf16[64,512]{1,0:T(8,128)(2,1)S(1)}, bf16[64,512]{1,0:T(8,128)(2,1)}, u32[]{:S(2)}) copy-start(bf16[64,512]{1,0:T(8,128)(2,1)} %param.14) | copy-start | bytes 196612
  12.0 27.7 %copy-start.3 = (bf16[128,256]{1,0:T(8,128)(2,1)S(1)}, bf16[128,256]{1,0:T(8,128)(2,1)}, u32[]{:S(2)}) copy-start(bf16[128,256]{1,0:T(8,128)(2,1)} %query_ref.1) | copy-start | bytes 196612
  12.0 27.7 %all-to-all-start = ((bf16[16,128,256]{2,1,0:T(8,128)(2,1)}), bf16[16,128,256]{2,1,0:T(8,128)(2,1)S(1)}, u32[]{:S(2)}, u32[]{:S(2)}) async-start(bf16[16,128,256]{2,1,0:T(8,128)(2,1)} %broadcast_in_dim.65), calls=%async_computation | async-start | bytes 2097152 | tf_op jit(solution)/shard_map/all_to_all | solution.py:32
  124.8 21.2 %all-to-all-start.5 = ((bf16[16,16,1024]{2,1,0:T(8,128)(2,1)}), bf16[16,16,1024]{2,1,0:T(8,128)(2,1)S(1)}, u32[]{:S(2)}, u32[]{:S(2)}) async-start(bf16[16,16,1024]{2,1,0:T(8,128)(2,1)} %shard_map.123), calls=%async_computation.5 | async-start | bytes 1048576 | tf_op jit(solution)/shard_map/all_to_all | solution.py:32
  147.2 27.1 %all-to-all-start.6 = ((bf16[32,24,128]{2,1,0:T(8,128)(2,1)}), bf16[32,24,128]{2,1,0:T(8,128)(2,1)S(1)}, u32[]{:S(2)}, u32[]{:S(2)}) async-start(bf16[32,24,128]{2,1,0:T(8,128)(2,1)} %pad_maximum_fusion.1), calls=%async_computation.6 | async-start | bytes 393216 | tf_op jit(solution)/shard_map/all_to_all | solution.py:32
  157.5 64.4 %all-gather.4.cloned.1.call-start = ((), (), s32[]{:S(2)}) async-start(), calls=%async_computation.9 | async-start | bytes 2359296 | tf_op jit(solution)/shard_map/all_gather | solution.py:368
  206.8 1.0 copy-start.2
  207.8 21.9 %all-to-all-start.8 = ((bf16[16,256,128]{2,1,0:T(8,128)(2,1)}), bf16[16,256,128]{2,1,0:T(8,128)(2,1)}, u32[]{:S(2)}, u32[]{:S(2)}) async-start(bf16[16,256,128]{2,1,0:T(8,128)(2,1)} %copy-done.2), calls=%async_computation.8 | async-start | bytes 2097152 | tf_op jit(solution)/shard_map/all_to_all | solution.py:32
Sparse Core Ops, SparseCore 0:
  10.1 93.0 all-gather.5
  160.4 61.3 all-gather.3

commit v7 on v6

--- a/solution.py
+++ b/solution.py
@@ -225,29 +225,58 @@
     )(context, grad, tail)
 
 
-def sum_kernel(parts_ref, out_ref):
-    total = parts_ref[0].astype(F32)
-    for block in range(1, parts_ref.shape[0]):
-        total += parts_ref[block].astype(F32)
-    out_ref[...] = jnp.broadcast_to(total.astype(BF)[None], out_ref.shape)
-
-
-def weight_sum(got, part):
-    blocks, _, columns = got.shape
-    whole = pl.BlockSpec((blocks, part, columns), lambda g: (0, 0, 0))
+def map_kernel(few, hidden_ref, error_ref, out_ref, total):
+    step = pl.program_id(0)
+    block = N_NEAR * N_FAR * few
+    part = None
+    for device in range(AT_ONCE):
+        pieces = []
+        for far in range(N_FAR):
+            zf, xl = far // N_XL, far % N_XL
+            for near in range(N_NEAR):
+                pieces.append(error_ref[near * N_ZF + zf, xl, device])
+        error = jnp.concatenate(pieces, axis=0).astype(BF)
+        product = lax.dot_general(
+            error,
+            hidden_ref[device * block : (device + 1) * block],
+            (((0,), (0,)), ((), ())),
+            preferred_element_type=F32,
+        )
+        part = product if part is None else part + product
+
+    @pl.when(step == 0)
+    def _():
+        total[...] = part
+
+    @pl.when(step == N_NEAR // AT_ONCE - 1)
+    def _():
+        out_ref[...] = -(total[...] + part).T
+
+
+def map_grad(hidden, error, few):
+    rows, d_cols = hidden.shape
+    columns = error.shape[-1]
+    steps = N_NEAR // AT_ONCE
     return pl.pallas_call(
-        sum_kernel,
-        grid=(1,),
-        in_specs=[whole],
-        out_specs=whole,
-        out_shape=jax.ShapeDtypeStruct((blocks, part, columns), BF),
-        compiler_params=pltpu.CompilerParams(vmem_limit_bytes=40 * 2**20),
+        functools.partial(map_kernel, few),
+        grid=(steps,),
+        in_specs=[
+            pl.BlockSpec((rows // steps, d_cols), lambda g: (g, 0)),
+            pl.BlockSpec(
+                error.shape[:2] + (AT_ONCE,) + error.shape[3:],
+                lambda g: (0, 0, g, 0, 0),
+            ),
+        ],
+        out_specs=pl.BlockSpec((d_cols, columns), lambda g: (0, 0)),
+        out_shape=jax.ShapeDtypeStruct((d_cols, columns), F32),
+        scratch_shapes=[pltpu.VMEM((columns, d_cols), F32)],
+        compiler_params=pltpu.CompilerParams(vmem_limit_bytes=12 * 2**20),
         cost_estimate=pl.CostEstimate(
-            flops=blocks * part * columns,
-            bytes_accessed=2 * 2**20,
+            flops=2 * rows * d_cols * columns,
+            bytes_accessed=4 * 2**20,
             transcendentals=0,
         ),
-    )(got)
+    )(hidden, error)
 
 
 def on_device(
@@ -357,20 +386,17 @@
         [error.astype(BF), *split(gain_part), jnp.zeros((14, columns), BF)], axis=0
     )
 
-    contract_rows = (((0,), (0,)), ((), ()))
     got = exchange(weight_parts(student_context, grad_state.astype(BF), tail), MP)
-    grad_wo = exchange(weight_sum(got, part), MP).reshape(width, columns)
+    grad_wo = jnp.sum(got[:, :part].astype(F32), axis=0).astype(BF)
+    grad_wo = to_all(grad_wo, MP, N_MP).reshape(width, columns)
     error_all = got[:, part : part + rows]
     first = part + rows
     grad_gain = jnp.sum(got[:, first : first + 2].astype(F32), axis=(0, 1))
 
     hidden_near = hidden_near.reshape(N_MP * sub, d_cols)
     hidden_all = lax.all_gather(hidden_near, NEAR, axis=0, tiled=True)
-    error_all = error_all.reshape(N_NEAR, N_ZF, N_XL, N_NEAR, few, columns)
-    error_all = error_all.transpose(3, 1, 2, 0, 4, 5).reshape(total, columns)
-    grad_proj = -lax.dot_general(
-        hidden_all, error_all, contract_rows, preferred_element_type=F32
-    )
+    error_all = error_all.reshape(N_MP, N_XL, N_NEAR, few, columns)
+    grad_proj = map_grad(hidden_all, error_all.astype(F32), few)
     grad_wo, grad_proj = lax.optimization_barrier((grad_wo, grad_proj))
     return (grad_wo, grad_gain, grad_proj)
 

time: 240 us -> 238 us (level)
  matrix products: 3.46 us -> 0.42 us
  local copies, waits for them, and re-layouts: 8.66 us -> 11.5 us
    dot_general x1 -> x0, matrix products: 3.04 us -> none  [on_device(): lax.dot_general(hidden_all, error_all, contract_rows, preferred_element_t...]
  transfers between devices with their start and end apart: 6 -> 6, of which waited for: 6 -> 6; matrix products, arithmetic and copies ran while one was open for 4% -> 4% of each run, Pallas kernels for 1% -> 2%
where the time goes in v7:
time: 238 us; the launch traced here: 237 us
  blocking collectives  106 us (45%)
  waiting for transfers between devices  57.1 us (24%)
  starting transfers between devices  33.2 us (14%)
  between operations  14.4 us (6%)
  local copies, waits for them, and re-layouts  11.5 us (5%)
  Pallas kernels  9.5 us (4%)
  other arithmetic  4.74 us (2%)
    all_to_all x5, blocking collectives, exchange(): return lax.all_to_all(pieces, axes, 0, 0, tiled=True)  106 us
    all_to_all x4, waiting for transfers between devices, exchange(): return lax.all_to_all(pieces, axes, 0, 0, tiled=True)  47.1 us
    all_to_all x4, starting transfers between devices, exchange(): return lax.all_to_all(pieces, axes, 0, 0, tiled=True)  33.1 us
    all_gather x1, waiting for transfers between devices, on_device(): hidden_all = lax.all_gather(hidden_near, NEAR, axis=0, tiled=True)  7.28 us
  transfers between devices with their start and end apart: 6, of which 6 were waited for; matrix products, arithmetic and copies ran while one was open for 4% of the time, Pallas kernels for 2%

profile of v7, /device:TPU:1, one launch (start us, length us, event | category | flops | bytes accessed | tf_op | source)
XLA Modules:
  0.0 236.6 jit_solution(3071213512134004404)
XLA Ops:
  8.2 1.7 pad_maximum_fusion
  11.9 10.3 %all-to-all-start = ((bf16[16,128,256]{2,1,0:T(8,128)(2,1)}), bf16[16,128,256]{2,1,0:T(8,128)(2,1)S(1)}, u32[]{:S(2)}, u32[]{:S(2)}) async-start(bf16[16,128,256]{2,1,0:T(8,128)(2,1)} %broadcast_in_dim.71), calls=%async_computation | async-start | bytes 2097152 | tf_op jit(solution)/shard_map/all_to_all | solution.py:32
  23.1 16.4 %all-to-all-done.kv_ref = bf16[16,128,256]{2,1,0:T(8,128)(2,1)S(1)} async-done(((bf16[16,128,256]{2,1,0:T(8,128)(2,1)}), bf16[16,128,256]{2,1,0:T(8,128)(2,1)S(1)}, u32[]{:S(2)}, u32[]{:S(2)}) %all-to-all-start) | async-done | bytes 1048608 | tf_op jit(solution)/shard_map/all_to_all | solution.py:32
  39.5 1.6 shard_map.121
  41.2 37.1 %all_to_all.45 = bf16[8,16,640]{2,1,0:T(8,128)(2,1)S(1)} all-to-all(bf16[8,16,640]{2,1,0:T(8,128)(2,1)S(1)} %shard_map.121), channel_id=1, replica_groups=mesh['zn'=8,'zf'=2,'xl'=2,'xh'=2,'y'=4,'core'=2] {'zn'}, dimensions={0} | all-to-all | bytes 327680 | tf_op jit(solution)/shard_map/all_to_all | solution.py:32
  78.3 22.2 %all_to_all.46 = bf16[16,128,256]{2,1,0:T(8,128)(2,1)} all-to-all(bf16[16,128,256]{2,1,0:T(8,128)(2,1)S(1)} %broadcast_in_dim.73), channel_id=1, replica_groups=mesh['zn'=8,'zf'=2,'xl'=2,'xh'=2,'y'=4,'core'=2] {'xh','y','core'}, dimensions={0} | all-to-all | bytes 2097152 | tf_op jit(solution)/shard_map/all_to_all | solution.py:32
  100.6 2.7 %all-gather.6.cloned.1.call-done = bf16[3072,512]{1,0:T(8,128)(2,1)} async-done(((bf16[384,512]{1,0:T(8,128)(2,1)}), bf16[3072,512]{1,0:T(8,128)(2,1)}) %all-gather.6.cloned.1.call-update) | async-done | bytes 3145744 | tf_op jit(solution)/shard_map/all_gather | solution.py:311
  103.2 3.1 %shard_map.122 = bf16[4,64,512]{2,1,0:T(8,128)(2,1)} custom-call(bf16[16,8,16,256]{3,2,1,0:T(8,128)(2,1)} %bitcast.100, bf16[8,384,512]{2,1,0:T(8,128)(2,1)} %bitcast.98), custom_call_target="tpu_custom_call" | custom-call | flops 536870912 | bytes 4194304 | tf_op jit(solution)/shard_map/pallas_call | solution.py:78
  106.3 8.0 %all_to_all.47 = bf16[4,64,512]{2,1,0:T(8,128)(2,1)S(1)} all-to-all(bf16[4,64,512]{2,1,0:T(8,128)(2,1)} %shard_map.122), channel_id=1, replica_groups=mesh['zn'=8,'zf'=2,'xl'=2,'xh'=2,'y'=4,'core'=2] {'zf','xl'}, dimensions={0} | all-to-all | bytes 524288 | tf_op jit(solution)/shard_map/all_to_all | solution.py:32
  114.4 7.6 %all_to_all.48.hidden_ref = bf16[4,64,512]{2,1,0:T(8,128)(2,1)} all-to-all(bf16[4,64,512]{2,1,0:T(8,128)(2,1)S(1)} %broadcast_in_dim.74), channel_id=1, replica_groups=mesh['zn'=8,'zf'=2,'xl'=2,'xh'=2,'y'=4,'core'=2] {'zf','xl'}, dimensions={0} | all-to-all | bytes 524288 | tf_op jit(solution)/shard_map/all_to_all | solution.py:32
  122.0 2.7 %shard_map.123 = bf16[16,16,1024]{2,1,0:T(8,128)(2,1)} custom-call(bf16[4,64,512]{2,1,0:T(8,128)(2,1)} %all_to_all.48.hidden_ref, bf16[8,384,512]{2,1,0:T(8,128)(2,1)} %bitcast.99), custom_call_target="tpu_custom_call" | custom-call | flops 268435456 | bytes 2097152 | tf_op jit(solution)/shard_map/pallas_call | solution.py:125
  124.7 10.2 %all-to-all-start.5 = ((bf16[16,16,1024]{2,1,0:T(8,128)(2,1)}), bf16[16,16,1024]{2,1,0:T(8,128)(2,1)S(1)}, u32[]{:S(2)}, u32[]{:S(2)}) async-start(bf16[16,16,1024]{2,1,0:T(8,128)(2,1)} %shard_map.123), calls=%async_computation.5 | async-start | bytes 1048576 | tf_op jit(solution)/shard_map/all_to_all | solution.py:32
  135.7 10.5 %all-to-all-done.5 = bf16[16,16,1024]{2,1,0:T(8,128)(2,1)S(1)} async-done(((bf16[16,16,1024]{2,1,0:T(8,128)(2,1)}), bf16[16,16,1024]{2,1,0:T(8,128)(2,1)S(1)}, u32[]{:S(2)}, u32[]{:S(2)}) %all-to-all-start.5) | async-done | bytes 524320 | tf_op jit(solution)/shard_map/all_to_all | solution.py:32
  147.4 8.8 %all-to-all-start.6 = ((bf16[32,24,128]{2,1,0:T(8,128)(2,1)}), bf16[32,24,128]{2,1,0:T(8,128)(2,1)S(1)}, u32[]{:S(2)}, u32[]{:S(2)}) async-start(bf16[32,24,128]{2,1,0:T(8,128)(2,1)} %pad_maximum_fusion.1), calls=%async_computation.6 | async-start | bytes 393216 | tf_op jit(solution)/shard_map/all_to_all | solution.py:32
  157.1 15.9 %all-to-all-done.6 = bf16[32,24,128]{2,1,0:T(8,128)(2,1)S(1)} async-done(((bf16[32,24,128]{2,1,0:T(8,128)(2,1)}), bf16[32,24,128]{2,1,0:T(8,128)(2,1)S(1)}, u32[]{:S(2)}, u32[]{:S(2)}) %all-to-all-start.6) | async-done | bytes 196640 | tf_op jit(solution)/shard_map/all_to_all | solution.py:32
  174.3 30.9 %all_to_all.49 = bf16[16,400,128]{2,1,0:T(8,128)(2,1)S(1)} all-to-all(bf16[16,400,128]{2,1,0:T(8,128)(2,1)S(1)} %shard_map.124), channel_id=1, replica_groups=mesh['zn'=8,'zf'=2,'xl'=2,'xh'=2,'y'=4,'core'=2] {'xh','y','core'}, dimensions={0} | all-to-all | bytes 3276800 | tf_op jit(solution)/shard_map/all_to_all | solution.py:32
  205.2 1.2 copy-done.4
  206.5 1.2 broadcast_in_dim.80
  207.6 3.9 %all-to-all-start.8 = ((bf16[16,256,128]{2,1,0:T(8,128)(2,1)}), bf16[16,256,128]{2,1,0:T(8,128)(2,1)S(1)}, u32[]{:S(2)}, u32[]{:S(2)}) async-start(bf16[16,256,128]{2,1,0:T(8,128)(2,1)} %broadcast_in_dim.80), calls=%async_computation.8 | async-start | bytes 2097152 | tf_op jit(solution)/shard_map/all_to_all | solution.py:32
  212.7 1.3 convert_reduce_fusion.3
  214.0 7.3 %all-gather.4.cloned.1.call-done.hidden_ref = bf16[2048,512]{1,0:T(8,128)(2,1)} async-done(((bf16[256,512]{1,0:T(8,128)(2,1)}), bf16[2048,512]{1,0:T(8,128)(2,1)}) %all-gather.4.cloned.1.call-update) | async-done | bytes 2097168 | tf_op jit(solution)/shard_map/all_gather | solution.py:397
  221.3 1.6 copy-done.2
  222.9 1.6 shard_map.125
  224.5 4.3 %all-to-all-done.8 = bf16[16,256,128]{2,1,0:T(8,128)(2,1)S(1)} async-done(((bf16[16,256,128]{2,1,0:T(8,128)(2,1)}), bf16[16,256,128]{2,1,0:T(8,128)(2,1)S(1)}, u32[]{:S(2)}, u32[]{:S(2)}) %all-to-all-start.8) | async-done | bytes 1048608 | tf_op jit(solution)/shard_map/all_to_all | solution.py:32
  (69 shorter events, 10.3 us)
Async XLA Ops:
  7.2 15.1 %copy-start = (bf16[4096,128]{1,0:T(8,128)(2,1)S(1)}, bf16[4096,128]{1,0:T(8,128)(2,1)}, u32[]{:S(2)}) copy-start(bf16[4096,128]{1,0:T(8,128)(2,1)} %param.18) | copy-start | bytes 3145732
  7.2 96.1 %all-gather.6.cloned.1.call-start = ((), (), s32[]{:S(2)}) async-start(), calls=%async_computation.10 | async-start | bytes 3538944 | tf_op jit(solution)/shard_map/all_gather | solution.py:311
  10.8 11.5 %copy-start.1 = (bf16[128,4096]{1,0:T(8,128)(2,1)S(1)}, bf16[128,4096]{1,0:T(8,128)(2,1)}, u32[]{:S(2)}) copy-start(bf16[128,4096]{1,0:T(8,128)(2,1)} %context_ref.1) | copy-start | bytes 3145732
  10.8 11.5 %copy-start.6 = (bf16[128,128]{1,0:T(8,128)(2,1)S(1)}, bf16[128,128]{1,0:T(8,128)(2,1)}, u32[]{:S(2)}) copy-start(bf16[128,128]{1,0:T(8,128)(2,1)} %param.17) | copy-start | bytes 98308
  11.9 27.6 %all-to-all-start = ((bf16[16,128,256]{2,1,0:T(8,128)(2,1)}), bf16[16,128,256]{2,1,0:T(8,128)(2,1)S(1)}, u32[]{:S(2)}, u32[]{:S(2)}) async-start(bf16[16,128,256]{2,1,0:T(8,128)(2,1)} %broadcast_in_dim.71), calls=%async_computation | async-start | bytes 2097152 | tf_op jit(solution)/shard_map/all_to_all | solution.py:32
  22.2 0.8 copy-start.5
  22.2 17.3 %copy-start.3 = (bf16[128,256]{1,0:T(8,128)(2,1)S(1)}, bf16[128,256]{1,0:T(8,128)(2,1)}, u32[]{:S(2)}) copy-start(bf16[128,256]{1,0:T(8,128)(2,1)} %query_ref.1) | copy-start | bytes 196612
  124.7 21.5 %all-to-all-start.5 = ((bf16[16,16,1024]{2,1,0:T(8,128)(2,1)}), bf16[16,16,1024]{2,1,0:T(8,128)(2,1)S(1)}, u32[]{:S(2)}, u32[]{:S(2)}) async-start(bf16[16,16,1024]{2,1,0:T(8,128)(2,1)} %shard_map.123), calls=%async_computation.5 | async-start | bytes 1048576 | tf_op jit(solution)/shard_map/all_to_all | solution.py:32
  147.4 25.6 %all-to-all-start.6 = ((bf16[32,24,128]{2,1,0:T(8,128)(2,1)}), bf16[32,24,128]{2,1,0:T(8,128)(2,1)S(1)}, u32[]{:S(2)}, u32[]{:S(2)}) async-start(bf16[32,24,128]{2,1,0:T(8,128)(2,1)} %pad_maximum_fusion.1), calls=%async_computation.6 | async-start | bytes 393216 | tf_op jit(solution)/shard_map/all_to_all | solution.py:32
  156.2 65.1 %all-gather.4.cloned.1.call-start = ((), (), s32[]{:S(2)}) async-start(), calls=%async_computation.9 | async-start | bytes 2359296 | tf_op jit(solution)/shard_map/all_gather | solution.py:397
  205.2 1.2 copy-start.4
  207.6 21.2 %all-to-all-start.8 = ((bf16[16,256,128]{2,1,0:T(8,128)(2,1)}), bf16[16,256,128]{2,1,0:T(8,128)(2,1)S(1)}, u32[]{:S(2)}, u32[]{:S(2)}) async-start(bf16[16,256,128]{2,1,0:T(8,128)(2,1)} %broadcast_in_dim.80), calls=%async_computation.8 | async-start | bytes 2097152 | tf_op jit(solution)/shard_map/all_to_all | solution.py:32
  221.3 1.6 copy-start.2
Sparse Core Ops, SparseCore 0:
  10.1 93.0 all-gather.5
  159.1 62.1 all-gather.3

commit v8 on v7

--- a/solution.py
+++ b/solution.py
@@ -277,6 +277,29 @@
             transcendentals=0,
         ),
     )(hidden, error)
+
+
+def pack_kernel(out_ref, map_ref, packed_ref):
+    head_rows, d_cols = out_ref.shape
+    columns = map_ref.shape[1]
+    packed_ref[:head_rows] = out_ref[...]
+    for fold in range(d_cols // columns):
+        lanes = slice(fold * columns, (fold + 1) * columns)
+        packed_ref[head_rows:, lanes] = map_ref[lanes]
+
+
+def pack(teacher_out, distill_proj):
+    head_rows, d_cols = teacher_out.shape
+    vmem = pl.BlockSpec(memory_space=pltpu.VMEM)
+    return pl.pallas_call(
+        pack_kernel,
+        in_specs=[vmem] * 2,
+        out_specs=vmem,
+        out_shape=jax.ShapeDtypeStruct(
+            (head_rows + distill_proj.shape[1], d_cols), BF
+        ),
+        compiler_params=pltpu.CompilerParams(vmem_limit_bytes=60 * 2**20),
+    )(teacher_out, distill_proj)
 
 
 def on_device(
@@ -304,10 +327,7 @@
     head_rows, d_cols = teacher_out.shape
     few = sub // N_XL
 
-    folds = d_cols // columns
-    folded = distill_proj.reshape(folds, columns, columns)
-    folded = folded.transpose(1, 0, 2).reshape(columns, d_cols)
-    packed = jnp.concatenate([teacher_out, folded], axis=0)
+    packed = pack(teacher_out, distill_proj)
     packed_all = lax.all_gather(packed, NEAR, axis=0, tiled=False)
 
     def by_near(values):

time: 238 us -> 238 us (level)
  no operation moved by 1% of the time
where the time goes in v8:
time: 238 us; the launch traced here: 237 us
  blocking collectives  106 us (45%)
  waiting for transfers between devices  58.3 us (24%)
  starting transfers between devices  33.1 us (14%)
  between operations  14.4 us (6%)
  Pallas kernels  11.4 us (5%)
  local copies, waits for them, and re-layouts  10.5 us (4%)
  other arithmetic  3.01 us (1%)
    all_to_all x5, blocking collectives, exchange(): return lax.all_to_all(pieces, axes, 0, 0, tiled=True)  106 us
    all_to_all x4, waiting for transfers between devices, exchange(): return lax.all_to_all(pieces, axes, 0, 0, tiled=True)  47.8 us
    all_to_all x4, starting transfers between devices, exchange(): return lax.all_to_all(pieces, axes, 0, 0, tiled=True)  33 us
    all_gather x1, waiting for transfers between devices, on_device(): hidden_all = lax.all_gather(hidden_near, NEAR, axis=0, tiled=True)  6.6 us
  transfers between devices with their start and end apart: 6, of which 6 were waited for; matrix products, arithmetic and copies ran while one was open for 4% of the time, Pallas kernels for 2%

profile of v8, /device:TPU:1, one launch (start us, length us, event | category | flops | bytes accessed | tf_op | source)
XLA Modules:
  0.0 236.9 jit_solution(5880051355957157402)
XLA Ops:
  7.2 1.9 shard_map.122
  11.0 10.3 %all-to-all-start = ((bf16[16,128,256]{2,1,0:T(8,128)(2,1)}), bf16[16,128,256]{2,1,0:T(8,128)(2,1)S(1)}, u32[]{:S(2)}, u32[]{:S(2)}) async-start(bf16[16,128,256]{2,1,0:T(8,128)(2,1)} %broadcast_in_dim.71), calls=%async_computation | async-start | bytes 2097152 | tf_op jit(solution)/shard_map/all_to_all | solution.py:32
  22.2 16.4 %all-to-all-done.kv_ref = bf16[16,128,256]{2,1,0:T(8,128)(2,1)S(1)} async-done(((bf16[16,128,256]{2,1,0:T(8,128)(2,1)}), bf16[16,128,256]{2,1,0:T(8,128)(2,1)S(1)}, u32[]{:S(2)}, u32[]{:S(2)}) %all-to-all-start) | async-done | bytes 1048608 | tf_op jit(solution)/shard_map/all_to_all | solution.py:32
  38.6 1.6 shard_map.121
  40.3 34.4 %all_to_all.45 = bf16[8,16,640]{2,1,0:T(8,128)(2,1)S(1)} all-to-all(bf16[8,16,640]{2,1,0:T(8,128)(2,1)S(1)} %shard_map.121), channel_id=1, replica_groups=mesh['zn'=8,'zf'=2,'xl'=2,'xh'=2,'y'=4,'core'=2] {'zn'}, dimensions={0} | all-to-all | bytes 327680 | tf_op jit(solution)/shard_map/all_to_all | solution.py:32
  74.8 24.7 %all_to_all.46 = bf16[16,128,256]{2,1,0:T(8,128)(2,1)} all-to-all(bf16[16,128,256]{2,1,0:T(8,128)(2,1)S(1)} %broadcast_in_dim.73), channel_id=1, replica_groups=mesh['zn'=8,'zf'=2,'xl'=2,'xh'=2,'y'=4,'core'=2] {'xh','y','core'}, dimensions={0} | all-to-all | bytes 2097152 | tf_op jit(solution)/shard_map/all_to_all | solution.py:32
  99.6 3.9 %all-gather.6.cloned.1.call-done = bf16[3072,512]{1,0:T(8,128)(2,1)} async-done(((bf16[384,512]{1,0:T(8,128)(2,1)}), bf16[3072,512]{1,0:T(8,128)(2,1)}) %all-gather.6.cloned.1.call-update) | async-done | bytes 3145744 | tf_op jit(solution)/shard_map/all_gather | solution.py:331
  103.5 3.1 %shard_map.123 = bf16[4,64,512]{2,1,0:T(8,128)(2,1)} custom-call(bf16[16,8,16,256]{3,2,1,0:T(8,128)(2,1)} %bitcast.93, bf16[8,384,512]{2,1,0:T(8,128)(2,1)} %bitcast.91), custom_call_target="tpu_custom_call" | custom-call | flops 536870912 | bytes 4194304 | tf_op jit(solution)/shard_map/pallas_call | solution.py:78
  106.6 8.1 %all_to_all.47 = bf16[4,64,512]{2,1,0:T(8,128)(2,1)S(1)} all-to-all(bf16[4,64,512]{2,1,0:T(8,128)(2,1)} %shard_map.123), channel_id=1, replica_groups=mesh['zn'=8,'zf'=2,'xl'=2,'xh'=2,'y'=4,'core'=2] {'zf','xl'}, dimensions={0} | all-to-all | bytes 524288 | tf_op jit(solution)/shard_map/all_to_all | solution.py:32
  114.8 7.6 %all_to_all.48.hidden_ref = bf16[4,64,512]{2,1,0:T(8,128)(2,1)} all-to-all(bf16[4,64,512]{2,1,0:T(8,128)(2,1)S(1)} %broadcast_in_dim.74), channel_id=1, replica_groups=mesh['zn'=8,'zf'=2,'xl'=2,'xh'=2,'y'=4,'core'=2] {'zf','xl'}, dimensions={0} | all-to-all | bytes 524288 | tf_op jit(solution)/shard_map/all_to_all | solution.py:32
  122.4 2.7 %shard_map.124 = bf16[16,16,1024]{2,1,0:T(8,128)(2,1)} custom-call(bf16[4,64,512]{2,1,0:T(8,128)(2,1)} %all_to_all.48.hidden_ref, bf16[8,384,512]{2,1,0:T(8,128)(2,1)} %bitcast.92), custom_call_target="tpu_custom_call" | custom-call | flops 268435456 | bytes 2097152 | tf_op jit(solution)/shard_map/pallas_call | solution.py:125
  125.1 9.7 %all-to-all-start.5 = ((bf16[16,16,1024]{2,1,0:T(8,128)(2,1)}), bf16[16,16,1024]{2,1,0:T(8,128)(2,1)S(1)}, u32[]{:S(2)}, u32[]{:S(2)}) async-start(bf16[16,16,1024]{2,1,0:T(8,128)(2,1)} %shard_map.124), calls=%async_computation.5 | async-start | bytes 1048576 | tf_op jit(solution)/shard_map/all_to_all | solution.py:32
  135.6 10.5 %all-to-all-done.5 = bf16[16,16,1024]{2,1,0:T(8,128)(2,1)S(1)} async-done(((bf16[16,16,1024]{2,1,0:T(8,128)(2,1)}), bf16[16,16,1024]{2,1,0:T(8,128)(2,1)S(1)}, u32[]{:S(2)}, u32[]{:S(2)}) %all-to-all-start.5) | async-done | bytes 524320 | tf_op jit(solution)/shard_map/all_to_all | solution.py:32
  147.3 9.1 %all-to-all-start.6 = ((bf16[32,24,128]{2,1,0:T(8,128)(2,1)}), bf16[32,24,128]{2,1,0:T(8,128)(2,1)S(1)}, u32[]{:S(2)}, u32[]{:S(2)}) async-start(bf16[32,24,128]{2,1,0:T(8,128)(2,1)} %pad_maximum_fusion), calls=%async_computation.6 | async-start | bytes 393216 | tf_op jit(solution)/shard_map/all_to_all | solution.py:32
  157.4 15.9 %all-to-all-done.6 = bf16[32,24,128]{2,1,0:T(8,128)(2,1)S(1)} async-done(((bf16[32,24,128]{2,1,0:T(8,128)(2,1)}), bf16[32,24,128]{2,1,0:T(8,128)(2,1)S(1)}, u32[]{:S(2)}, u32[]{:S(2)}) %all-to-all-start.6) | async-done | bytes 196640 | tf_op jit(solution)/shard_map/all_to_all | solution.py:32
  174.6 30.9 %all_to_all.49 = bf16[16,400,128]{2,1,0:T(8,128)(2,1)S(1)} all-to-all(bf16[16,400,128]{2,1,0:T(8,128)(2,1)S(1)} %shard_map.125), channel_id=1, replica_groups=mesh['zn'=8,'zf'=2,'xl'=2,'xh'=2,'y'=4,'core'=2] {'xh','y','core'}, dimensions={0} | all-to-all | bytes 3276800 | tf_op jit(solution)/shard_map/all_to_all | solution.py:32
  205.5 1.2 copy-done.4
  206.8 1.2 broadcast_in_dim.80
  207.9 3.9 %all-to-all-start.8 = ((bf16[16,256,128]{2,1,0:T(8,128)(2,1)}), bf16[16,256,128]{2,1,0:T(8,128)(2,1)S(1)}, u32[]{:S(2)}, u32[]{:S(2)}) async-start(bf16[16,256,128]{2,1,0:T(8,128)(2,1)} %broadcast_in_dim.80), calls=%async_computation.8 | async-start | bytes 2097152 | tf_op jit(solution)/shard_map/all_to_all | solution.py:32
  213.0 1.3 convert_reduce_fusion.3
  214.3 6.6 %all-gather.4.cloned.1.call-done.hidden_ref = bf16[2048,512]{1,0:T(8,128)(2,1)} async-done(((bf16[256,512]{1,0:T(8,128)(2,1)}), bf16[2048,512]{1,0:T(8,128)(2,1)}) %all-gather.4.cloned.1.call-update) | async-done | bytes 2097168 | tf_op jit(solution)/shard_map/all_gather | solution.py:417
  220.9 1.6 copy-done.2
  222.5 1.6 shard_map.126
  224.1 5.0 %all-to-all-done.8 = bf16[16,256,128]{2,1,0:T(8,128)(2,1)S(1)} async-done(((bf16[16,256,128]{2,1,0:T(8,128)(2,1)}), bf16[16,256,128]{2,1,0:T(8,128)(2,1)S(1)}, u32[]{:S(2)}, u32[]{:S(2)}) %all-to-all-start.8) | async-done | bytes 1048608 | tf_op jit(solution)/shard_map/all_to_all | solution.py:32
  (68 shorter events, 9.3 us)
Async XLA Ops:
  7.2 14.2 %copy-start = (bf16[4096,128]{1,0:T(8,128)(2,1)S(1)}, bf16[4096,128]{1,0:T(8,128)(2,1)}, u32[]{:S(2)}) copy-start(bf16[4096,128]{1,0:T(8,128)(2,1)} %param.18) | copy-start | bytes 3145732
  7.2 96.3 %all-gather.6.cloned.1.call-start = ((), (), s32[]{:S(2)}) async-start(), calls=%async_computation.10 | async-start | bytes 3538944 | tf_op jit(solution)/shard_map/all_gather | solution.py:331
  9.9 11.5 %copy-start.1 = (bf16[128,4096]{1,0:T(8,128)(2,1)S(1)}, bf16[128,4096]{1,0:T(8,128)(2,1)}, u32[]{:S(2)}) copy-start(bf16[128,4096]{1,0:T(8,128)(2,1)} %context_ref.1) | copy-start | bytes 3145732
  9.9 11.5 %copy-start.6 = (bf16[128,128]{1,0:T(8,128)(2,1)S(1)}, bf16[128,128]{1,0:T(8,128)(2,1)}, u32[]{:S(2)}) copy-start(bf16[128,128]{1,0:T(8,128)(2,1)} %param.17) | copy-start | bytes 98308
  11.0 27.6 %all-to-all-start = ((bf16[16,128,256]{2,1,0:T(8,128)(2,1)}), bf16[16,128,256]{2,1,0:T(8,128)(2,1)S(1)}, u32[]{:S(2)}, u32[]{:S(2)}) async-start(bf16[16,128,256]{2,1,0:T(8,128)(2,1)} %broadcast_in_dim.71), calls=%async_computation | async-start | bytes 2097152 | tf_op jit(solution)/shard_map/all_to_all | solution.py:32
  21.4 0.8 copy-start.5
  21.4 17.3 %copy-start.3 = (bf16[128,256]{1,0:T(8,128)(2,1)S(1)}, bf16[128,256]{1,0:T(8,128)(2,1)}, u32[]{:S(2)}) copy-start(bf16[128,256]{1,0:T(8,128)(2,1)} %query_ref.1) | copy-start | bytes 196612
  125.1 21.0 %all-to-all-start.5 = ((bf16[16,16,1024]{2,1,0:T(8,128)(2,1)}), bf16[16,16,1024]{2,1,0:T(8,128)(2,1)S(1)}, u32[]{:S(2)}, u32[]{:S(2)}) async-start(bf16[16,16,1024]{2,1,0:T(8,128)(2,1)} %shard_map.124), calls=%async_computation.5 | async-start | bytes 1048576 | tf_op jit(solution)/shard_map/all_to_all | solution.py:32
  147.3 25.9 %all-to-all-start.6 = ((bf16[32,24,128]{2,1,0:T(8,128)(2,1)}), bf16[32,24,128]{2,1,0:T(8,128)(2,1)S(1)}, u32[]{:S(2)}, u32[]{:S(2)}) async-start(bf16[32,24,128]{2,1,0:T(8,128)(2,1)} %pad_maximum_fusion), calls=%async_computation.6 | async-start | bytes 393216 | tf_op jit(solution)/shard_map/all_to_all | solution.py:32
  156.5 64.5 %all-gather.4.cloned.1.call-start = ((), (), s32[]{:S(2)}) async-start(), calls=%async_computation.9 | async-start | bytes 2359296 | tf_op jit(solution)/shard_map/all_gather | solution.py:417
  205.5 1.2 copy-start.4
  207.9 21.2 %all-to-all-start.8 = ((bf16[16,256,128]{2,1,0:T(8,128)(2,1)}), bf16[16,256,128]{2,1,0:T(8,128)(2,1)S(1)}, u32[]{:S(2)}, u32[]{:S(2)}) async-start(bf16[16,256,128]{2,1,0:T(8,128)(2,1)} %broadcast_in_dim.80), calls=%async_computation.8 | async-start | bytes 2097152 | tf_op jit(solution)/shard_map/all_to_all | solution.py:32
  220.9 1.6 copy-start.2
Sparse Core Ops, SparseCore 0:
  10.1 93.3 all-gather.5
  159.4 61.5 all-gather.3
